TPU v7x, 128 devices: a whole 4x4x4 slice. The times are simulated.
128 devices in a mesh: ty: 8 (over z, x_lo), tx: 16 (over x_hi, y, core).
Axes of the slice: x: 4 (x_hi: 2, x_lo: 2; x = x_hi * 2 + x_lo), y: 4, z: 4, core: 2. Of those that a mesh axis runs over, the one named last changes fastest.
Arguments:
- object_slices: float32 [2, 2, 2048, 4096], P(None, None, 'ty', 'tx'), may hold values from -4 to 4
- probe_rows: float32 [2048, 256], P(('ty', 'tx')), may hold values from -4 to 4
- measured: float32 [8, 16, 2, 256, 256], P('ty', None, None, 'tx'), may hold values from 0.2 to 1.6
- positions: int32 [8, 16, 2, 2], P('ty', 'tx'), may hold values from 0 to 255
- counts: int32 [8, 16], P('ty', 'tx'), may hold values from 1 to 2, as said below
Outputs:
- object_grad: float32 [2, 2, 2048, 4096], P(None, None, 'ty', 'tx')
- probe_grad: float32 [2048, 256], P(('ty', 'tx'))
Inputs may be any that keep to these rules, and one draw needn't show every extreme that they name: Slots s with s >= counts of their tile are unused; at least one tile has all 2 slots live.
All inputs are finite; a program needn't handle non-finite values.
Results may differ from a plain program's by a relative error of at most 0.0003.
Values sent between devices are 32-bit elements; how exact they have to be, the bound alone decides.
No kernel may reach another device: no remote copies, remote signals or barrier semaphores. Data moves between devices by JAX's collectives and lax.ppermute only.
A program may use at most 128 MiB of HBM per device.

v0:
```python
import math

import jax
import jax.numpy as jnp
from jax import lax
from jax.sharding import PartitionSpec as P

amp_floor = 0.5


def extended_2(cells, sides, width):
    for axis, dim in sides:
        count = lax.axis_size(axis)
        ends = count - 1
        head = lax.slice_in_dim(cells, 0, width, axis=dim)
        tail = lax.slice_in_dim(cells, cells.shape[dim] - width, cells.shape[dim], axis=dim)
        cells = jnp.concatenate(
            [
                lax.ppermute(tail, axis, [(i, (i + 1) % count) for i in range(ends)]),
                cells,
                lax.ppermute(head, axis, [((i + 1) % count, i) for i in range(ends)]),
            ],
            axis=dim,
        )
    return cells


def matmul_high(form, first, second):
    return jnp.einsum(form, first, second, precision=lax.Precision.HIGHEST)


def make_tables(pattern_side):
    indices = jnp.arange(pattern_side, dtype=jnp.int32)
    product = indices[:, None] * indices[None, :] % pattern_side
    angles = 2.0 * math.pi / pattern_side * product.astype(jnp.float32)
    norm_factor = 1.0 / math.sqrt(pattern_side)
    cos_table = jnp.cos(angles) * norm_factor
    sin_table = jnp.sin(angles) * norm_factor
    frequency = (indices + pattern_side // 2) % pattern_side - pattern_side // 2
    quad = (frequency[:, None] * frequency[:, None] + frequency[None, :] * frequency[None, :]) % (
        4 * pattern_side
    )
    phase = 2.0 * math.pi / (4 * pattern_side) * quad.astype(jnp.float32)
    return (cos_table, sin_table, jnp.cos(phase), jnp.sin(phase))


def transform(real_part, imag_part, cos_table, sin_table):
    left_real = matmul_high("kn,mnc->mkc", cos_table, real_part) - matmul_high(
        "kn,mnc->mkc", sin_table, imag_part
    )
    left_imag = matmul_high("kn,mnc->mkc", cos_table, imag_part) + matmul_high(
        "kn,mnc->mkc", sin_table, real_part
    )
    out_real = matmul_high("mkc,cl->mkl", left_real, cos_table) - matmul_high(
        "mkc,cl->mkl", left_imag, sin_table
    )
    out_imag = matmul_high("mkc,cl->mkl", left_imag, cos_table) + matmul_high(
        "mkc,cl->mkl", left_real, sin_table
    )
    return (out_real, out_imag)


def slot_loss(window, probe, amplitude, weight, tables):
    cos_table, sin_table, prop_real, prop_imag = tables
    real_part = probe[:, 0]
    imag_part = probe[:, 1]
    slice_count = window.shape[0]
    for which in range(slice_count):
        obj_real = window[which, 0]
        obj_imag = window[which, 1]
        real_part, imag_part = (
            real_part * obj_real - imag_part * obj_imag,
            real_part * obj_imag + imag_part * obj_real,
        )
        if which + 1 < slice_count:
            real_part, imag_part = transform(real_part, imag_part, cos_table, -sin_table)
            real_part, imag_part = (
                real_part * prop_real - imag_part * prop_imag,
                real_part * prop_imag + imag_part * prop_real,
            )
            real_part, imag_part = transform(real_part, imag_part, cos_table, sin_table)
    real_part, imag_part = transform(real_part, imag_part, cos_table, -sin_table)
    intensity = jnp.sum(real_part * real_part + imag_part * imag_part, axis=0)
    residual = jnp.sqrt(intensity + amp_floor) - amplitude
    return weight * jnp.sum(residual * residual)


def slot_gradient(window, probe, amplitude, weight, tables):
    loss_value, pullback = jax.vjp(
        lambda wind, prob: slot_loss(wind, prob, amplitude, weight, tables), window, probe
    )
    return pullback(jnp.ones_like(loss_value))


def fold_along(extended, along_dim, rim_width, tile_side):
    middle = lax.slice_in_dim(extended, 2 * rim_width, 2 * rim_width + tile_side, axis=along_dim)
    low_part = lax.slice_in_dim(extended, 0, rim_width, axis=along_dim)
    high_part = lax.slice_in_dim(
        extended, tile_side + 3 * rim_width, tile_side + 4 * rim_width, axis=along_dim
    )
    low_pads = [(0, 0)] * extended.ndim
    high_pads = [(0, 0)] * extended.ndim
    low_pads[along_dim] = (0, tile_side - rim_width)
    high_pads[along_dim] = (tile_side - rim_width, 0)
    return middle + jnp.pad(low_part, low_pads) + jnp.pad(high_part, high_pads)


def body(object_slices, probe_rows, measured, positions, counts):
    pattern_side = probe_rows.shape[1]
    rim_width = pattern_side // 2
    tile_side = object_slices.shape[2]
    slice_count = object_slices.shape[0]
    slot_count = positions.shape[2]
    probe_all = lax.all_gather(probe_rows, ("ty", "tx"), axis=0, tiled=True)
    mode_count = probe_all.shape[0] // (2 * pattern_side)
    probe = probe_all.reshape(mode_count, 2, pattern_side, pattern_side)
    patterns = lax.all_to_all(measured, "tx", split_axis=1, concat_axis=3, tiled=True)
    extended = extended_2(object_slices, (("ty", 2), ("tx", 3)), rim_width)
    loss_scale = 1.0 / math.sqrt(slot_count * lax.axis_size("ty") * lax.axis_size("tx"))
    tables = make_tables(pattern_side)
    zero_index = jnp.zeros((), jnp.int32)
    grad_buffer = jnp.zeros(extended.shape, jnp.float32)
    grad_total = jnp.zeros(probe.shape, jnp.float32)
    for which in range(slot_count):
        row_start = positions[0, 0, which, 0]
        col_start = positions[0, 0, which, 1]
        corner = (zero_index, zero_index, row_start, col_start)
        window = lax.dynamic_slice(extended, corner, (slice_count, 2, pattern_side, pattern_side))
        live_flag = (which < counts[0, 0]).astype(jnp.float32)
        grad_window, grad_probe = slot_gradient(
            window, probe, patterns[0, 0, which], live_flag * loss_scale, tables
        )
        current = lax.dynamic_slice(
            grad_buffer, corner, (slice_count, 2, pattern_side, pattern_side)
        )
        grad_buffer = lax.dynamic_update_slice(grad_buffer, current + grad_window, corner)
        grad_total = grad_total + grad_probe
    gathered = extended_2(grad_buffer, (("ty", 2), ("tx", 3)), rim_width)
    folded = fold_along(fold_along(gathered, 2, rim_width, tile_side), 3, rim_width, tile_side)
    probe_sum = lax.psum_scatter(
        grad_total.reshape(2 * mode_count * pattern_side, pattern_side),
        ("ty", "tx"),
        scatter_dimension=0,
        tiled=True,
    )
    return (folded, probe_sum)


def solution(mesh):
    in_specs = (
        P(None, None, "ty", "tx"),
        P(("ty", "tx"), None),
        P("ty", None, None, "tx", None),
        P("ty", "tx", None, None),
        P("ty", "tx"),
    )
    out_specs = (P(None, None, "ty", "tx"), P(("ty", "tx"), None))
    return jax.shard_map(body, mesh=mesh, in_specs=in_specs, out_specs=out_specs, check_vma=False)
```

profile of v0, /device:TPU:0, one launch (start us, length us, event | category | flops | bytes accessed | tf_op | source)
XLA Modules:
  0.0 1149.6 jit_solution(240416898177724791)
XLA Ops:
  9.3 3.5 collective-permute-start
  14.1 10.0 collective-permute-done
  24.3 14.2 %collective-permute-done.1 = f32[2,2,128,256]{3,2,1,0:T(8,128)S(1)} collective-permute-done((f32[2,2,128,256]{3,2,1,0:T(8,128)S(1)}, f32[2,2,128,256]{3,2,1,0:T(8,128)S(1)}, u32[]{:S(2)}, u32[]{:S(2)}) %collective-permute-start.1) | collective-permute-done | bytes 524320 | tf_op jit(solution)/shard_map/ppermute | solution.py:21
  43.5 10.2 all-to-all-start
  64.3 5.6 all-to-all-done
  73.4 144.8 %all-gather.2.cloned.1.call-done = f32[2048,256]{1,0:T(8,128)} async-done(((f32[16,256]{1,0:T(8,128)}), f32[2048,256]{1,0:T(8,128)}) %all-gather.2.cloned.1.call-update) | async-done | bytes 2097168 | tf_op jit(solution)/shard_map/all_gather | solution.py:114
  218.2 4.4 fusion.173
  228.2 3.1 fusion.171
  239.5 2.9 convolution_subtract_fusion.4
  253.3 3.0 fusion.22
  264.4 3.2 fusion.157
  275.9 2.9 fusion.41
  289.6 2.9 convolution_subtract_fusion.10
  298.1 2.8 fusion.39
  300.9 3.1 fusion.207
  312.1 2.9 convolution_subtract_fusion.8
  325.9 3.0 fusion.20
  334.3 2.8 fusion.37
  337.1 3.1 fusion.199
  340.2 2.8 fusion.38
  348.4 2.9 add_reduce_fusion
  351.2 2.8 add_reduce_fusion.1
  414.5 3.2 multiply_reduce_fusion.6
  456.7 6.0 add_bitcast_fusion.3
  465.3 11.6 %dynamic_update_slice.6 = f32[2,2,512,512]{3,2,1,0:T(8,128)} dynamic-update-slice(f32[2,2,512,512]{3,2,1,0:T(8,128)} %broadcast_in_dim.18, f32[2,2,256,256]{3,2,1,0:T(8,128)S(1)} %pad_add_fusion, s32[]{:T(128)} %constant.55.clone.1, s32[]{:T(128)} %constant.55.clone.1, s32[]{:T(128)S(6)} %select_n.300, s32[]{:T(128)S(6)} %select_n.301) | dynamic-update-slice | bytes 2097156 | tf_op jit(solution)/shard_map/dynamic_update_slice | solution.py:136
  479.9 11.9 %dynamic_update_slice.7 = f32[2,2,512,512]{3,2,1,0:T(8,128)} dynamic-update-slice(f32[2,2,512,512]{3,2,1,0:T(8,128)} %dynamic_update_slice.6, f32[2,2,256,256]{3,2,1,0:T(8,128)S(1)} %add_add_fusion.1, s32[]{:T(128)} %constant.55.clone.1, s32[]{:T(128)} %constant.55.clone.1, s32[]{:T(128)S(6)} %select_n.305, s32[]{:T(128)S(6)} %select_n.306) | dynamic-update-slice | bytes 2097156 | tf_op jit(solution)/shard_map/dynamic_update_slice | solution.py:136
  491.7 2.9 fusion.744
  494.6 2.9 collective-permute-start.4
  500.9 18.3 %collective-permute-done.4 = f32[2,2,128,512]{3,2,1,0:T(8,128)S(1)} collective-permute-done((f32[2,2,128,512]{3,2,1,0:T(8,128)}, f32[2,2,128,512]{3,2,1,0:T(8,128)S(1)}, u32[]{:S(2)}, u32[]{:S(2)}) %collective-permute-start.4) | collective-permute-done | bytes 1048608 | tf_op jit(solution)/shard_map/ppermute | solution.py:19
  519.3 24.0 %collective-permute-done.5 = f32[2,2,128,512]{3,2,1,0:T(8,128)S(1)} collective-permute-done((f32[2,2,128,512]{3,2,1,0:T(8,128)S(1)}, f32[2,2,128,512]{3,2,1,0:T(8,128)S(1)}, u32[]{:S(2)}, u32[]{:S(2)}) %collective-permute-start.5) | collective-permute-done | bytes 1048608 | tf_op jit(solution)/shard_map/ppermute | solution.py:21
  549.5 3.9 collective-permute-done.7
  558.6 584.0 %reduce-scatter.2.cloned.1.call-done = f32[16,256]{1,0:T(8,128)} async-done(((f32[2048,256]{1,0:T(8,128)}), f32[16,256]{1,0:T(8,128)}) %reduce-scatter.2.cloned.1.call-update) | async-done | bytes 16400 | tf_op jit(solution)/shard_map/reduce_scatter | solution.py:140
  (147 shorter events, 220.4 us)
Async XLA Ops:
  7.2 211.0 %all-gather.2.cloned.1.call-start = ((), (), s32[]{:S(2)}) async-start(), calls=%async_computation.2 | async-start | bytes 2113536 | tf_op jit(solution)/shard_map/all_gather | solution.py:114
  7.9 16.3 %copy-start.2 = (f32[2,2,256,256]{3,2,1,0:T(8,128)S(1)}, f32[2,2,256,256]{3,2,1,0:T(8,128)}, u32[]{:S(2)}) copy-start(f32[2,2,256,256]{3,2,1,0:T(8,128)} %param.5) | copy-start | bytes 3145732
  9.3 14.8 %collective-permute-start = (f32[2,2,128,256]{3,2,1,0:T(8,128)S(1)}, f32[2,2,128,256]{3,2,1,0:T(8,128)S(1)}, u32[]{:S(2)}, u32[]{:S(2)}) collective-permute-start(f32[2,2,128,256]{3,2,1,0:T(8,128)S(1)} %get-tuple-element.53), channel_id=1, source_target_pairs={{0,16},{16,32},{32,48},{48,64},{64,80},{80,96},{96,112},{1,17},{17... | collective-permute-start | bytes 1572872 | tf_op jit(solution)/shard_map/ppermute | solution.py:19
  12.8 25.7 %collective-permute-start.1 = (f32[2,2,128,256]{3,2,1,0:T(8,128)S(1)}, f32[2,2,128,256]{3,2,1,0:T(8,128)S(1)}, u32[]{:S(2)}, u32[]{:S(2)}) collective-permute-start(f32[2,2,128,256]{3,2,1,0:T(8,128)S(1)} %get-tuple-element.52), channel_id=1, source_target_pairs={{16,0},{32,16},{48,32},{64,48},{80,64},{96,80},{112,96},{17,1},{33... | collective-permute-start | bytes 1572872 | tf_op jit(solution)/shard_map/ppermute | solution.py:21
  38.5 15.3 %copy-start.12 = (s32[1,1,2,2]{3,2,1,0:T(2,128)S(1)}, s32[1,1,2,2]{3,2,1,0:T(2,128)}, u32[]{:S(2)}) copy-start(s32[1,1,2,2]{3,2,1,0:T(2,128)} %param.8) | copy-start | bytes 52
  40.0 30.8 %collective-permute-start.2 = (f32[2,2,512,128]{3,2,1,0:T(8,128)}, f32[2,2,512,128]{3,2,1,0:T(8,128)}, u32[]{:S(2)}, u32[]{:S(2)}) collective-permute-start(f32[2,2,512,128]{3,2,1,0:T(8,128)} %get-tuple-element.50), channel_id=1, source_target_pairs={{0,1},{1,2},{2,3},{3,4},{4,5},{5,6},{6,7},{7,8},{8,9},{9,10},{10,1... | collective-permute-start | bytes 3145736 | tf_op jit(solution)/shard_map/ppermute | solution.py:19
  42.2 28.5 %collective-permute-start.3 = (f32[2,2,512,128]{3,2,1,0:T(8,128)}, f32[2,2,512,128]{3,2,1,0:T(8,128)}, u32[]{:S(2)}, u32[]{:S(2)}) collective-permute-start(f32[2,2,512,128]{3,2,1,0:T(8,128)} %get-tuple-element.51), channel_id=1, source_target_pairs={{1,0},{2,1},{3,2},{4,3},{5,4},{6,5},{7,6},{8,7},{9,8},{10,9},{11,1... | collective-permute-start | bytes 3145736 | tf_op jit(solution)/shard_map/ppermute | solution.py:21
  43.5 26.4 %all-to-all-start = ((f32[1,16,2,16,256]{4,3,2,0,1:T(8,128)}), f32[1,16,2,16,256]{4,3,2,0,1:T(8,128)S(1)}, u32[]{:S(2)}, u32[]{:S(2)}) async-start(f32[1,16,2,16,256]{4,3,2,0,1:T(8,128)} %bitcast.39), calls=%async_computation | async-start | bytes 1048576 | tf_op jit(solution)/shard_map/all_to_all | solution.py:117
  53.7 1088.9 %reduce-scatter.2.cloned.1.call-start = ((), (), s32[]{:S(2)}) async-start(), calls=%async_computation.3 | async-start | bytes 2113536 | tf_op jit(solution)/shard_map/reduce_scatter | solution.py:140
  218.2 4.5 copy-start.1
  351.2 2.8 copy-start.7
  465.3 11.6 %copy-start.8 = (f32[256,256]{1,0:T(8,128)S(1)}, f32[256,256]{1,0:T(8,128)}, u32[]{:S(2)}) copy-start(f32[256,256]{1,0:T(8,128)} %get-tuple-element.19) | copy-start | bytes 786436
  465.3 11.7 %copy-start.9 = (f32[256,256]{1,0:T(8,128)S(1)}, f32[256,256]{1,0:T(8,128)}, u32[]{:S(2)}) copy-start(f32[256,256]{1,0:T(8,128)} %get-tuple-element.42) | copy-start | bytes 786436
  465.3 11.7 %copy-start.10 = (f32[256,256]{1,0:T(8,128)S(1)}, f32[256,256]{1,0:T(8,128)}, u32[]{:S(2)}) copy-start(f32[256,256]{1,0:T(8,128)} %get-tuple-element.43) | copy-start | bytes 786436
  465.3 11.7 %copy-start.11 = (f32[256,256]{1,0:T(8,128)S(1)}, f32[256,256]{1,0:T(8,128)}, u32[]{:S(2)}) copy-start(f32[256,256]{1,0:T(8,128)} %get-tuple-element.46) | copy-start | bytes 786436
  491.7 7.3 copy-start.3
  491.7 7.3 copy-start.4
  491.7 7.3 copy-start.5
  491.7 7.3 copy-start.6
  494.6 24.6 %collective-permute-start.4 = (f32[2,2,128,512]{3,2,1,0:T(8,128)}, f32[2,2,128,512]{3,2,1,0:T(8,128)S(1)}, u32[]{:S(2)}, u32[]{:S(2)}) collective-permute-start(f32[2,2,128,512]{3,2,1,0:T(8,128)} %get-tuple-element.26), channel_id=1, source_target_pairs={{0,16},{16,32},{32,48},{48,64},{64,80},{80,96},{96,112},{1,17},{17... | collective-permute-start | bytes 3145736 | tf_op jit(solution)/shard_map/ppermute | solution.py:19
  497.6 45.7 %collective-permute-start.5 = (f32[2,2,128,512]{3,2,1,0:T(8,128)S(1)}, f32[2,2,128,512]{3,2,1,0:T(8,128)S(1)}, u32[]{:S(2)}, u32[]{:S(2)}) collective-permute-start(f32[2,2,128,512]{3,2,1,0:T(8,128)S(1)} %get-tuple-element.27), channel_id=1, source_target_pairs={{16,0},{32,16},{48,32},{64,48},{80,64},{96,80},{112,96},{17,1},{33... | collective-permute-start | bytes 3145736 | tf_op jit(solution)/shard_map/ppermute | solution.py:21
  543.3 10.2 copy-start
  545.2 4.3 collective-permute-start.6
  546.6 9.2 copy-start.13
  546.6 6.8 collective-permute-start.7
Sparse Core Ops, SparseCore 0:
  9.7 208.4 all-gather.1
  501.1 641.4 reduce-scatter.1
where the time goes:
time: 1160 us; the launch traced here: 1150 us
  waiting for transfers between devices  807 us (70%)
  matrix products  243 us (21%)
  local copies, waits for them, and re-layouts  35.9 us (3%)
  starting transfers between devices  25.7 us (2%)
  between operations  23.8 us (2%)
  other arithmetic  13.8 us (1%)
    reduce_scatter x1, waiting for transfers between devices, body(): lax.psum_scatter(grad_total.reshape(2 * mode_count * pattern_side, patter...  584 us
    dot_general x96, matrix products, matmul_high(): return jnp.einsum(form, first, second, precision=lax.Precision.HIGHEST)  243 us
    all_gather x1, waiting for transfers between devices, body(): probe_all = lax.all_gather(probe_rows, ('ty', 'tx'), axis=0, tiled=True)  145 us
    ppermute x4, waiting for transfers between devices, extended_2(): lax.ppermute(head, axis, [((i + 1) % count, i) for i in range(ends)])  42.1 us
    ppermute x4, waiting for transfers between devices, extended_2(): lax.ppermute(tail, axis, [(i, (i + 1) % count) for i in range(ends)])  30 us
    dynamic_update_slice x2, local copies, waits for them, and re-layouts, body(): lax.dynamic_update_slice(grad_buffer, current + grad_window, corner)  23.5 us
  transfers between devices with their start and end apart: 11, of which 9 were waited for; matrix products, arithmetic and copies ran while one was open for 2% of the time, Pallas kernels for 0%

commit v1 on v0

v1 whole, which is shorter than its diff:
```python
import functools

import jax
import jax.numpy as jnp
import ml_dtypes
import numpy as np
from jax import lax
from jax.experimental import pallas as pl
from jax.experimental.pallas import tpu as pltpu
from jax.sharding import Mesh
from jax.sharding import PartitionSpec as P

W = 256
H = 128
MODES = 4
SLOTS = 2
amp_floor = 0.5
f32 = jnp.float32
bf16 = jnp.bfloat16
VMEM_BYTES = 50 << 20


def real_form(a):
    return np.block([[a.real, -a.imag], [a.imag, a.real]])


def make_tables():
    k = np.arange(W)
    dft_matrix = np.exp(-2j * np.pi * ((k[:, None] * k[None, :]) % W) / W) / np.sqrt(W)
    freq = (k + H) % W - H
    phase = np.exp(2j * np.pi * ((freq * freq) % (4 * W)) / (4 * W))
    circ = dft_matrix.conj() @ np.diag(phase) @ dft_matrix
    c0, c1 = circ[:H, :H], circ[H:, :H]
    mats = [(c0 + c1) / 2, (c0 - c1) / 2, dft_matrix[0::2, :H], dft_matrix[1::2, :H]]
    high, low = [], []
    for mat in mats:
        full = real_form(mat)
        for form in (full, full.T):
            top = form.astype(np.float32).astype(ml_dtypes.bfloat16)
            high.append(top)
            low.append((form - top.astype(np.float64)).astype(np.float32).astype(ml_dtypes.bfloat16))
    return np.stack(high), np.stack(low)


def split(x):
    top = x.astype(bf16)
    return top, (x - top.astype(f32)).astype(bf16)


dot = functools.partial(jnp.dot, preferred_element_type=f32)


def left_product(tabs, i, x):
    top, rest = split(x)
    hi, lo = tabs
    return dot(hi[i], top) + dot(lo[i], top) + dot(hi[i], rest)


def right_product(tabs, i, x):
    top, rest = split(x)
    hi, lo = tabs
    return dot(top, hi[i]) + dot(top, lo[i]) + dot(rest, hi[i])


def halves(x, axis):
    return (x[:H], x[H:]) if axis == 0 else (x[:, :H], x[:, H:])


def one_side(tabs, axis, ia, ib, xr, xi, fold_in, fold_out):
    (ar, br), (ai, bi) = halves(xr, axis), halves(xi, axis)
    if fold_in:
        ar, br, ai, bi = ar + br, ar - br, ai + bi, ai - bi
    product = left_product if axis == 0 else right_product
    ya = product(tabs, ia, jnp.concatenate([ar, ai], axis))
    yb = product(tabs, ib, jnp.concatenate([br, bi], axis))
    if fold_out:
        ya, yb = ya + yb, ya - yb
    (ar, ai), (br, bi) = halves(ya, axis), halves(yb, axis)
    return jnp.concatenate([ar, br], axis), jnp.concatenate([ai, bi], axis)


def propagate(tabs, xr, xi, adjoint):
    t = 1 if adjoint else 0
    xr, xi = one_side(tabs, 0, 0 + t, 2 + t, xr, xi, True, True)
    return one_side(tabs, 1, 1 - t, 3 - t, xr, xi, True, True)


def dft(tabs, xr, xi):
    xr, xi = one_side(tabs, 0, 4, 6, xr, xi, True, False)
    return one_side(tabs, 1, 5, 7, xr, xi, True, False)


def dft_adjoint(tabs, xr, xi):
    xr, xi = one_side(tabs, 0, 5, 7, xr, xi, False, True)
    return one_side(tabs, 1, 4, 6, xr, xi, False, True)


def params():
    return pltpu.CompilerParams(vmem_limit_bytes=VMEM_BYTES)


def struct(*shape):
    return jax.ShapeDtypeStruct(shape, f32)


def whole(*shape):
    return pl.BlockSpec(shape, lambda *_: (0,) * len(shape))


TABLE_SPECS = [whole(8, W, W), whole(8, W, W)]
SMEM = pl.BlockSpec(memory_space=pltpu.SMEM)
mode_block = pl.BlockSpec((1, 2, W, W), lambda m, s: (m, 0, 0, 0))
slot_block = pl.BlockSpec((1, 2, W, W), lambda m, s: (s, 0, 0, 0))
both_block = pl.BlockSpec((1, 1, 2, W, W), lambda m, s: (m, s, 0, 0, 0))
VMEM = pl.BlockSpec(memory_space=pltpu.VMEM)


def extract_kernel(pos, mid, top, bot, lft, rgt, cl, cr, win, ext):
    for p in range(2):
        ext[p, H : H + W, H : H + W] = mid[p]
        ext[p, 0:H, H : H + W] = top[p]
        ext[p, H + W :, H : H + W] = bot[p]
        ext[p, H : H + W, 0:H] = lft[p]
        ext[p, H : H + W, H + W :] = rgt[p]
        ext[p, 0:H, 0:H] = cl[0, p]
        ext[p, H + W :, 0:H] = cl[1, p]
        ext[p, 0:H, H + W :] = cr[0, p]
        ext[p, H + W :, H + W :] = cr[1, p]
    for s in range(SLOTS):
        r = pos[s, 0]
        c = pos[s, 1]
        rows = pl.ds(pl.multiple_of(r // 8 * 8, 8), W + 8)
        cols = pl.ds(pl.multiple_of(c // H * H, H), W + H)
        for p in range(2):
            part = pltpu.roll(ext[p, rows, cols], lax.rem(W + H - c % H, W + H), 1)[:, :W]
            win[s, p] = pltpu.roll(part, lax.rem(W + 8 - r % 8, W + 8), 0)[:W]


def extract(pos, mid, top, bot, lft, rgt, cl, cr):
    return pl.pallas_call(
        extract_kernel,
        in_specs=[SMEM] + [VMEM] * 7,
        out_specs=VMEM,
        out_shape=struct(SLOTS, 2, W, W),
        scratch_shapes=[pltpu.VMEM((2, 2 * W, 2 * W), f32)],
        compiler_params=params(),
    )(pos, mid, top, bot, lft, rgt, cl, cr)


def place_kernel(pos, grad, mid, top, bot, lft, rgt, cl, cr, ext):
    ext[...] = jnp.zeros_like(ext)
    for s in range(SLOTS):
        r = pos[s, 0]
        c = pos[s, 1]
        rows = pl.ds(pl.multiple_of(r // 8 * 8, 8), W + 8)
        cols = pl.ds(pl.multiple_of(c // H * H, H), W + H)
        for p in range(2):
            part = jnp.concatenate([grad[s, p], jnp.zeros((8, W), f32)], 0)
            part = pltpu.roll(part, r % 8, 0)
            part = jnp.concatenate([part, jnp.zeros((W + 8, H), f32)], 1)
            ext[p, rows, cols] += pltpu.roll(part, c % H, 1)
    for p in range(2):
        mid[p] = ext[p, H : H + W, H : H + W]
        top[p] = ext[p, 0:H, H : H + W]
        bot[p] = ext[p, H + W :, H : H + W]
        lft[p] = ext[p, H : H + W, 0:H]
        rgt[p] = ext[p, H : H + W, H + W :]
        cl[0, p] = ext[p, 0:H, 0:H]
        cl[1, p] = ext[p, H + W :, 0:H]
        cr[0, p] = ext[p, 0:H, H + W :]
        cr[1, p] = ext[p, H + W :, H + W :]


def place(pos, grad):
    return pl.pallas_call(
        place_kernel,
        in_specs=[SMEM, VMEM],
        out_specs=[VMEM] * 7,
        out_shape=[
            struct(2, W, W),
            struct(2, H, W),
            struct(2, H, W),
            struct(2, W, H),
            struct(2, W, H),
            struct(2, 2, H, H),
            struct(2, 2, H, H),
        ],
        scratch_shapes=[pltpu.VMEM((2, 2 * W, 2 * W), f32)],
        compiler_params=params(),
    )(pos, grad)


def first_kernel(hi, lo, probe, win, u):
    pr, pi = probe[0, 0], probe[0, 1]
    a, b = win[0, 0], win[0, 1]
    ur, ui = propagate((hi, lo), pr * a - pi * b, pr * b + pi * a, False)
    u[0, 0, 0] = ur
    u[0, 0, 1] = ui


def first(tabs, probe, win):
    return pl.pallas_call(
        first_kernel,
        grid=(probe.shape[0], SLOTS),
        in_specs=TABLE_SPECS + [mode_block, slot_block],
        out_specs=both_block,
        out_shape=struct(probe.shape[0], SLOTS, 2, W, W),
        compiler_params=params(),
    )(*tabs, probe, win)


def second_kernel(hi, lo, u, win, far, intensity):
    m, s = pl.program_id(0), pl.program_id(1)
    ur, ui = u[0, 0, 0], u[0, 0, 1]
    a, b = win[0, 0], win[0, 1]
    fr, fi = dft((hi, lo), ur * a - ui * b, ur * b + ui * a)
    far[0, 0, 0] = fr
    far[0, 0, 1] = fi
    power = fr * fr + fi * fi

    @pl.when(m == 0)
    def _():
        intensity[s] = power

    @pl.when(m != 0)
    def _():
        intensity[s] += power


def second(tabs, u, win):
    return pl.pallas_call(
        second_kernel,
        grid=(MODES, SLOTS),
        in_specs=TABLE_SPECS + [both_block, slot_block],
        out_specs=[both_block, whole(SLOTS, W, W)],
        out_shape=[struct(MODES, SLOTS, 2, W, W), struct(SLOTS, W, W)],
        compiler_params=params(),
    )(*tabs, u, win)


def scale_kernel(loss_scale, counts, perm, meas, intensity, scale):
    order = perm[...]
    for s in range(SLOTS):
        x = meas[:, s].reshape(W, W)
        pieces = []
        for _ in range(3):
            piece = x.astype(bf16)
            x = x - piece.astype(f32)
            pieces.append(piece)
        x = (dot(order, pieces[0]) + dot(order, pieces[1])) + dot(order, pieces[2])
        pieces = []
        for _ in range(3):
            piece = x.astype(bf16)
            x = x - piece.astype(f32)
            pieces.append(piece)
        turned = order.T
        x = (dot(pieces[0], turned) + dot(pieces[1], turned)) + dot(pieces[2], turned)
        weight = jnp.where(s < counts[0, 0], 2.0 * loss_scale, 0.0)
        scale[s] = weight * (1.0 - x * lax.rsqrt(intensity[s] + amp_floor))


def residual_scale(loss_scale, counts, meas, intensity):
    perm = np.zeros((W, W), ml_dtypes.bfloat16)
    perm[np.arange(W), np.concatenate([np.arange(0, W, 2), np.arange(1, W, 2)])] = 1
    return pl.pallas_call(
        functools.partial(scale_kernel, loss_scale),
        in_specs=[SMEM, VMEM, VMEM, VMEM],
        out_specs=VMEM,
        out_shape=struct(SLOTS, W, W),
        compiler_params=params(),
    )(counts, perm, meas, intensity)


def third_kernel(hi, lo, scale, far, u, win, grad_u, grad_win):
    m, s = pl.program_id(0), pl.program_id(1)
    factor = scale[0]
    gr, gi = dft_adjoint((hi, lo), factor * far[0, 0, 0], factor * far[0, 0, 1])
    ur, ui = u[0, 0, 0], u[0, 0, 1]
    a, b = win[0, 0], win[0, 1]
    grad_u[0, 0, 0] = gr * a + gi * b
    grad_u[0, 0, 1] = gi * a - gr * b
    wr = gr * ur + gi * ui
    wi = gi * ur - gr * ui

    @pl.when(m == 0)
    def _():
        grad_win[s, 0] = wr
        grad_win[s, 1] = wi

    @pl.when(m != 0)
    def _():
        grad_win[s, 0] += wr
        grad_win[s, 1] += wi


def third(tabs, scale, far, u, win):
    return pl.pallas_call(
        third_kernel,
        grid=(MODES, SLOTS),
        in_specs=TABLE_SPECS
        + [pl.BlockSpec((1, W, W), lambda m, s: (s, 0, 0)), both_block, both_block, slot_block],
        out_specs=[both_block, whole(SLOTS, 2, W, W)],
        out_shape=[struct(MODES, SLOTS, 2, W, W), struct(SLOTS, 2, W, W)],
        compiler_params=params(),
    )(*tabs, scale, far, u, win)


def fourth_kernel(hi, lo, grad_u, probe, win, grad_probe, grad_win):
    m, s = pl.program_id(0), pl.program_id(1)
    gr, gi = propagate((hi, lo), grad_u[0, 0, 0], grad_u[0, 0, 1], True)
    pr, pi = probe[0, 0], probe[0, 1]
    a, b = win[0, 0], win[0, 1]
    qr = gr * a + gi * b
    qi = gi * a - gr * b
    wr = gr * pr + gi * pi
    wi = gi * pr - gr * pi

    @pl.when(s == 0)
    def _():
        grad_probe[0, 0] = qr
        grad_probe[0, 1] = qi

    @pl.when(s != 0)
    def _():
        grad_probe[0, 0] += qr
        grad_probe[0, 1] += qi

    @pl.when(m == 0)
    def _():
        grad_win[s, 0] = wr
        grad_win[s, 1] = wi

    @pl.when(m != 0)
    def _():
        grad_win[s, 0] += wr
        grad_win[s, 1] += wi


def fourth(tabs, grad_u, probe, win):
    return pl.pallas_call(
        fourth_kernel,
        grid=(MODES, SLOTS),
        in_specs=TABLE_SPECS + [both_block, mode_block, slot_block],
        out_specs=[mode_block, whole(SLOTS, 2, W, W)],
        out_shape=[struct(MODES, 2, W, W), struct(SLOTS, 2, W, W)],
        compiler_params=params(),
    )(*tabs, grad_u, probe, win)


TY = ("z", "xl")
TX = ("xh", "y", "c")
PLANE = ("xl", "xh", "y")
SWAP = [(0, 1), (1, 0)]


def up_perm(count):
    return [(i, i + 1) for i in range(count - 1)]


def down_perm(count):
    return [(i + 1, i) for i in range(count - 1)]


def fold_rims(pieces):
    mid, top, bot, lft, rgt, cl, cr = pieces
    from_right = lax.ppermute(cl, TX, down_perm(16))
    from_left = lax.ppermute(cr, TX, up_perm(16))
    lft = lax.ppermute(lft, TX, down_perm(16))
    rgt = lax.ppermute(rgt, TX, up_perm(16))
    rims = jnp.stack([top, bot])
    rims = rims + jnp.concatenate([from_left, from_right], 3)
    below = lax.ppermute(rims[0], TY, down_perm(8))
    above = lax.ppermute(rims[1], TY, up_perm(8))
    return mid + jnp.concatenate([above, below], 1) + jnp.concatenate([rgt, lft], 2)


def body(object_slices, probe_rows, measured, positions, counts):
    tabs = tuple(jnp.asarray(t) for t in make_tables())
    pos = positions[0, 0]
    wins = []
    for j in range(2):
        mid = object_slices[j]
        top = lax.ppermute(mid[:, H:], TY, up_perm(8))
        bot = lax.ppermute(mid[:, :H], TY, down_perm(8))
        lft = lax.ppermute(mid[:, :, H:], TX, up_perm(16))
        rgt = lax.ppermute(mid[:, :, :H], TX, down_perm(16))
        rims = jnp.stack([top, bot])
        cl = lax.ppermute(rims[..., H:], TX, up_perm(16))
        cr = lax.ppermute(rims[..., :H], TX, down_perm(16))
        wins.append(extract(pos, mid, top, bot, lft, rgt, cl, cr))
    spread = jnp.broadcast_to(probe_rows[None], (32, 16, W))
    own = lax.all_to_all(spread, PLANE + ("c",), split_axis=0, concat_axis=0, tiled=True)
    own = own.reshape(2, W, W)
    chunks = [own] + [
        lax.ppermute(own, "z", [((i + j) % 4, i) for i in range(4)]) for j in range(1, 4)
    ]
    probe = jnp.stack(chunks)
    meas = lax.all_to_all(measured[0], TX, split_axis=0, concat_axis=0, tiled=True)
    u = first(tabs, probe, wins[0])
    far, intensity = second(tabs, u, wins[1])
    scale = residual_scale(1.0 / 16.0, counts, meas, intensity)
    grad_u, grad_win1 = third(tabs, scale, far, u, wins[1])
    folded1 = fold_rims(place(pos, grad_win1))
    grad_probe, grad_win0 = fourth(tabs, grad_u, probe, wins[0])
    folded0 = fold_rims(place(pos, grad_win0))
    core = lax.axis_index("c")
    cut = grad_probe.reshape(MODES, 16, 2, 16, W)
    mine = jnp.where(core == 0, cut[:, :, 0], cut[:, :, 1])
    other = jnp.where(core == 0, cut[:, :, 1], cut[:, :, 0])
    mine = mine + lax.ppermute(other, "c", SWAP)
    total = mine[0]
    for j in range(1, 4):
        total = total + lax.ppermute(mine[j], "z", [(i, (i + j) % 4) for i in range(4)])
    pieces = lax.all_to_all(total, PLANE, split_axis=0, concat_axis=0, tiled=True)
    return jnp.stack([folded0, folded1]), jnp.sum(pieces.reshape(16, 16, W), 0)


def solution(mesh):
    fine = Mesh(mesh.devices.reshape(4, 2, 2, 4, 2), ("z", "xl", "xh", "y", "c"))
    in_specs = (
        P(None, None, TY, TX),
        P(TY + TX, None),
        P(TY, None, None, TX, None),
        P(TY, TX, None, None),
        P(TY, TX),
    )
    out_specs = (P(None, None, TY, TX), P(TY + TX, None))
    return jax.shard_map(
        body, mesh=fine, in_specs=in_specs, out_specs=out_specs, check_vma=False
    )
```

time: 1160 us -> 203 us (0.17)
  the two profiles are of different devices: /device:TPU:0 before, /device:TPU:32 now
where the time goes in v1:
time: 203 us; the launch traced here: 201 us
  starting transfers between devices  123 us (61%)
  Pallas kernels  50.7 us (25%)
  other arithmetic  11.1 us (5%)
  waiting for transfers between devices  8.39 us (4%)
  local copies, waits for them, and re-layouts  5.89 us (3%)
    all_to_all x1, starting transfers between devices, body(): lax.all_to_all(total, PLANE, split_axis=0, concat_axis=0, tiled=True)  21.9 us
    all_to_all x1, starting transfers between devices, body(): lax.all_to_all(measured[0], TX, split_axis=0, concat_axis=0, tiled=True)  14.1 us
    ppermute x2, starting transfers between devices, fold_rims(): below = lax.ppermute(rims[0], TY, down_perm(8))  11.6 us
    pallas_call x1, Pallas kernels, third(): pl.pallas_call(third_kernel, grid=(MODES, SLOTS), in_specs=TABLE_SPECS +...  11.4 us
    all_to_all x1, starting transfers between devices, body(): lax.all_to_all(spread, PLANE + ('c',), split_axis=0, concat_axis=0, tiled...  11.4 us
    pallas_call x1, Pallas kernels, fourth(): pl.pallas_call(fourth_kernel, grid=(MODES, SLOTS), in_specs=TABLE_SPECS +...  11.1 us
    pallas_call x1, Pallas kernels, second(): pl.pallas_call(second_kernel, grid=(MODES, SLOTS), in_specs=TABLE_SPECS +...  9.74 us
    pallas_call x1, Pallas kernels, first(): pl.pallas_call(first_kernel, grid=(probe.shape[0], SLOTS), in_specs=TABLE...  9.59 us
  transfers between devices with their start and end apart: 34, of which 2 were waited for; matrix products, arithmetic and copies ran while one was open for 5% of the time, Pallas kernels for 13%

profile of v1, /device:TPU:32, one launch (start us, length us, event | category | flops | bytes accessed | tf_op | source)
XLA Modules:
  0.0 201.0 jit_solution(14725710602459447376)
XLA Ops:
  2.0 3.4 %collective-permute-start.3 = (f32[2,128,256]{2,1,0:T(8,128)S(1)}, f32[2,128,256]{2,1,0:T(8,128)S(1)}, u32[]{:S(2)}, u32[]{:S(2)}) collective-permute-start(f32[2,128,256]{2,1,0:T(8,128)S(1)} %get-tuple-element.62), channel_id=1, source_target_pairs={{0,16},{16,32},{32,48},{48,64},{64,80},{80,96},{96,112},{1,17},{17... | collective-permute-start | bytes 786440 | tf_op jit(solution)/shard_map/ppermute | solution.py:383
  5.4 3.3 %collective-permute-start.4 = (f32[2,128,256]{2,1,0:T(8,128)S(1)}, f32[2,128,256]{2,1,0:T(8,128)S(1)}, u32[]{:S(2)}, u32[]{:S(2)}) collective-permute-start(f32[2,128,256]{2,1,0:T(8,128)S(1)} %get-tuple-element.61), channel_id=1, source_target_pairs={{16,0},{32,16},{48,32},{64,48},{80,64},{96,80},{112,96},{17,1},{33... | collective-permute-start | bytes 786440 | tf_op jit(solution)/shard_map/ppermute | solution.py:384
  12.2 11.4 %all-to-all-start.1 = ((f32[32,16,256]{2,1,0:T(8,128)}), f32[32,16,256]{2,1,0:T(8,128)}, u32[]{:S(2)}, u32[]{:S(2)}) async-start(f32[32,16,256]{2,1,0:T(8,128)} %broadcast_in_dim.2), calls=%async_computation.1 | async-start | bytes 1048576 | tf_op jit(solution)/shard_map/all_to_all | solution.py:392
  23.7 3.6 %collective-permute-start.9 = (f32[2,128,256]{2,1,0:T(8,128)S(1)}, f32[2,128,256]{2,1,0:T(8,128)S(1)}, u32[]{:S(2)}, u32[]{:S(2)}) collective-permute-start(f32[2,128,256]{2,1,0:T(8,128)S(1)} %get-tuple-element.56), channel_id=1, source_target_pairs={{0,16},{16,32},{32,48},{48,64},{64,80},{80,96},{96,112},{1,17},{17... | collective-permute-start | bytes 786440 | tf_op jit(solution)/shard_map/ppermute | solution.py:383
  28.2 3.1 %collective-permute-start.10 = (f32[2,128,256]{2,1,0:T(8,128)S(1)}, f32[2,128,256]{2,1,0:T(8,128)S(1)}, u32[]{:S(2)}, u32[]{:S(2)}) collective-permute-start(f32[2,128,256]{2,1,0:T(8,128)S(1)} %get-tuple-element.55), channel_id=1, source_target_pairs={{16,0},{32,16},{48,32},{64,48},{80,64},{96,80},{112,96},{17,1},{33... | collective-permute-start | bytes 786440 | tf_op jit(solution)/shard_map/ppermute | solution.py:384
  31.3 1.6 collective-permute-start.11
  35.1 4.7 %collective-permute-start.7 = (f32[2,2,128,128]{3,2,1,0:T(8,128)}, f32[2,2,128,128]{3,2,1,0:T(8,128)S(1)}, u32[]{:S(2)}, u32[]{:S(2)}) collective-permute-start(f32[2,2,128,128]{3,2,1,0:T(8,128)} %get-tuple-element.58), channel_id=1, source_target_pairs={{0,1},{1,2},{2,3},{3,4},{4,5},{5,6},{6,7},{7,8},{8,9},{9,10},{10,1... | collective-permute-start | bytes 786440 | tf_op jit(solution)/shard_map/ppermute | solution.py:388
  41.1 2.2 %collective-permute-done.10.bot = f32[2,128,256]{2,1,0:T(8,128)S(1)} collective-permute-done((f32[2,128,256]{2,1,0:T(8,128)S(1)}, f32[2,128,256]{2,1,0:T(8,128)S(1)}, u32[]{:S(2)}, u32[]{:S(2)}) %collective-permute-start.10) | collective-permute-done | bytes 262176 | tf_op jit(solution)/shard_map/ppermute | solution.py:384
  43.3 3.4 %collective-permute-start.1 = (f32[2,256,256]{2,1,0:T(8,128)}, f32[2,256,256]{2,1,0:T(8,128)}, u32[]{:S(2)}, u32[]{:S(2)}) collective-permute-start(f32[2,256,256]{2,1,0:T(8,128)} %bitcast.3), channel_id=1, source_target_pairs={{64,0},{96,32},{0,64},{32,96},{65,1},{97,33},{1,65},{33,97},{66,2}... | collective-permute-start | bytes 1572872 | tf_op jit(solution)/shard_map/ppermute | solution.py:395
  46.8 14.1 %all-to-all-start = ((f32[16,2,16,256]{3,2,1,0:T(8,128)}), f32[16,2,16,256]{3,2,1,0:T(8,128)}, u32[]{:S(2)}, u32[]{:S(2)}) async-start(f32[16,2,16,256]{3,2,1,0:T(8,128)} %bitcast.78), calls=%async_computation | async-start | bytes 1048576 | tf_op jit(solution)/shard_map/all_to_all | solution.py:398
  62.5 3.0 %collective-permute-start.13 = (f32[2,2,128,128]{3,2,1,0:T(8,128)}, f32[2,2,128,128]{3,2,1,0:T(8,128)}, u32[]{:S(2)}, u32[]{:S(2)}) collective-permute-start(f32[2,2,128,128]{3,2,1,0:T(8,128)} %get-tuple-element.52), channel_id=1, source_target_pairs={{0,1},{1,2},{2,3},{3,4},{4,5},{5,6},{6,7},{7,8},{8,9},{9,10},{10,1... | collective-permute-start | bytes 786440 | tf_op jit(solution)/shard_map/ppermute | solution.py:388
  69.4 1.9 shard_map.95.win
  71.3 2.2 %shard_map.97.win = f32[2,2,256,256]{3,2,1,0:T(8,128)S(1)} custom-call(s32[2,2]{1,0:T(2,128)S(1)} %bitcast.73, f32[2,256,256]{2,1,0:T(8,128)S(1)} %get-tuple-element.45.mid, f32[2,128,256]{2,1,0:T(8,128)S(1)} %collective-permute-done.9.top, f32[2,128,256]{2,1,0:T(8,128)S(1)} %collective-permute-done.10.bot, f32[2,256,128]{2,1,0:T(8,128)S(1)} %copy-done.7, ...), custom_call_target="tpu_custom_call" | custom-call | tf_op jit(solution)/shard_map/pallas_call | solution.py:140
  73.6 3.3 %pad_maximum_fusion.probe = f32[4,2,256,256]{3,2,1,0:T(8,128)} fusion(f32[1,2,256,256]{3,2,1,0:T(8,128)} %bitcast.6, f32[1,2,256,256]{3,2,1,0:T(8,128)} %bitcast.5, f32[1,2,256,256]{3,2,1,0:T(8,128)} %bitcast.4, f32[1,2,256,256]{3,2,1,0:T(8,128)} %bitcast.2), kind=kLoop, calls=%fused_computation | loop fusion | flops 1572864 | bytes 4194304 | tf_op jit(solution)/shard_map/stack | solution.py:397
  77.0 9.6 %shard_map.96.u = f32[4,2,2,256,256]{4,3,2,1,0:T(8,128)} custom-call(bf16[8,256,256]{2,1,0:T(8,128)(2,1)S(1)} %copy-done, bf16[8,256,256]{2,1,0:T(8,128)(2,1)S(1)} %copy-done.1, f32[4,2,256,256]{3,2,1,0:T(8,128)} %pad_maximum_fusion.probe, f32[2,2,256,256]{3,2,1,0:T(8,128)S(1)} %shard_map.95.win), custom_call_target="tpu_custom_call" | custom-call | tf_op jit(solution)/shard_map/pallas_call | solution.py:202
  86.6 9.7 %shard_map.98 = (f32[4,2,2,256,256]{4,3,2,1,0:T(8,128)}, f32[2,256,256]{2,1,0:T(8,128)S(1)}) custom-call(bf16[8,256,256]{2,1,0:T(8,128)(2,1)S(1)} %copy-done, bf16[8,256,256]{2,1,0:T(8,128)(2,1)S(1)} %copy-done.1, f32[4,2,2,256,256]{4,3,2,1,0:T(8,128)} %shard_map.96.u, f32[2,2,256,256]{3,2,1,0:T(8,128)S(1)} %shard_map.97.win), custom_call_target="tpu_custom_call" | custom-call | tf_op jit(solution)/shard_map/pallas_call | solution.py:231
  96.3 1.9 shard_map.99.scale
  98.2 11.4 %shard_map.100 = (f32[4,2,2,256,256]{4,3,2,1,0:T(8,128)}, f32[2,2,256,256]{3,2,1,0:T(8,128)S(1)}) custom-call(bf16[8,256,256]{2,1,0:T(8,128)(2,1)S(1)} %copy-done, bf16[8,256,256]{2,1,0:T(8,128)(2,1)S(1)} %copy-done.1, f32[2,256,256]{2,1,0:T(8,128)S(1)} %shard_map.99.scale, f32[4,2,2,256,256]{4,3,2,1,0:T(8,128)} %get-tuple-element.23.far, ...), custom_call_target="tpu_custom_call" | custom-call | tf_op jit(solution)/shard_map/pallas_call | solution.py:297
  109.6 11.1 %shard_map.101 = (f32[4,2,256,256]{3,2,1,0:T(8,128)}, f32[2,2,256,256]{3,2,1,0:T(8,128)S(1)}) custom-call(bf16[8,256,256]{2,1,0:T(8,128)(2,1)S(1)} %copy-done, bf16[8,256,256]{2,1,0:T(8,128)(2,1)S(1)} %copy-done.1, f32[4,2,2,256,256]{4,3,2,1,0:T(8,128)} %get-tuple-element.24.grad_u, f32[4,2,256,256]{3,2,1,0:T(8,128)} %pad_maximum_fusion.probe, ...), custom_call_target="tpu_custom_call" | custom-call | tf_op jit(solution)/shard_map/pallas_call | solution.py:340
  120.7 1.8 select_bitcast_fusion
  122.5 3.2 %collective-permute-start.27 = (f32[4,16,16,256]{3,2,1,0:T(8,128)S(1)}, f32[4,16,16,256]{3,2,1,0:T(8,128)S(1)}, u32[]{:S(2)}, u32[]{:S(2)}) collective-permute-start(f32[4,16,16,256]{3,2,1,0:T(8,128)S(1)} %select_bitcast_fusion), channel_id=1, source_target_pairs={{0,1},{1,0},{2,3},{3,2},{4,5},{5,4},{6,7},{7,6},{8,9},{9,8},{10,11... | collective-permute-start | bytes 3145736 | tf_op jit(solution)/shard_map/ppermute | solution.py:410
  127.1 2.1 %collective-permute-start.15 = (f32[2,2,128,128]{3,2,1,0:T(8,128)S(1)}, f32[2,2,128,128]{3,2,1,0:T(8,128)S(1)}, u32[]{:S(2)}, u32[]{:S(2)}) collective-permute-start(f32[2,2,128,128]{3,2,1,0:T(8,128)S(1)} %get-tuple-element.29), channel_id=1, source_target_pairs={{0,1},{1,2},{2,3},{3,4},{4,5},{5,6},{6,7},{7,8},{8,9},{9,10},{10,1... | collective-permute-start | bytes 786440 | tf_op jit(solution)/shard_map/ppermute | solution.py:367
  130.5 3.8 %collective-permute-start.19 = (f32[2,256,128]{2,1,0:T(8,128)S(1)}, f32[2,256,128]{2,1,0:T(8,128)S(1)}, u32[]{:S(2)}, u32[]{:S(2)}) collective-permute-start(f32[2,256,128]{2,1,0:T(8,128)S(1)} %get-tuple-element.31), channel_id=1, source_target_pairs={{0,1},{1,2},{2,3},{3,4},{4,5},{5,6},{6,7},{7,8},{8,9},{9,10},{10,1... | collective-permute-start | bytes 786440 | tf_op jit(solution)/shard_map/ppermute | solution.py:369
  137.1 4.3 %collective-permute-start.21 = (f32[2,2,128,128]{3,2,1,0:T(8,128)S(1)}, f32[2,2,128,128]{3,2,1,0:T(8,128)S(1)}, u32[]{:S(2)}, u32[]{:S(2)}) collective-permute-start(f32[2,2,128,128]{3,2,1,0:T(8,128)S(1)} %get-tuple-element.37), channel_id=1, source_target_pairs={{0,1},{1,2},{2,3},{3,4},{4,5},{5,6},{6,7},{7,8},{8,9},{9,10},{10,1... | collective-permute-start | bytes 786440 | tf_op jit(solution)/shard_map/ppermute | solution.py:367
  142.8 2.1 %collective-permute-start.17 = (f32[2,128,256]{2,1,0:T(8,128)S(1)}, f32[2,128,256]{2,1,0:T(8,128)S(1)}, u32[]{:S(2)}, u32[]{:S(2)}) collective-permute-start(f32[2,128,256]{2,1,0:T(8,128)S(1)} %get-tuple-element.47), channel_id=1, source_target_pairs={{0,16},{16,32},{32,48},{48,64},{64,80},{80,96},{96,112},{1,17},{17... | collective-permute-start | bytes 786440 | tf_op jit(solution)/shard_map/ppermute | solution.py:373
  145.3 4.8 %collective-permute-start.18 = (f32[2,128,256]{2,1,0:T(8,128)S(1)}, f32[2,128,256]{2,1,0:T(8,128)S(1)}, u32[]{:S(2)}, u32[]{:S(2)}) collective-permute-start(f32[2,128,256]{2,1,0:T(8,128)S(1)} %get-tuple-element.48), channel_id=1, source_target_pairs={{16,0},{32,16},{48,32},{64,48},{80,64},{96,80},{112,96},{17,1},{33... | collective-permute-start | bytes 786440 | tf_op jit(solution)/shard_map/ppermute | solution.py:372
  151.1 2.6 %collective-permute-start.30 = (f32[16,16,256]{2,1,0:T(8,128)S(1)}, f32[16,16,256]{2,1,0:T(8,128)S(1)}, u32[]{:S(2)}, u32[]{:S(2)}) collective-permute-start(f32[16,16,256]{2,1,0:T(8,128)S(1)} %get-tuple-element.43), channel_id=1, source_target_pairs={{0,96},{32,0},{64,32},{96,64},{1,97},{33,1},{65,33},{97,65},{2,98}... | collective-permute-start | bytes 786440 | tf_op jit(solution)/shard_map/ppermute | solution.py:413
  153.7 5.2 %collective-permute-start.25 = (f32[2,256,128]{2,1,0:T(8,128)S(1)}, f32[2,256,128]{2,1,0:T(8,128)}, u32[]{:S(2)}, u32[]{:S(2)}) collective-permute-start(f32[2,256,128]{2,1,0:T(8,128)S(1)} %get-tuple-element.39), channel_id=1, source_target_pairs={{0,1},{1,2},{2,3},{3,4},{4,5},{5,6},{6,7},{7,8},{8,9},{9,10},{10,1... | collective-permute-start | bytes 786440 | tf_op jit(solution)/shard_map/ppermute | solution.py:369
  160.2 1.9 collective-permute-start.23
  162.2 6.8 %collective-permute-start.24 = (f32[2,128,256]{2,1,0:T(8,128)S(1)}, f32[2,128,256]{2,1,0:T(8,128)}, u32[]{:S(2)}, u32[]{:S(2)}) collective-permute-start(f32[2,128,256]{2,1,0:T(8,128)S(1)} %get-tuple-element.50), channel_id=1, source_target_pairs={{16,0},{32,16},{48,32},{64,48},{80,64},{96,80},{112,96},{17,1},{33... | collective-permute-start | bytes 786440 | tf_op jit(solution)/shard_map/ppermute | solution.py:372
  169.9 21.9 %all-to-all-start.2 = ((f32[16,16,256]{2,1,0:T(8,128)}), f32[16,16,256]{2,1,0:T(8,128)S(1)}, u32[]{:S(2)}, u32[]{:S(2)}) async-start(f32[16,16,256]{2,1,0:T(8,128)} %fusion.10), calls=%async_computation.2 | async-start | bytes 524288 | tf_op jit(solution)/shard_map/all_to_all | solution.py:414
  194.2 6.1 %all-to-all-done.2 = f32[16,16,256]{2,1,0:T(8,128)S(1)} async-done(((f32[16,16,256]{2,1,0:T(8,128)}), f32[16,16,256]{2,1,0:T(8,128)S(1)}, u32[]{:S(2)}, u32[]{:S(2)}) %all-to-all-start.2) | async-done | bytes 262176 | tf_op jit(solution)/shard_map/all_to_all | solution.py:414
  (98 shorter events, 27.5 us)
Async XLA Ops:
  2.0 26.3 %collective-permute-start.3 = (f32[2,128,256]{2,1,0:T(8,128)S(1)}, f32[2,128,256]{2,1,0:T(8,128)S(1)}, u32[]{:S(2)}, u32[]{:S(2)}) collective-permute-start(f32[2,128,256]{2,1,0:T(8,128)S(1)} %get-tuple-element.62), channel_id=1, source_target_pairs={{0,16},{16,32},{32,48},{48,64},{64,80},{80,96},{96,112},{1,17},{17... | collective-permute-start | bytes 786440 | tf_op jit(solution)/shard_map/ppermute | solution.py:383
  5.4 26.0 %collective-permute-start.4 = (f32[2,128,256]{2,1,0:T(8,128)S(1)}, f32[2,128,256]{2,1,0:T(8,128)S(1)}, u32[]{:S(2)}, u32[]{:S(2)}) collective-permute-start(f32[2,128,256]{2,1,0:T(8,128)S(1)} %get-tuple-element.61), channel_id=1, source_target_pairs={{16,0},{32,16},{48,32},{64,48},{80,64},{96,80},{112,96},{17,1},{33... | collective-permute-start | bytes 786440 | tf_op jit(solution)/shard_map/ppermute | solution.py:384
  8.8 24.1 %collective-permute-start.5 = (f32[2,256,128]{2,1,0:T(8,128)S(1)}, f32[2,256,128]{2,1,0:T(8,128)S(1)}, u32[]{:S(2)}, u32[]{:S(2)}) collective-permute-start(f32[2,256,128]{2,1,0:T(8,128)S(1)} %get-tuple-element.60), channel_id=1, source_target_pairs={{0,1},{1,2},{2,3},{3,4},{4,5},{5,6},{6,7},{7,8},{8,9},{9,10},{10,1... | collective-permute-start | bytes 786440 | tf_op jit(solution)/shard_map/ppermute | solution.py:385
  10.1 25.0 %collective-permute-start.6 = (f32[2,256,128]{2,1,0:T(8,128)S(1)}, f32[2,256,128]{2,1,0:T(8,128)S(1)}, u32[]{:S(2)}, u32[]{:S(2)}) collective-permute-start(f32[2,256,128]{2,1,0:T(8,128)S(1)} %get-tuple-element.59), channel_id=1, source_target_pairs={{1,0},{2,1},{3,2},{4,3},{5,4},{6,5},{7,6},{8,7},{9,8},{10,9},{11,1... | collective-permute-start | bytes 786440 | tf_op jit(solution)/shard_map/ppermute | solution.py:386
  12.2 31.0 %all-to-all-start.1 = ((f32[32,16,256]{2,1,0:T(8,128)}), f32[32,16,256]{2,1,0:T(8,128)}, u32[]{:S(2)}, u32[]{:S(2)}) async-start(f32[32,16,256]{2,1,0:T(8,128)} %broadcast_in_dim.2), calls=%async_computation.1 | async-start | bytes 1048576 | tf_op jit(solution)/shard_map/all_to_all | solution.py:392
  23.7 16.1 %collective-permute-start.9 = (f32[2,128,256]{2,1,0:T(8,128)S(1)}, f32[2,128,256]{2,1,0:T(8,128)S(1)}, u32[]{:S(2)}, u32[]{:S(2)}) collective-permute-start(f32[2,128,256]{2,1,0:T(8,128)S(1)} %get-tuple-element.56), channel_id=1, source_target_pairs={{0,16},{16,32},{32,48},{48,64},{64,80},{80,96},{96,112},{1,17},{17... | collective-permute-start | bytes 786440 | tf_op jit(solution)/shard_map/ppermute | solution.py:383
  28.2 15.0 %collective-permute-start.10 = (f32[2,128,256]{2,1,0:T(8,128)S(1)}, f32[2,128,256]{2,1,0:T(8,128)S(1)}, u32[]{:S(2)}, u32[]{:S(2)}) collective-permute-start(f32[2,128,256]{2,1,0:T(8,128)S(1)} %get-tuple-element.55), channel_id=1, source_target_pairs={{16,0},{32,16},{48,32},{64,48},{80,64},{96,80},{112,96},{17,1},{33... | collective-permute-start | bytes 786440 | tf_op jit(solution)/shard_map/ppermute | solution.py:384
  31.3 11.9 %collective-permute-start.11 = (f32[2,256,128]{2,1,0:T(8,128)}, f32[2,256,128]{2,1,0:T(8,128)S(1)}, u32[]{:S(2)}, u32[]{:S(2)}) collective-permute-start(f32[2,256,128]{2,1,0:T(8,128)} %get-tuple-element.54), channel_id=1, source_target_pairs={{0,1},{1,2},{2,3},{3,4},{4,5},{5,6},{6,7},{7,8},{8,9},{9,10},{10,1... | collective-permute-start | bytes 786440 | tf_op jit(solution)/shard_map/ppermute | solution.py:385
  32.9 13.7 %collective-permute-start.12 = (f32[2,256,128]{2,1,0:T(8,128)}, f32[2,256,128]{2,1,0:T(8,128)S(1)}, u32[]{:S(2)}, u32[]{:S(2)}) collective-permute-start(f32[2,256,128]{2,1,0:T(8,128)} %get-tuple-element.53), channel_id=1, source_target_pairs={{1,0},{2,1},{3,2},{4,3},{5,4},{6,5},{7,6},{8,7},{9,8},{10,9},{11,1... | collective-permute-start | bytes 786440 | tf_op jit(solution)/shard_map/ppermute | solution.py:386
  35.1 26.7 %collective-permute-start.7 = (f32[2,2,128,128]{3,2,1,0:T(8,128)}, f32[2,2,128,128]{3,2,1,0:T(8,128)S(1)}, u32[]{:S(2)}, u32[]{:S(2)}) collective-permute-start(f32[2,2,128,128]{3,2,1,0:T(8,128)} %get-tuple-element.58), channel_id=1, source_target_pairs={{0,1},{1,2},{2,3},{3,4},{4,5},{5,6},{6,7},{7,8},{8,9},{9,10},{10,1... | collective-permute-start | bytes 786440 | tf_op jit(solution)/shard_map/ppermute | solution.py:388
  39.8 25.7 %collective-permute-start.8 = (f32[2,2,128,128]{3,2,1,0:T(8,128)}, f32[2,2,128,128]{3,2,1,0:T(8,128)}, u32[]{:S(2)}, u32[]{:S(2)}) collective-permute-start(f32[2,2,128,128]{3,2,1,0:T(8,128)} %get-tuple-element.57), channel_id=1, source_target_pairs={{1,0},{2,1},{3,2},{4,3},{5,4},{6,5},{7,6},{8,7},{9,8},{10,9},{11,1... | collective-permute-start | bytes 786440 | tf_op jit(solution)/shard_map/ppermute | solution.py:389
  43.3 30.3 %collective-permute-start = (f32[2,256,256]{2,1,0:T(8,128)}, f32[2,256,256]{2,1,0:T(8,128)}, u32[]{:S(2)}, u32[]{:S(2)}) collective-permute-start(f32[2,256,256]{2,1,0:T(8,128)} %bitcast.3), channel_id=1, source_target_pairs={{32,0},{64,32},{96,64},{0,96},{33,1},{65,33},{97,65},{1,97},{34,2}... | collective-permute-start | bytes 1572872 | tf_op jit(solution)/shard_map/ppermute | solution.py:395
  43.3 30.3 %collective-permute-start.1 = (f32[2,256,256]{2,1,0:T(8,128)}, f32[2,256,256]{2,1,0:T(8,128)}, u32[]{:S(2)}, u32[]{:S(2)}) collective-permute-start(f32[2,256,256]{2,1,0:T(8,128)} %bitcast.3), channel_id=1, source_target_pairs={{64,0},{96,32},{0,64},{32,96},{65,1},{97,33},{1,65},{33,97},{66,2}... | collective-permute-start | bytes 1572872 | tf_op jit(solution)/shard_map/ppermute | solution.py:395
  46.7 26.9 %collective-permute-start.2 = (f32[2,256,256]{2,1,0:T(8,128)}, f32[2,256,256]{2,1,0:T(8,128)}, u32[]{:S(2)}, u32[]{:S(2)}) collective-permute-start(f32[2,256,256]{2,1,0:T(8,128)} %bitcast.3), channel_id=1, source_target_pairs={{96,0},{0,32},{32,64},{64,96},{97,1},{1,33},{33,65},{65,97},{98,2}... | collective-permute-start | bytes 1572872 | tf_op jit(solution)/shard_map/ppermute | solution.py:395
  46.8 49.5 %all-to-all-start = ((f32[16,2,16,256]{3,2,1,0:T(8,128)}), f32[16,2,16,256]{3,2,1,0:T(8,128)}, u32[]{:S(2)}, u32[]{:S(2)}) async-start(f32[16,2,16,256]{3,2,1,0:T(8,128)} %bitcast.78), calls=%async_computation | async-start | bytes 1048576 | tf_op jit(solution)/shard_map/all_to_all | solution.py:398
  122.5 20.3 %collective-permute-start.27 = (f32[4,16,16,256]{3,2,1,0:T(8,128)S(1)}, f32[4,16,16,256]{3,2,1,0:T(8,128)S(1)}, u32[]{:S(2)}, u32[]{:S(2)}) collective-permute-start(f32[4,16,16,256]{3,2,1,0:T(8,128)S(1)} %select_bitcast_fusion), channel_id=1, source_target_pairs={{0,1},{1,0},{2,3},{3,2},{4,5},{5,4},{6,7},{7,6},{8,9},{9,8},{10,11... | collective-permute-start | bytes 3145736 | tf_op jit(solution)/shard_map/ppermute | solution.py:410
  127.1 9.9 %collective-permute-start.15 = (f32[2,2,128,128]{3,2,1,0:T(8,128)S(1)}, f32[2,2,128,128]{3,2,1,0:T(8,128)S(1)}, u32[]{:S(2)}, u32[]{:S(2)}) collective-permute-start(f32[2,2,128,128]{3,2,1,0:T(8,128)S(1)} %get-tuple-element.29), channel_id=1, source_target_pairs={{0,1},{1,2},{2,3},{3,4},{4,5},{5,6},{6,7},{7,8},{8,9},{9,10},{10,1... | collective-permute-start | bytes 786440 | tf_op jit(solution)/shard_map/ppermute | solution.py:367
  129.2 12.1 %collective-permute-start.16 = (f32[2,2,128,128]{3,2,1,0:T(8,128)S(1)}, f32[2,2,128,128]{3,2,1,0:T(8,128)S(1)}, u32[]{:S(2)}, u32[]{:S(2)}) collective-permute-start(f32[2,2,128,128]{3,2,1,0:T(8,128)S(1)} %get-tuple-element.30), channel_id=1, source_target_pairs={{1,0},{2,1},{3,2},{4,3},{5,4},{6,5},{7,6},{8,7},{9,8},{10,9},{11,1... | collective-permute-start | bytes 786440 | tf_op jit(solution)/shard_map/ppermute | solution.py:366
  130.5 14.8 %collective-permute-start.19 = (f32[2,256,128]{2,1,0:T(8,128)S(1)}, f32[2,256,128]{2,1,0:T(8,128)S(1)}, u32[]{:S(2)}, u32[]{:S(2)}) collective-permute-start(f32[2,256,128]{2,1,0:T(8,128)S(1)} %get-tuple-element.31), channel_id=1, source_target_pairs={{0,1},{1,2},{2,3},{3,4},{4,5},{5,6},{6,7},{7,8},{8,9},{9,10},{10,1... | collective-permute-start | bytes 786440 | tf_op jit(solution)/shard_map/ppermute | solution.py:369
  134.3 16.8 %collective-permute-start.20 = (f32[2,256,128]{2,1,0:T(8,128)S(1)}, f32[2,256,128]{2,1,0:T(8,128)S(1)}, u32[]{:S(2)}, u32[]{:S(2)}) collective-permute-start(f32[2,256,128]{2,1,0:T(8,128)S(1)} %get-tuple-element.32), channel_id=1, source_target_pairs={{1,0},{2,1},{3,2},{4,3},{5,4},{6,5},{7,6},{8,7},{9,8},{10,9},{11,1... | collective-permute-start | bytes 786440 | tf_op jit(solution)/shard_map/ppermute | solution.py:368
  137.1 13.1 %collective-permute-start.21 = (f32[2,2,128,128]{3,2,1,0:T(8,128)S(1)}, f32[2,2,128,128]{3,2,1,0:T(8,128)S(1)}, u32[]{:S(2)}, u32[]{:S(2)}) collective-permute-start(f32[2,2,128,128]{3,2,1,0:T(8,128)S(1)} %get-tuple-element.37), channel_id=1, source_target_pairs={{0,1},{1,2},{2,3},{3,4},{4,5},{5,6},{6,7},{7,8},{8,9},{9,10},{10,1... | collective-permute-start | bytes 786440 | tf_op jit(solution)/shard_map/ppermute | solution.py:367
  141.4 8.9 %collective-permute-start.22 = (f32[2,2,128,128]{3,2,1,0:T(8,128)S(1)}, f32[2,2,128,128]{3,2,1,0:T(8,128)S(1)}, u32[]{:S(2)}, u32[]{:S(2)}) collective-permute-start(f32[2,2,128,128]{3,2,1,0:T(8,128)S(1)} %get-tuple-element.38), channel_id=1, source_target_pairs={{1,0},{2,1},{3,2},{4,3},{5,4},{6,5},{7,6},{8,7},{9,8},{10,9},{11,1... | collective-permute-start | bytes 786440 | tf_op jit(solution)/shard_map/ppermute | solution.py:366
  142.8 11.0 %collective-permute-start.17 = (f32[2,128,256]{2,1,0:T(8,128)S(1)}, f32[2,128,256]{2,1,0:T(8,128)S(1)}, u32[]{:S(2)}, u32[]{:S(2)}) collective-permute-start(f32[2,128,256]{2,1,0:T(8,128)S(1)} %get-tuple-element.47), channel_id=1, source_target_pairs={{0,16},{16,32},{32,48},{48,64},{64,80},{80,96},{96,112},{1,17},{17... | collective-permute-start | bytes 786440 | tf_op jit(solution)/shard_map/ppermute | solution.py:373
  145.3 13.6 %collective-permute-start.18 = (f32[2,128,256]{2,1,0:T(8,128)S(1)}, f32[2,128,256]{2,1,0:T(8,128)S(1)}, u32[]{:S(2)}, u32[]{:S(2)}) collective-permute-start(f32[2,128,256]{2,1,0:T(8,128)S(1)} %get-tuple-element.48), channel_id=1, source_target_pairs={{16,0},{32,16},{48,32},{64,48},{80,64},{96,80},{112,96},{17,1},{33... | collective-permute-start | bytes 786440 | tf_op jit(solution)/shard_map/ppermute | solution.py:372
  150.2 10.1 %collective-permute-start.28 = (f32[16,16,256]{2,1,0:T(8,128)S(1)}, f32[16,16,256]{2,1,0:T(8,128)S(1)}, u32[]{:S(2)}, u32[]{:S(2)}) collective-permute-start(f32[16,16,256]{2,1,0:T(8,128)S(1)} %get-tuple-element.42), channel_id=1, source_target_pairs={{0,32},{32,64},{64,96},{96,0},{1,33},{33,65},{65,97},{97,1},{2,34}... | collective-permute-start | bytes 786440 | tf_op jit(solution)/shard_map/ppermute | solution.py:413
  150.3 11.9 %collective-permute-start.29 = (f32[16,16,256]{2,1,0:T(8,128)S(1)}, f32[16,16,256]{2,1,0:T(8,128)S(1)}, u32[]{:S(2)}, u32[]{:S(2)}) collective-permute-start(f32[16,16,256]{2,1,0:T(8,128)S(1)} %get-tuple-element.44), channel_id=1, source_target_pairs={{0,64},{32,96},{64,0},{96,32},{1,65},{33,97},{65,1},{97,33},{2,66}... | collective-permute-start | bytes 786440 | tf_op jit(solution)/shard_map/ppermute | solution.py:413
  151.1 18.0 %collective-permute-start.30 = (f32[16,16,256]{2,1,0:T(8,128)S(1)}, f32[16,16,256]{2,1,0:T(8,128)S(1)}, u32[]{:S(2)}, u32[]{:S(2)}) collective-permute-start(f32[16,16,256]{2,1,0:T(8,128)S(1)} %get-tuple-element.43), channel_id=1, source_target_pairs={{0,96},{32,0},{64,32},{96,64},{1,97},{33,1},{65,33},{97,65},{2,98}... | collective-permute-start | bytes 786440 | tf_op jit(solution)/shard_map/ppermute | solution.py:413
  153.7 38.1 %collective-permute-start.25 = (f32[2,256,128]{2,1,0:T(8,128)S(1)}, f32[2,256,128]{2,1,0:T(8,128)}, u32[]{:S(2)}, u32[]{:S(2)}) collective-permute-start(f32[2,256,128]{2,1,0:T(8,128)S(1)} %get-tuple-element.39), channel_id=1, source_target_pairs={{0,1},{1,2},{2,3},{3,4},{4,5},{5,6},{6,7},{7,8},{8,9},{9,10},{10,1... | collective-permute-start | bytes 786440 | tf_op jit(solution)/shard_map/ppermute | solution.py:369
  158.9 32.9 %collective-permute-start.26 = (f32[2,256,128]{2,1,0:T(8,128)S(1)}, f32[2,256,128]{2,1,0:T(8,128)}, u32[]{:S(2)}, u32[]{:S(2)}) collective-permute-start(f32[2,256,128]{2,1,0:T(8,128)S(1)} %get-tuple-element.40), channel_id=1, source_target_pairs={{1,0},{2,1},{3,2},{4,3},{5,4},{6,5},{7,6},{8,7},{9,8},{10,9},{11,1... | collective-permute-start | bytes 786440 | tf_op jit(solution)/shard_map/ppermute | solution.py:368
  160.2 31.6 %collective-permute-start.23 = (f32[2,128,256]{2,1,0:T(8,128)S(1)}, f32[2,128,256]{2,1,0:T(8,128)}, u32[]{:S(2)}, u32[]{:S(2)}) collective-permute-start(f32[2,128,256]{2,1,0:T(8,128)S(1)} %get-tuple-element.49), channel_id=1, source_target_pairs={{0,16},{16,32},{32,48},{48,64},{64,80},{80,96},{96,112},{1,17},{17... | collective-permute-start | bytes 786440 | tf_op jit(solution)/shard_map/ppermute | solution.py:373
  162.2 29.7 %collective-permute-start.24 = (f32[2,128,256]{2,1,0:T(8,128)S(1)}, f32[2,128,256]{2,1,0:T(8,128)}, u32[]{:S(2)}, u32[]{:S(2)}) collective-permute-start(f32[2,128,256]{2,1,0:T(8,128)S(1)} %get-tuple-element.50), channel_id=1, source_target_pairs={{16,0},{32,16},{48,32},{64,48},{80,64},{96,80},{112,96},{17,1},{33... | collective-permute-start | bytes 786440 | tf_op jit(solution)/shard_map/ppermute | solution.py:372
  169.9 30.4 %all-to-all-start.2 = ((f32[16,16,256]{2,1,0:T(8,128)}), f32[16,16,256]{2,1,0:T(8,128)S(1)}, u32[]{:S(2)}, u32[]{:S(2)}) async-start(f32[16,16,256]{2,1,0:T(8,128)} %fusion.10), calls=%async_computation.2 | async-start | bytes 524288 | tf_op jit(solution)/shard_map/all_to_all | solution.py:414
  (18 other events, 205.7 us)

commit v2 on v1

v2 whole, which is shorter than its diff:
```python
import functools

import jax
import jax.numpy as jnp
import ml_dtypes
import numpy as np
from jax import lax
from jax.experimental import pallas as pl
from jax.experimental.pallas import tpu as pltpu
from jax.sharding import Mesh
from jax.sharding import PartitionSpec as P

W = 256
H = 128
MODES = 4
SLOTS = 2
amp_floor = 0.5
f32 = jnp.float32
bf16 = jnp.bfloat16
VMEM_BYTES = 24 << 20


def real_form(a):
    return np.block([[a.real, -a.imag], [a.imag, a.real]])


def make_tables():
    k = np.arange(W)
    dft_matrix = np.exp(-2j * np.pi * ((k[:, None] * k[None, :]) % W) / W) / np.sqrt(W)
    freq = (k + H) % W - H
    phase = np.exp(2j * np.pi * ((freq * freq) % (4 * W)) / (4 * W))
    circ = dft_matrix.conj() @ np.diag(phase) @ dft_matrix
    c0, c1 = circ[:H, :H], circ[H:, :H]
    mats = [(c0 + c1) / 2, (c0 - c1) / 2, dft_matrix[0::2, :H], dft_matrix[1::2, :H]]
    high, low = [], []
    for mat in mats:
        full = real_form(mat)
        for form in (full, full.T):
            top = form.astype(np.float32).astype(ml_dtypes.bfloat16)
            high.append(top)
            low.append((form - top.astype(np.float64)).astype(np.float32).astype(ml_dtypes.bfloat16))
    return np.stack(high), np.stack(low)


def split(x):
    top = x.astype(bf16)
    return top, (x - top.astype(f32)).astype(bf16)


dot = functools.partial(jnp.dot, preferred_element_type=f32)


def left_product(tabs, i, x):
    top, rest = split(x)
    hi, lo = tabs
    return dot(hi[i], top) + dot(lo[i], top) + dot(hi[i], rest)


def right_product(tabs, i, x):
    top, rest = split(x)
    hi, lo = tabs
    return dot(top, hi[i]) + dot(top, lo[i]) + dot(rest, hi[i])


def halves(x, axis):
    return (x[:H], x[H:]) if axis == 0 else (x[:, :H], x[:, H:])


def one_side(tabs, axis, ia, ib, xr, xi, fold_in, fold_out):
    (ar, br), (ai, bi) = halves(xr, axis), halves(xi, axis)
    if fold_in:
        ar, br, ai, bi = ar + br, ar - br, ai + bi, ai - bi
    product = left_product if axis == 0 else right_product
    ya = product(tabs, ia, jnp.concatenate([ar, ai], axis))
    yb = product(tabs, ib, jnp.concatenate([br, bi], axis))
    if fold_out:
        ya, yb = ya + yb, ya - yb
    (ar, ai), (br, bi) = halves(ya, axis), halves(yb, axis)
    return jnp.concatenate([ar, br], axis), jnp.concatenate([ai, bi], axis)


def propagate(tabs, xr, xi, adjoint):
    t = 1 if adjoint else 0
    xr, xi = one_side(tabs, 0, 0 + t, 2 + t, xr, xi, True, True)
    return one_side(tabs, 1, 1 - t, 3 - t, xr, xi, True, True)


def dft(tabs, xr, xi):
    xr, xi = one_side(tabs, 0, 4, 6, xr, xi, True, False)
    return one_side(tabs, 1, 5, 7, xr, xi, True, False)


def dft_adjoint(tabs, xr, xi):
    xr, xi = one_side(tabs, 0, 5, 7, xr, xi, False, True)
    return one_side(tabs, 1, 4, 6, xr, xi, False, True)


def params():
    return pltpu.CompilerParams(vmem_limit_bytes=VMEM_BYTES)


def struct(*shape):
    return jax.ShapeDtypeStruct(shape, f32)


def whole(*shape):
    return pl.BlockSpec(shape, lambda *_: (0,) * len(shape))


TABLE_SPECS = [whole(8, W, W), whole(8, W, W)]
SMEM = pl.BlockSpec(memory_space=pltpu.SMEM)
mode_block = pl.BlockSpec((1, 2, W, W), lambda m, s: (m, 0, 0, 0))
slot_block = pl.BlockSpec((1, 2, W, W), lambda m, s: (s, 0, 0, 0))
both_block = pl.BlockSpec((1, 1, 2, W, W), lambda m, s: (m, s, 0, 0, 0))
VMEM = pl.BlockSpec(memory_space=pltpu.VMEM)


def cost(transforms):
    return pl.CostEstimate(flops=transforms * 1_200_000_000, bytes_accessed=1 << 20, transcendentals=0)


def row_slices_kernel(mid, up, down):
    up[...] = mid[:, :, H:, :]
    down[...] = mid[:, :, :H, :]


def row_slices(mid):
    block = pl.BlockSpec((1, 2, H, W), lambda j: (j, 0, 0, 0))
    return pl.pallas_call(
        row_slices_kernel,
        grid=(2,),
        in_specs=[pl.BlockSpec((1, 2, W, W), lambda j: (j, 0, 0, 0))],
        out_specs=[block, block],
        out_shape=[struct(2, 2, H, W)] * 2,
        compiler_params=params(),
    )(mid)


def column_slices_kernel(mid, top, bot, right, left):
    for out, cols in ((right, slice(H, W)), (left, slice(0, H))):
        out[:, :, 0:H] = top[:, :, :, cols]
        out[:, :, H : H + W] = mid[:, :, :, cols]
        out[:, :, H + W :] = bot[:, :, :, cols]


def column_slices(mid, top, bot):
    rim = pl.BlockSpec((1, 2, H, W), lambda j: (j, 0, 0, 0))
    tall = pl.BlockSpec((1, 2, 2 * W, H), lambda j: (j, 0, 0, 0))
    return pl.pallas_call(
        column_slices_kernel,
        grid=(2,),
        in_specs=[pl.BlockSpec((1, 2, W, W), lambda j: (j, 0, 0, 0)), rim, rim],
        out_specs=[tall, tall],
        out_shape=[struct(2, 2, 2 * W, H)] * 2,
        compiler_params=params(),
    )(mid, top, bot)


def corner(pos, s):
    r = pos[s, 0]
    c = pos[s, 1]
    rows = pl.ds(pl.multiple_of(r // 8 * 8, 8), W + 8)
    cols = [pl.ds(pl.multiple_of(c // H * H + k * H, H), H) for k in range(3)]
    return rows, cols, r % 8, c % H


def extract_kernel(pos, mid, top, bot, lft, rgt, win, ext):
    lane = lax.broadcasted_iota(jnp.int32, (W + 8, H), 1)
    sub = lax.broadcasted_iota(jnp.int32, (W // 8, 8, H), 1)
    for j in range(2):
        for p in range(2):
            ext[p, 0:H, H : H + W] = top[j, p]
            ext[p, H : H + W, H : H + W] = mid[j, p]
            ext[p, H + W :, H : H + W] = bot[j, p]
            ext[p, :, 0:H] = lft[j, p]
            ext[p, :, H + W :] = rgt[j, p]
        for s in range(SLOTS):
            rows, cols, dr, dc = corner(pos, s)
            for p in range(2):
                turned = [pltpu.roll(ext[p, rows, col], (H - dc) % H, 1) for col in cols]
                for k in range(2):
                    x = jnp.where(lane < H - dc, turned[k], turned[k + 1])
                    x = pltpu.roll(x.reshape(W // 8 + 1, 8, H), (8 - dr) % 8, 1)
                    x = jnp.where(sub < 8 - dr, x[:-1], x[1:])
                    win[s, j, p, :, k * H : k * H + H] = x.reshape(W, H)


def extract(pos, mid, top, bot, lft, rgt):
    return pl.pallas_call(
        extract_kernel,
        in_specs=[SMEM] + [VMEM] * 5,
        out_specs=VMEM,
        out_shape=struct(SLOTS, 2, 2, W, W),
        scratch_shapes=[pltpu.VMEM((2, 2 * W, 2 * W), f32)],
        compiler_params=params(),
        cost_estimate=cost(3),
    )(pos, mid, top, bot, lft, rgt)


def place_kernel(pos, grad, mid, top, bot, lft, rgt, ext):
    lane = lax.broadcasted_iota(jnp.int32, (W + 8, H), 1)
    sub = lax.broadcasted_iota(jnp.int32, (W // 8 + 1, 8, H), 1)
    group = jnp.zeros((1, 8, H), f32)
    for j in range(2):
        ext[...] = jnp.zeros_like(ext)
        for s in range(SLOTS):
            rows, cols, dr, dc = corner(pos, s)
            for p in range(2):
                turned = []
                for k in range(2):
                    x = grad[s, j, p, :, k * H : k * H + H].reshape(W // 8, 8, H)
                    x = pltpu.roll(x, dr, 1)
                    x = jnp.where(
                        sub >= dr,
                        jnp.concatenate([x, group], 0),
                        jnp.concatenate([group, x], 0),
                    )
                    turned.append(pltpu.roll(x.reshape(W + 8, H), dc, 1))
                ext[p, rows, cols[0]] += jnp.where(lane >= dc, turned[0], 0.0)
                ext[p, rows, cols[1]] += jnp.where(lane >= dc, turned[1], turned[0])
                ext[p, rows, cols[2]] += jnp.where(lane >= dc, 0.0, turned[1])
        for p in range(2):
            top[j, p] = ext[p, 0:H, H : H + W]
            mid[j, p] = ext[p, H : H + W, H : H + W]
            bot[j, p] = ext[p, H + W :, H : H + W]
            lft[j, p] = ext[p, :, 0:H]
            rgt[j, p] = ext[p, :, H + W :]


def place(pos, grad):
    return pl.pallas_call(
        place_kernel,
        in_specs=[SMEM, VMEM],
        out_specs=[VMEM] * 5,
        out_shape=[
            struct(2, 2, W, W),
            struct(2, 2, H, W),
            struct(2, 2, H, W),
            struct(2, 2, 2 * W, H),
            struct(2, 2, 2 * W, H),
        ],
        scratch_shapes=[pltpu.VMEM((2, 2 * W, 2 * W), f32)],
        compiler_params=params(),
        cost_estimate=cost(3),
    )(pos, grad)


def rims_kernel(top, bot, right, left, above, below, rows, sides, sems):
    pairs = [(top, rows.at[0]), (bot, rows.at[1])]
    for k, cells in ((0, pl.ds(0, H)), (1, pl.ds(H + W, H))):
        pairs.append((left.at[:, :, cells, :], sides.at[2 * k]))
        pairs.append((right.at[:, :, cells, :], sides.at[2 * k + 1]))
    copies = [pltpu.make_async_copy(a, b, sems.at[k]) for k, (a, b) in enumerate(pairs)]
    for copy in copies:
        copy.start()
    for copy in copies:
        copy.wait()
    for k, out in ((0, above), (1, below)):
        out[:, :, :, 0:H] = rows[k, :, :, :, 0:H] + sides[2 * k]
        out[:, :, :, H:] = rows[k, :, :, :, H:] + sides[2 * k + 1]


def rims(top, bot, from_right, from_left):
    return pl.pallas_call(
        rims_kernel,
        in_specs=[pl.BlockSpec(memory_space=pl.ANY)] * 4,
        out_specs=[VMEM] * 2,
        out_shape=[struct(2, 2, H, W)] * 2,
        scratch_shapes=[
            pltpu.VMEM((2, 2, 2, H, W), f32),
            pltpu.VMEM((4, 2, 2, H, H), f32),
            pltpu.SemaphoreType.DMA((6,)),
        ],
        compiler_params=params(),
    )(top, bot, from_right, from_left)


def combine_kernel(mid, right, left, above, below, out):
    near, far = slice(H, W), slice(W, W + H)
    out[:, :, 0:H, 0:H] = mid[:, :, 0:H, 0:H] + above[:, :, :, 0:H] + left[:, :, near]
    out[:, :, 0:H, H:] = mid[:, :, 0:H, H:] + above[:, :, :, H:] + right[:, :, near]
    out[:, :, H:, 0:H] = mid[:, :, H:, 0:H] + below[:, :, :, 0:H] + left[:, :, far]
    out[:, :, H:, H:] = mid[:, :, H:, H:] + below[:, :, :, H:] + right[:, :, far]


def combine(mid, from_right, from_left, above, below):
    return pl.pallas_call(
        combine_kernel,
        in_specs=[VMEM] * 5,
        out_specs=VMEM,
        out_shape=struct(2, 2, W, W),
        compiler_params=params(),
    )(mid, from_right, from_left, above, below)


probe_block = pl.BlockSpec((4, 1, 4, 16, W), lambda m, s: (0, m, 0, 0, 0))
grad_block = pl.BlockSpec((1, 4, 4, 16, W), lambda m, s: (m, 0, 0, 0, 0))
PROBE = (4, 4, 4, 16, W)


def block_rows(x, y, c):
    return pl.ds(pl.multiple_of((x % 2) * 128 + y * 32 + c * 16, 16), 16)


def join_probe(core, mine, other, probe):
    c = core[0]
    for x in range(4):
        for y in range(4):
            probe[x // 2, block_rows(x, y, c), :] = mine[y, 0, x]
            probe[x // 2, block_rows(x, y, 1 - c), :] = other[y, 0, x]


def cut_probe(core, probe, mine, other):
    c = core[0]
    for x in range(4):
        for y in range(4):
            mine[0, x, y] = probe[x // 2, block_rows(x, y, c), :]
            other[0, x, y] = probe[x // 2, block_rows(x, y, 1 - c), :]


def forward_kernel(core, hi, lo, mine, other, win, u, far, intensity, probe):
    m, s = pl.program_id(0), pl.program_id(1)

    @pl.when(s == 0)
    def _():
        join_probe(core, mine, other, probe)

    pr, pi = probe[0], probe[1]
    a, b = win[0, 0, 0], win[0, 0, 1]
    ur, ui = propagate((hi, lo), pr * a - pi * b, pr * b + pi * a, False)
    u[0, 0, 0] = ur
    u[0, 0, 1] = ui
    a, b = win[0, 1, 0], win[0, 1, 1]
    fr, fi = dft((hi, lo), ur * a - ui * b, ur * b + ui * a)
    far[0, 0, 0] = fr
    far[0, 0, 1] = fi
    power = fr * fr + fi * fi

    @pl.when(m == 0)
    def _():
        intensity[s] = power

    @pl.when(m != 0)
    def _():
        intensity[s] += power


window_block = pl.BlockSpec((1, 2, 2, W, W), lambda m, s: (s, 0, 0, 0, 0))


def forward(tabs, core, mine, other, win):
    return pl.pallas_call(
        forward_kernel,
        grid=(MODES, SLOTS),
        in_specs=[SMEM] + TABLE_SPECS + [probe_block, probe_block, window_block],
        out_specs=[both_block, both_block, whole(SLOTS, W, W)],
        scratch_shapes=[pltpu.VMEM((2, W, W), f32)],
        out_shape=[
            struct(MODES, SLOTS, 2, W, W),
            struct(MODES, SLOTS, 2, W, W),
            struct(SLOTS, W, W),
        ],
        compiler_params=params(),
        cost_estimate=cost(16),
    )(core, *tabs, mine, other, win)


def pieces_of(x):
    out = []
    for _ in range(3):
        out.append(x.astype(bf16))
        x = x - out[-1].astype(f32)
    return out


def even_odd_order():
    perm = np.zeros((W, W), ml_dtypes.bfloat16)
    perm[np.arange(W), np.concatenate([np.arange(0, W, 2), np.arange(1, W, 2)])] = 1
    return jnp.asarray(np.stack([perm, perm.T]))


def reordered(order, x):
    a, b, c = pieces_of(x)
    x = (dot(order[0], a) + dot(order[0], b)) + dot(order[0], c)
    a, b, c = pieces_of(x)
    return (dot(a, order[1]) + dot(b, order[1])) + dot(c, order[1])


def backward_kernel(
    loss_scale, core, counts, order, hi, lo, meas, intensity, far, u, mine, other, win,
    grad_mine, grad_other, grad_win, scale, probe, grad_probe,
):
    m, s = pl.program_id(0), pl.program_id(1)

    @pl.when(s == 0)
    def _():
        join_probe(core, mine, other, probe)

    @pl.when(m == 0)
    def _():
        weight = jnp.where(s < counts[0, 0], 2.0 * loss_scale, 0.0)
        amplitude = reordered(order, meas[:, 0].reshape(W, W))
        scale[s] = weight * (1.0 - amplitude * lax.rsqrt(intensity[0] + amp_floor))

    factor = scale[s]
    gr, gi = dft_adjoint((hi, lo), factor * far[0, 0, 0], factor * far[0, 0, 1])
    ur, ui = u[0, 0, 0], u[0, 0, 1]
    vr = gr * ur + gi * ui
    vi = gi * ur - gr * ui
    a, b = win[0, 1, 0], win[0, 1, 1]
    gr, gi = propagate((hi, lo), gr * a + gi * b, gi * a - gr * b, True)
    pr, pi = probe[0], probe[1]
    wr = gr * pr + gi * pi
    wi = gi * pr - gr * pi
    a, b = win[0, 0, 0], win[0, 0, 1]
    qr = gr * a + gi * b
    qi = gi * a - gr * b

    @pl.when(s == 0)
    def _():
        grad_probe[0] = qr
        grad_probe[1] = qi

    @pl.when(s != 0)
    def _():
        grad_probe[0] += qr
        grad_probe[1] += qi
        cut_probe(core, grad_probe, grad_mine, grad_other)

    @pl.when(m == 0)
    def _():
        grad_win[s, 0, 0] = wr
        grad_win[s, 0, 1] = wi
        grad_win[s, 1, 0] = vr
        grad_win[s, 1, 1] = vi

    @pl.when(m != 0)
    def _():
        grad_win[s, 0, 0] += wr
        grad_win[s, 0, 1] += wi
        grad_win[s, 1, 0] += vr
        grad_win[s, 1, 1] += vi


def backward(tabs, loss_scale, core, counts, meas, intensity, far, u, mine, other, win):
    return pl.pallas_call(
        functools.partial(backward_kernel, loss_scale),
        grid=(MODES, SLOTS),
        in_specs=[SMEM, SMEM, whole(2, W, W)]
        + TABLE_SPECS
        + [
            pl.BlockSpec((16, 1, 16, W), lambda m, s: (0, jnp.where(m == 0, s, 1), 0, 0)),
            pl.BlockSpec((1, W, W), lambda m, s: (jnp.where(m == 0, s, 1), 0, 0)),
        ]
        + [both_block, both_block, probe_block, probe_block, window_block],
        out_specs=[grad_block, grad_block, whole(SLOTS, 2, 2, W, W)],
        out_shape=[struct(*PROBE), struct(*PROBE), struct(SLOTS, 2, 2, W, W)],
        scratch_shapes=[
            pltpu.VMEM((SLOTS, W, W), f32),
            pltpu.VMEM((2, W, W), f32),
            pltpu.VMEM((2, W, W), f32),
        ],
        compiler_params=params(),
        cost_estimate=cost(16),
    )(core, counts, even_odd_order(), *tabs, meas, intensity, far, u, mine, other, win)


TY = ("z", "xl")
TX = ("xh", "y", "c")
ZX = ("z", "xl", "xh")
SWAP = [(0, 1), (1, 0)]


def up_perm(count):
    return [(i, i + 1) for i in range(count - 1)]


def down_perm(count):
    return [(i + 1, i) for i in range(count - 1)]


def after(x, *earlier):
    return lax.optimization_barrier((x,) + earlier)[0]


def exchange(x, axes):
    return lax.all_to_all(x, axes, split_axis=0, concat_axis=0, tiled=True)


def body(object_slices, probe_rows, measured, positions, counts):
    tabs = tuple(jnp.asarray(t) for t in make_tables())
    pos = positions[0, 0]
    core = lax.axis_index("c").reshape(1)

    mid = object_slices
    up, down = row_slices(mid)
    probe_rows = after(jnp.broadcast_to(probe_rows[None], (16, 16, W)), up, down)
    probe_rows = exchange(probe_rows, ZX)
    top = lax.ppermute(up, TY, up_perm(8))
    bot = lax.ppermute(down, TY, down_perm(8))
    probe_rows = after(probe_rows, top)
    mine = exchange(jnp.broadcast_to(probe_rows.reshape(1, 256, W), (4, 256, W)), "y")
    mine = mine.reshape(*PROBE)
    meas = exchange(after(measured[0], top), TX)
    right, left = column_slices(mid, top, bot)
    lft = lax.ppermute(right, TX, up_perm(16))
    rgt = lax.ppermute(left, TX, down_perm(16))
    other = lax.ppermute(mine, "c", SWAP)
    lft, rgt, meas = lax.optimization_barrier((lft, rgt, meas))
    win = extract(pos, mid, top, bot, lft, rgt)
    u, farfield, intensity = forward(tabs, core, mine, other, win)
    mine, other, grad_win = backward(
        tabs, 1.0 / 16.0, core, counts, meas, intensity, farfield, u, mine, other, win
    )
    mine = mine + lax.ppermute(other, "c", SWAP)
    mid, top, bot, lft, rgt = place(pos, grad_win)
    from_right = lax.ppermute(lft, TX, down_perm(16))
    from_left = lax.ppermute(rgt, TX, up_perm(16))
    mine = exchange(after(mine.reshape(16, 64, W), lft, rgt), ZX)
    above, below = rims(top, bot, from_right, from_left)
    above_sum = lax.ppermute(below, TY, up_perm(8))
    below_sum = lax.ppermute(above, TY, down_perm(8))
    mine = jnp.sum(after(mine, above, below), 0).reshape(4, 16, W)
    mine = exchange(mine, "y")
    probe_grad = jnp.sum(mine, 0)
    return combine(mid, from_right, from_left, above_sum, below_sum), probe_grad


def solution(mesh):
    fine = Mesh(mesh.devices.reshape(4, 2, 2, 4, 2), ("z", "xl", "xh", "y", "c"))
    in_specs = (
        P(None, None, TY, TX),
        P(TY + TX, None),
        P(TY, None, None, TX, None),
        P(TY, TX, None, None),
        P(TY, TX),
    )
    out_specs = (P(None, None, TY, TX), P(TY + TX, None))
    return jax.shard_map(
        body, mesh=fine, in_specs=in_specs, out_specs=out_specs, check_vma=False
    )
```

time: 203 us -> 166 us (0.82)
  the two profiles are of different devices: /device:TPU:32 before, /device:TPU:27 now
where the time goes in v2:
time: 166 us; the launch traced here: 165 us
  starting transfers between devices  62.1 us (37%)
  waiting for transfers between devices  48.3 us (29%)
  Pallas kernels  42.3 us (25%)
  local copies, waits for them, and re-layouts  6.87 us (4%)
  other arithmetic  3.74 us (2%)
    all_to_all x5, starting transfers between devices, exchange(): return lax.all_to_all(x, axes, split_axis=0, concat_axis=0, tiled=True)  29.5 us
    all_to_all x5, waiting for transfers between devices, exchange(): return lax.all_to_all(x, axes, split_axis=0, concat_axis=0, tiled=True)  22.3 us
    pallas_call x1, Pallas kernels, backward(): pl.pallas_call(functools.partial(backward_kernel, loss_scale), grid=(MODE...  16.6 us
    pallas_call x1, Pallas kernels, forward(): pl.pallas_call(forward_kernel, grid=(MODES, SLOTS), in_specs=[SMEM] + TAB...  13.5 us
    ppermute x1, waiting for transfers between devices, body(): below_sum = lax.ppermute(above, TY, down_perm(8))  10.3 us
    ppermute x1, starting transfers between devices, body(): from_left = lax.ppermute(rgt, TX, up_perm(16))  6.77 us
    ppermute x1, waiting for transfers between devices, body(): from_right = lax.ppermute(lft, TX, down_perm(16))  6.66 us
    ppermute x1, starting transfers between devices, body(): above_sum = lax.ppermute(below, TY, up_perm(8))  6.07 us
  transfers between devices with their start and end apart: 15, of which 8 were waited for; matrix products, arithmetic and copies ran while one was open for 3% of the time, Pallas kernels for 7%

profile of v2, /device:TPU:27, one launch (start us, length us, event | category | flops | bytes accessed | tf_op | source)
XLA Modules:
  0.0 164.8 jit_solution(31787422489810858)
XLA Ops:
  2.7 3.5 %collective-permute-start = (f32[2,2,128,256]{3,2,1,0:T(8,128)S(1)}, f32[2,2,128,256]{3,2,1,0:T(8,128)S(1)}, u32[]{:S(2)}, u32[]{:S(2)}) collective-permute-start(f32[2,2,128,256]{3,2,1,0:T(8,128)S(1)} %get-tuple-element.27), channel_id=1, source_target_pairs={{0,16},{16,32},{32,48},{48,64},{64,80},{80,96},{96,112},{1,17},{17... | collective-permute-start | bytes 1572872 | tf_op jit(solution)/shard_map/ppermute | solution.py:499
  6.2 1.4 broadcast_in_dim.6
  7.7 7.3 %all-to-all-start.1 = ((f32[16,16,256]{2,1,0:T(8,128)}), f32[16,16,256]{2,1,0:T(8,128)S(1)}, u32[]{:S(2)}, u32[]{:S(2)}) async-start(f32[16,16,256]{2,1,0:T(8,128)} %broadcast_in_dim.6), calls=%async_computation.1 | async-start | bytes 524288 | tf_op jit(solution)/shard_map/all_to_all | solution.py:487
  15.0 2.0 %collective-permute-start.1 = (f32[2,2,128,256]{3,2,1,0:T(8,128)}, f32[2,2,128,256]{3,2,1,0:T(8,128)S(1)}, u32[]{:S(2)}, u32[]{:S(2)}) collective-permute-start(f32[2,2,128,256]{3,2,1,0:T(8,128)} %get-tuple-element.28), channel_id=1, source_target_pairs={{16,0},{32,16},{48,32},{64,48},{80,64},{96,80},{112,96},{17,1},{33... | collective-permute-start | bytes 1572872 | tf_op jit(solution)/shard_map/ppermute | solution.py:500
  17.0 7.9 %all-to-all-done.1 = f32[16,16,256]{2,1,0:T(8,128)S(1)} async-done(((f32[16,16,256]{2,1,0:T(8,128)}), f32[16,16,256]{2,1,0:T(8,128)S(1)}, u32[]{:S(2)}, u32[]{:S(2)}) %all-to-all-start.1) | async-done | bytes 262176 | tf_op jit(solution)/shard_map/all_to_all | solution.py:487
  25.9 4.1 %all-to-all-start.2 = ((f32[4,256,256]{2,1,0:T(8,128)}), f32[4,256,256]{2,1,0:T(8,128)S(1)}, u32[]{:S(2)}, u32[]{:S(2)}) async-start(f32[4,256,256]{2,1,0:T(8,128)} %broadcast_in_dim.15), calls=%async_computation.2 | async-start | bytes 2097152 | tf_op jit(solution)/shard_map/all_to_all | solution.py:487
  30.1 3.0 %collective-permute-done.1.bot = f32[2,2,128,256]{3,2,1,0:T(8,128)S(1)} collective-permute-done((f32[2,2,128,256]{3,2,1,0:T(8,128)}, f32[2,2,128,256]{3,2,1,0:T(8,128)S(1)}, u32[]{:S(2)}, u32[]{:S(2)}) %collective-permute-start.1) | collective-permute-done | bytes 524320 | tf_op jit(solution)/shard_map/ppermute | solution.py:500
  33.1 1.5 shard_map.96
  34.6 4.9 %collective-permute-start.2 = (f32[2,2,512,128]{3,2,1,0:T(8,128)}, f32[2,2,512,128]{3,2,1,0:T(8,128)}, u32[]{:S(2)}, u32[]{:S(2)}) collective-permute-start(f32[2,2,512,128]{3,2,1,0:T(8,128)} %get-tuple-element.29), channel_id=1, source_target_pairs={{0,1},{1,2},{2,3},{3,4},{4,5},{5,6},{6,7},{7,8},{8,9},{9,10},{10,1... | collective-permute-start | bytes 3145736 | tf_op jit(solution)/shard_map/ppermute | solution.py:506
  39.4 1.9 %collective-permute-start.3 = (f32[2,2,512,128]{3,2,1,0:T(8,128)}, f32[2,2,512,128]{3,2,1,0:T(8,128)}, u32[]{:S(2)}, u32[]{:S(2)}) collective-permute-start(f32[2,2,512,128]{3,2,1,0:T(8,128)} %get-tuple-element.30), channel_id=1, source_target_pairs={{1,0},{2,1},{3,2},{4,3},{5,4},{6,5},{7,6},{8,7},{9,8},{10,9},{11,1... | collective-permute-start | bytes 3145736 | tf_op jit(solution)/shard_map/ppermute | solution.py:507
  41.4 3.0 %collective-permute-start.4 = (f32[4,4,4,16,256]{4,3,2,1,0:T(8,128)S(1)}, f32[4,4,4,16,256]{4,3,2,1,0:T(8,128)}, u32[]{:S(2)}, u32[]{:S(2)}) collective-permute-start(f32[4,4,4,16,256]{4,3,2,1,0:T(8,128)S(1)} %bitcast.7), channel_id=1, source_target_pairs={{0,1},{1,0},{2,3},{3,2},{4,5},{5,4},{6,7},{7,6},{8,9},{9,8},{10,11... | collective-permute-start | bytes 3145736 | tf_op jit(solution)/shard_map/ppermute | solution.py:508
  44.4 7.5 %all-to-all-start = ((f32[16,2,16,256]{3,2,1,0:T(8,128)}), f32[16,2,16,256]{3,2,1,0:T(8,128)S(1)}, u32[]{:S(2)}, u32[]{:S(2)}) async-start(f32[16,2,16,256]{3,2,1,0:T(8,128)} %bitcast.14), calls=%async_computation | async-start | bytes 1048576 | tf_op jit(solution)/shard_map/all_to_all | solution.py:487
  52.5 13.1 %all-to-all-done.meas = f32[16,2,16,256]{3,2,1,0:T(8,128)S(1)} async-done(((f32[16,2,16,256]{3,2,1,0:T(8,128)}), f32[16,2,16,256]{3,2,1,0:T(8,128)S(1)}, u32[]{:S(2)}, u32[]{:S(2)}) %all-to-all-start) | async-done | bytes 524320 | tf_op jit(solution)/shard_map/all_to_all | solution.py:487
  66.6 3.0 %shard_map.97.win = f32[2,2,2,256,256]{4,3,2,1,0:T(8,128)S(1)} custom-call(s32[2,2]{1,0:T(2,128)S(1)} %bitcast.10, f32[2,2,256,256]{3,2,1,0:T(8,128)S(1)} %copy-done.1, f32[2,2,128,256]{3,2,1,0:T(8,128)S(1)} %collective-permute-done.top, f32[2,2,128,256]{3,2,1,0:T(8,128)S(1)} %copy-done.3, f32[2,2,512,128]{3,2,1,0:T(8,128)} %collective-permute-done.2.lft, ...), custom_call_target="tpu_custom_call" | custom-call | flops 3600000000 | bytes 1048576 | tf_op jit(solution)/shard_map/pallas_call | solution.py:189
  69.7 13.5 %shard_map.98 = (f32[4,2,2,256,256]{4,3,2,1,0:T(8,128)S(1)}, f32[4,2,2,256,256]{4,3,2,1,0:T(8,128)S(1)}, f32[2,256,256]{2,1,0:T(8,128)S(1)}) custom-call(s32[1]{0:T(128)} %bitcast.1.core, bf16[8,256,256]{2,1,0:T(8,128)(2,1)S(1)} %copy-done.10, bf16[8,256,256]{2,1,0:T(8,128)(2,1)S(1)} %copy-done.9, f32[4,4,4,16,256]{4,3,2,1,0:T(8,128)S(1)} %bitcast.8, ...), custom_call_target="tpu_custom_call" | custom-call | flops 19200000000 | bytes 1048576 | tf_op jit(solution)/shard_map/pallas_call | solution.py:352
  83.2 16.6 %shard_map.99 = (f32[4,4,4,16,256]{4,3,2,1,0:T(8,128)S(1)}, f32[4,4,4,16,256]{4,3,2,1,0:T(8,128)S(1)}, f32[2,2,2,256,256]{4,3,2,1,0:T(8,128)S(1)}) custom-call(s32[1]{0:T(128)} %bitcast.1.core, s32[1,1]{1,0:T(1,128)S(6)} %copy.10.counts, bf16[2,256,256]{2,1,0:T(8,128)(2,1)S(1)} %copy-done.11, bf16[8,256,256]{2,1,0:T(8,128)(2,1)S(1)} %copy-done.10, ...), custom_call_target="tpu_custom_call" | custom-call | flops 19200000000 | bytes 1048576 | tf_op jit(solution)/shard_map/pallas_call | solution.py:446
  99.9 3.2 %shard_map.100 = (f32[2,2,256,256]{3,2,1,0:T(8,128)S(1)}, f32[2,2,128,256]{3,2,1,0:T(8,128)S(1)}, f32[2,2,128,256]{3,2,1,0:T(8,128)S(1)}, f32[2,2,512,128]{3,2,1,0:T(8,128)}, f32[2,2,512,128]{3,2,1,0:T(8,128)}) custom-call(s32[2,2]{1,0:T(2,128)S(1)} %bitcast.11, f32[2,2,2,256,256]{4,3,2,1,0:T(8,128)S(1)} %get-tuple-element.40.grad), custom_call_target="tpu_custom_call" | custom-call | flops 3600000000 | bytes 1048576 | tf_op jit(solution)/shard_map/pallas_call | solution.py:231
  103.1 2.4 %collective-permute-start.5 = (f32[2,2,512,128]{3,2,1,0:T(8,128)}, f32[2,2,512,128]{3,2,1,0:T(8,128)S(1)}, u32[]{:S(2)}, u32[]{:S(2)}) collective-permute-start(f32[2,2,512,128]{3,2,1,0:T(8,128)} %get-tuple-element.42), channel_id=1, source_target_pairs={{1,0},{2,1},{3,2},{4,3},{5,4},{6,5},{7,6},{8,7},{9,8},{10,9},{11,1... | collective-permute-start | bytes 3145736 | tf_op jit(solution)/shard_map/ppermute | solution.py:517
  105.6 6.8 %collective-permute-start.6 = (f32[2,2,512,128]{3,2,1,0:T(8,128)}, f32[2,2,512,128]{3,2,1,0:T(8,128)S(1)}, u32[]{:S(2)}, u32[]{:S(2)}) collective-permute-start(f32[2,2,512,128]{3,2,1,0:T(8,128)} %get-tuple-element.43), channel_id=1, source_target_pairs={{0,1},{1,2},{2,3},{3,4},{4,5},{5,6},{6,7},{7,8},{8,9},{9,10},{10,1... | collective-permute-start | bytes 3145736 | tf_op jit(solution)/shard_map/ppermute | solution.py:518
  112.3 1.2 add.3
  113.6 6.6 %all-to-all-start.3 = ((f32[16,64,256]{2,1,0:T(8,128)}), f32[16,64,256]{2,1,0:T(8,128)}, u32[]{:S(2)}, u32[]{:S(2)}) async-start(f32[16,64,256]{2,1,0:T(8,128)} %bitcast.12), calls=%async_computation.3 | async-start | bytes 2097152 | tf_op jit(solution)/shard_map/all_to_all | solution.py:487
  120.2 6.7 %collective-permute-done.5.right = f32[2,2,512,128]{3,2,1,0:T(8,128)S(1)} collective-permute-done((f32[2,2,512,128]{3,2,1,0:T(8,128)}, f32[2,2,512,128]{3,2,1,0:T(8,128)S(1)}, u32[]{:S(2)}, u32[]{:S(2)}) %collective-permute-start.5) | collective-permute-done | bytes 1048608 | tf_op jit(solution)/shard_map/ppermute | solution.py:517
  126.9 3.1 %collective-permute-done.6.left = f32[2,2,512,128]{3,2,1,0:T(8,128)S(1)} collective-permute-done((f32[2,2,512,128]{3,2,1,0:T(8,128)}, f32[2,2,512,128]{3,2,1,0:T(8,128)S(1)}, u32[]{:S(2)}, u32[]{:S(2)}) %collective-permute-start.6) | collective-permute-done | bytes 1048608 | tf_op jit(solution)/shard_map/ppermute | solution.py:518
  132.1 1.2 shard_map.101
  133.3 6.1 %collective-permute-start.7 = (f32[2,2,128,256]{3,2,1,0:T(8,128)}, f32[2,2,128,256]{3,2,1,0:T(8,128)}, u32[]{:S(2)}, u32[]{:S(2)}) collective-permute-start(f32[2,2,128,256]{3,2,1,0:T(8,128)} %get-tuple-element.46), channel_id=1, source_target_pairs={{0,16},{16,32},{32,48},{48,64},{64,80},{80,96},{96,112},{1,17},{17... | collective-permute-start | bytes 1572872 | tf_op jit(solution)/shard_map/ppermute | solution.py:521
  139.4 1.9 %collective-permute-start.8 = (f32[2,2,128,256]{3,2,1,0:T(8,128)}, f32[2,2,128,256]{3,2,1,0:T(8,128)}, u32[]{:S(2)}, u32[]{:S(2)}) collective-permute-start(f32[2,2,128,256]{3,2,1,0:T(8,128)} %get-tuple-element.47), channel_id=1, source_target_pairs={{16,0},{32,16},{48,32},{64,48},{80,64},{96,80},{112,96},{17,1},{33... | collective-permute-start | bytes 1572872 | tf_op jit(solution)/shard_map/ppermute | solution.py:522
  141.3 1.4 all-to-all-done.3
  142.7 1.9 %reduce_sum.18 = f32[64,256]{1,0:T(8,128)} reduce(f32[16,64,256]{2,1,0:T(8,128)} %all-to-all-done.3, f32[]{:T(128)} %constant.4.clone.1), dimensions={0}, to_apply=%region_0.0 | reduce | flops 245760 | bytes 1114116 | tf_op jit(solution)/shard_map/reduce_sum | solution.py:523
  144.6 3.9 %all-to-all-start.4 = ((f32[4,16,256]{2,1,0:T(8,128)}), f32[4,16,256]{2,1,0:T(8,128)S(1)}, u32[]{:S(2)}, u32[]{:S(2)}) async-start(f32[4,16,256]{2,1,0:T(8,128)} %bitcast.6), calls=%async_computation.4 | async-start | bytes 131072 | tf_op jit(solution)/shard_map/all_to_all | solution.py:487
  148.6 2.9 %collective-permute-done.7.above = f32[2,2,128,256]{3,2,1,0:T(8,128)} collective-permute-done((f32[2,2,128,256]{3,2,1,0:T(8,128)}, f32[2,2,128,256]{3,2,1,0:T(8,128)}, u32[]{:S(2)}, u32[]{:S(2)}) %collective-permute-start.7) | collective-permute-done | bytes 524320 | tf_op jit(solution)/shard_map/ppermute | solution.py:521
  151.5 10.3 %collective-permute-done.8.below = f32[2,2,128,256]{3,2,1,0:T(8,128)} collective-permute-done((f32[2,2,128,256]{3,2,1,0:T(8,128)}, f32[2,2,128,256]{3,2,1,0:T(8,128)}, u32[]{:S(2)}, u32[]{:S(2)}) %collective-permute-start.8) | collective-permute-done | bytes 524320 | tf_op jit(solution)/shard_map/ppermute | solution.py:522
  161.8 2.4 %shard_map.102 = f32[2,2,256,256]{3,2,1,0:T(8,128)} custom-call(f32[2,2,256,256]{3,2,1,0:T(8,128)S(1)} %get-tuple-element.41.mid, f32[2,2,512,128]{3,2,1,0:T(8,128)S(1)} %collective-permute-done.5.right, f32[2,2,512,128]{3,2,1,0:T(8,128)S(1)} %collective-permute-done.6.left, f32[2,2,128,256]{3,2,1,0:T(8,128)} %collective-permute-done.7.above, ...), custom_call_target="tpu_custom_call" | custom-call | tf_op jit(solution)/shard_map/pallas_call | solution.py:287
  (35 shorter events, 7.0 us)
Async XLA Ops:
  0.6 1.2 copy-start
  1.9 31.2 %copy-start.1 = (f32[2,2,256,256]{3,2,1,0:T(8,128)S(1)}, f32[2,2,256,256]{3,2,1,0:T(8,128)}, u32[]{:S(2)}) copy-start(f32[2,2,256,256]{3,2,1,0:T(8,128)} %mid.5) | copy-start | bytes 3145732
  1.9 63.7 %copy-start.8 = (s32[1,1,2,2]{3,2,1,0:T(2,128)S(1)}, s32[1,1,2,2]{3,2,1,0:T(2,128)}, u32[]{:S(2)}) copy-start(s32[1,1,2,2]{3,2,1,0:T(2,128)} %param.11) | copy-start | bytes 52
  2.7 22.2 %collective-permute-start = (f32[2,2,128,256]{3,2,1,0:T(8,128)S(1)}, f32[2,2,128,256]{3,2,1,0:T(8,128)S(1)}, u32[]{:S(2)}, u32[]{:S(2)}) collective-permute-start(f32[2,2,128,256]{3,2,1,0:T(8,128)S(1)} %get-tuple-element.27), channel_id=1, source_target_pairs={{0,16},{16,32},{32,48},{48,64},{64,80},{80,96},{96,112},{1,17},{17... | collective-permute-start | bytes 1572872 | tf_op jit(solution)/shard_map/ppermute | solution.py:499
  7.7 17.2 %all-to-all-start.1 = ((f32[16,16,256]{2,1,0:T(8,128)}), f32[16,16,256]{2,1,0:T(8,128)S(1)}, u32[]{:S(2)}, u32[]{:S(2)}) async-start(f32[16,16,256]{2,1,0:T(8,128)} %broadcast_in_dim.6), calls=%async_computation.1 | async-start | bytes 524288 | tf_op jit(solution)/shard_map/all_to_all | solution.py:487
  15.0 18.1 %collective-permute-start.1 = (f32[2,2,128,256]{3,2,1,0:T(8,128)}, f32[2,2,128,256]{3,2,1,0:T(8,128)S(1)}, u32[]{:S(2)}, u32[]{:S(2)}) collective-permute-start(f32[2,2,128,256]{3,2,1,0:T(8,128)} %get-tuple-element.28), channel_id=1, source_target_pairs={{16,0},{32,16},{48,32},{64,48},{80,64},{96,80},{112,96},{17,1},{33... | collective-permute-start | bytes 1572872 | tf_op jit(solution)/shard_map/ppermute | solution.py:500
  25.9 15.4 %all-to-all-start.2 = ((f32[4,256,256]{2,1,0:T(8,128)}), f32[4,256,256]{2,1,0:T(8,128)S(1)}, u32[]{:S(2)}, u32[]{:S(2)}) async-start(f32[4,256,256]{2,1,0:T(8,128)} %broadcast_in_dim.15), calls=%async_computation.2 | async-start | bytes 2097152 | tf_op jit(solution)/shard_map/all_to_all | solution.py:487
  33.1 11.3 %copy-start.2 = (f32[2,2,128,256]{3,2,1,0:T(8,128)}, f32[2,2,128,256]{3,2,1,0:T(8,128)S(1)}, u32[]{:S(2)}) copy-start(f32[2,2,128,256]{3,2,1,0:T(8,128)S(1)} %collective-permute-done.1.bot) | copy-start | bytes 1572868
  34.6 31.0 %collective-permute-start.2 = (f32[2,2,512,128]{3,2,1,0:T(8,128)}, f32[2,2,512,128]{3,2,1,0:T(8,128)}, u32[]{:S(2)}, u32[]{:S(2)}) collective-permute-start(f32[2,2,512,128]{3,2,1,0:T(8,128)} %get-tuple-element.29), channel_id=1, source_target_pairs={{0,1},{1,2},{2,3},{3,4},{4,5},{5,6},{6,7},{7,8},{8,9},{9,10},{10,1... | collective-permute-start | bytes 3145736 | tf_op jit(solution)/shard_map/ppermute | solution.py:506
  39.4 26.1 %collective-permute-start.3 = (f32[2,2,512,128]{3,2,1,0:T(8,128)}, f32[2,2,512,128]{3,2,1,0:T(8,128)}, u32[]{:S(2)}, u32[]{:S(2)}) collective-permute-start(f32[2,2,512,128]{3,2,1,0:T(8,128)} %get-tuple-element.30), channel_id=1, source_target_pairs={{1,0},{2,1},{3,2},{4,3},{5,4},{6,5},{7,6},{8,7},{9,8},{10,9},{11,1... | collective-permute-start | bytes 3145736 | tf_op jit(solution)/shard_map/ppermute | solution.py:507
  41.4 28.2 %collective-permute-start.4 = (f32[4,4,4,16,256]{4,3,2,1,0:T(8,128)S(1)}, f32[4,4,4,16,256]{4,3,2,1,0:T(8,128)}, u32[]{:S(2)}, u32[]{:S(2)}) collective-permute-start(f32[4,4,4,16,256]{4,3,2,1,0:T(8,128)S(1)} %bitcast.7), channel_id=1, source_target_pairs={{0,1},{1,0},{2,3},{3,2},{4,5},{5,4},{6,7},{7,6},{8,9},{9,8},{10,11... | collective-permute-start | bytes 3145736 | tf_op jit(solution)/shard_map/ppermute | solution.py:508
  44.4 21.2 %all-to-all-start = ((f32[16,2,16,256]{3,2,1,0:T(8,128)}), f32[16,2,16,256]{3,2,1,0:T(8,128)S(1)}, u32[]{:S(2)}, u32[]{:S(2)}) async-start(f32[16,2,16,256]{3,2,1,0:T(8,128)} %bitcast.14), calls=%async_computation | async-start | bytes 1048576 | tf_op jit(solution)/shard_map/all_to_all | solution.py:487
  65.6 1.0 copy-start.3
  66.6 3.0 %copy-start.9 = (bf16[8,256,256]{2,1,0:T(8,128)(2,1)S(1)}, bf16[8,256,256]{2,1,0:T(8,128)(2,1)}, u32[]{:S(2)}) copy-start(bf16[8,256,256]{2,1,0:T(8,128)(2,1)} %constant.13.clone.lo) | copy-start | bytes 3145732
  66.6 3.0 %copy-start.10 = (bf16[8,256,256]{2,1,0:T(8,128)(2,1)S(1)}, bf16[8,256,256]{2,1,0:T(8,128)(2,1)}, u32[]{:S(2)}) copy-start(bf16[8,256,256]{2,1,0:T(8,128)(2,1)} %constant.12.clone.hi) | copy-start | bytes 3145732
  69.7 13.6 %copy-start.11 = (bf16[2,256,256]{2,1,0:T(8,128)(2,1)S(1)}, bf16[2,256,256]{2,1,0:T(8,128)(2,1)}, u32[]{:S(2)}) copy-start(bf16[2,256,256]{2,1,0:T(8,128)(2,1)} %constant.14.clone.order) | copy-start | bytes 786436
  99.9 12.5 %collective-permute-start.9 = (f32[4,4,4,16,256]{4,3,2,1,0:T(8,128)S(1)}, f32[4,4,4,16,256]{4,3,2,1,0:T(8,128)S(1)}, u32[]{:S(2)}, u32[]{:S(2)}) collective-permute-start(f32[4,4,4,16,256]{4,3,2,1,0:T(8,128)S(1)} %get-tuple-element.49), channel_id=1, source_target_pairs={{0,1},{1,0},{2,3},{3,2},{4,5},{5,4},{6,7},{7,6},{8,9},{9,8},{10,11... | collective-permute-start | bytes 3145736 | tf_op jit(solution)/shard_map/ppermute | solution.py:515
  103.1 10.4 %copy-start.4 = (f32[2,2,128,256]{3,2,1,0:T(8,128)}, f32[2,2,128,256]{3,2,1,0:T(8,128)S(1)}, u32[]{:S(2)}) copy-start(f32[2,2,128,256]{3,2,1,0:T(8,128)S(1)} %get-tuple-element.44.top) | copy-start | bytes 1572868
  103.1 10.4 %copy-start.6 = (f32[2,2,128,256]{3,2,1,0:T(8,128)}, f32[2,2,128,256]{3,2,1,0:T(8,128)S(1)}, u32[]{:S(2)}) copy-start(f32[2,2,128,256]{3,2,1,0:T(8,128)S(1)} %get-tuple-element.45.bot) | copy-start | bytes 1572868
  103.1 23.7 %collective-permute-start.5 = (f32[2,2,512,128]{3,2,1,0:T(8,128)}, f32[2,2,512,128]{3,2,1,0:T(8,128)S(1)}, u32[]{:S(2)}, u32[]{:S(2)}) collective-permute-start(f32[2,2,512,128]{3,2,1,0:T(8,128)} %get-tuple-element.42), channel_id=1, source_target_pairs={{1,0},{2,1},{3,2},{4,3},{5,4},{6,5},{7,6},{8,7},{9,8},{10,9},{11,1... | collective-permute-start | bytes 3145736 | tf_op jit(solution)/shard_map/ppermute | solution.py:517
  105.6 24.4 %collective-permute-start.6 = (f32[2,2,512,128]{3,2,1,0:T(8,128)}, f32[2,2,512,128]{3,2,1,0:T(8,128)S(1)}, u32[]{:S(2)}, u32[]{:S(2)}) collective-permute-start(f32[2,2,512,128]{3,2,1,0:T(8,128)} %get-tuple-element.43), channel_id=1, source_target_pairs={{0,1},{1,2},{2,3},{3,4},{4,5},{5,6},{6,7},{7,8},{8,9},{9,10},{10,1... | collective-permute-start | bytes 3145736 | tf_op jit(solution)/shard_map/ppermute | solution.py:518
  113.6 29.1 %all-to-all-start.3 = ((f32[16,64,256]{2,1,0:T(8,128)}), f32[16,64,256]{2,1,0:T(8,128)}, u32[]{:S(2)}, u32[]{:S(2)}) async-start(f32[16,64,256]{2,1,0:T(8,128)} %bitcast.12), calls=%async_computation.3 | async-start | bytes 2097152 | tf_op jit(solution)/shard_map/all_to_all | solution.py:487
  130.0 1.0 copy-start.5
  131.0 1.0 copy-start.7
  133.3 18.2 %collective-permute-start.7 = (f32[2,2,128,256]{3,2,1,0:T(8,128)}, f32[2,2,128,256]{3,2,1,0:T(8,128)}, u32[]{:S(2)}, u32[]{:S(2)}) collective-permute-start(f32[2,2,128,256]{3,2,1,0:T(8,128)} %get-tuple-element.46), channel_id=1, source_target_pairs={{0,16},{16,32},{32,48},{48,64},{64,80},{80,96},{96,112},{1,17},{17... | collective-permute-start | bytes 1572872 | tf_op jit(solution)/shard_map/ppermute | solution.py:521
  139.4 22.4 %collective-permute-start.8 = (f32[2,2,128,256]{3,2,1,0:T(8,128)}, f32[2,2,128,256]{3,2,1,0:T(8,128)}, u32[]{:S(2)}, u32[]{:S(2)}) collective-permute-start(f32[2,2,128,256]{3,2,1,0:T(8,128)} %get-tuple-element.47), channel_id=1, source_target_pairs={{16,0},{32,16},{48,32},{64,48},{80,64},{96,80},{112,96},{17,1},{33... | collective-permute-start | bytes 1572872 | tf_op jit(solution)/shard_map/ppermute | solution.py:522
  144.6 19.5 %all-to-all-start.4 = ((f32[4,16,256]{2,1,0:T(8,128)}), f32[4,16,256]{2,1,0:T(8,128)S(1)}, u32[]{:S(2)}, u32[]{:S(2)}) async-start(f32[4,16,256]{2,1,0:T(8,128)} %bitcast.6), calls=%async_computation.4 | async-start | bytes 131072 | tf_op jit(solution)/shard_map/all_to_all | solution.py:487

commit v3 on v2

v3 whole, which is shorter than its diff:
```python
import functools

import jax
import jax.numpy as jnp
import ml_dtypes
import numpy as np
from jax import lax
from jax.experimental import pallas as pl
from jax.experimental.pallas import tpu as pltpu
from jax.sharding import Mesh
from jax.sharding import PartitionSpec as P

W = 256
H = 128
MODES = 4
SLOTS = 2
amp_floor = 0.5
f32 = jnp.float32
bf16 = jnp.bfloat16
VMEM_BYTES = 24 << 20
MAIN_BYTES = 60 << 20


def real_form(a):
    return np.block([[a.real, -a.imag], [a.imag, a.real]])


def make_tables():
    k = np.arange(W)
    dft_matrix = np.exp(-2j * np.pi * ((k[:, None] * k[None, :]) % W) / W) / np.sqrt(W)
    freq = (k + H) % W - H
    phase = np.exp(2j * np.pi * ((freq * freq) % (4 * W)) / (4 * W))
    circ = dft_matrix.conj() @ np.diag(phase) @ dft_matrix
    c0, c1 = circ[:H, :H], circ[H:, :H]
    mats = [(c0 + c1) / 2, (c0 - c1) / 2, dft_matrix[0::2, :H], dft_matrix[1::2, :H]]
    high, low = [], []
    for mat in mats:
        full = real_form(mat)
        for form in (full, full.T):
            top = form.astype(np.float32).astype(ml_dtypes.bfloat16)
            high.append(top)
            low.append((form - top.astype(np.float64)).astype(np.float32).astype(ml_dtypes.bfloat16))
    return np.stack(high), np.stack(low)


def split(x):
    top = x.astype(bf16)
    return top, (x - top.astype(f32)).astype(bf16)


dot = functools.partial(jnp.dot, preferred_element_type=f32)


def left_product(tabs, i, x):
    top, rest = split(x)
    hi, lo = tabs
    return dot(hi[i], top) + dot(lo[i], top) + dot(hi[i], rest)


def right_product(tabs, i, x):
    top, rest = split(x)
    hi, lo = tabs
    return dot(top, hi[i]) + dot(top, lo[i]) + dot(rest, hi[i])


def halves(x, axis):
    return (x[:H], x[H:]) if axis == 0 else (x[:, :H], x[:, H:])


def one_side(tabs, axis, ia, ib, xr, xi, fold_in, fold_out):
    (ar, br), (ai, bi) = halves(xr, axis), halves(xi, axis)
    if fold_in:
        ar, br, ai, bi = ar + br, ar - br, ai + bi, ai - bi
    product = left_product if axis == 0 else right_product
    ya = product(tabs, ia, jnp.concatenate([ar, ai], axis))
    yb = product(tabs, ib, jnp.concatenate([br, bi], axis))
    if fold_out:
        ya, yb = ya + yb, ya - yb
    (ar, ai), (br, bi) = halves(ya, axis), halves(yb, axis)
    return jnp.concatenate([ar, br], axis), jnp.concatenate([ai, bi], axis)


def propagate(tabs, xr, xi, adjoint):
    t = 1 if adjoint else 0
    xr, xi = one_side(tabs, 0, 0 + t, 2 + t, xr, xi, True, True)
    return one_side(tabs, 1, 1 - t, 3 - t, xr, xi, True, True)


def dft(tabs, xr, xi):
    xr, xi = one_side(tabs, 0, 4, 6, xr, xi, True, False)
    return one_side(tabs, 1, 5, 7, xr, xi, True, False)


def dft_adjoint(tabs, xr, xi):
    xr, xi = one_side(tabs, 0, 5, 7, xr, xi, False, True)
    return one_side(tabs, 1, 4, 6, xr, xi, False, True)


def params():
    return pltpu.CompilerParams(vmem_limit_bytes=VMEM_BYTES)


def struct(*shape):
    return jax.ShapeDtypeStruct(shape, f32)


SMEM = pl.BlockSpec(memory_space=pltpu.SMEM)
VMEM = pl.BlockSpec(memory_space=pltpu.VMEM)
HBM = pl.BlockSpec(memory_space=pltpu.HBM)


def cost(transforms):
    return pl.CostEstimate(flops=transforms * 1_200_000_000, bytes_accessed=1 << 20, transcendentals=0)


def rim_starts(where):
    c, xl = where[0], where[2]
    at = lambda flag, one, zero: pl.multiple_of(flag * (one - zero) + zero, H)
    row_near, row_far = at(xl, 0, H + W), at(xl, H + W, 0)
    col_near, col_far = at(c, 0, H + W), at(c, H + W, 0)
    return (row_near, row_far), (col_near, col_far)


def half_starts(where):
    c, xl = where[0], where[2]
    at = lambda flag, one, zero: pl.multiple_of(flag * (one - zero) + zero, H)
    return (at(xl, 0, H), at(xl, H, 0)), (at(c, 0, H), at(c, H, 0))


def row_slices_kernel(where, mid, near, far):
    starts, _ = half_starts(where)
    near[...] = mid[:, :, pl.ds(starts[0], H), :]
    far[...] = mid[:, :, pl.ds(starts[1], H), :]


def row_slices(where, mid):
    block = pl.BlockSpec((1, 2, H, W), lambda j: (j, 0, 0, 0))
    return pl.pallas_call(
        row_slices_kernel,
        grid=(2,),
        in_specs=[SMEM, pl.BlockSpec((1, 2, W, W), lambda j: (j, 0, 0, 0))],
        out_specs=[block, block],
        out_shape=[struct(2, 2, H, W)] * 2,
        compiler_params=params(),
    )(where, mid)


def column_slices_kernel(where, mid, row_near, row_far, near, far):
    rows, _ = rim_starts(where)
    _, cols = half_starts(where)
    for out, col in ((near, cols[0]), (far, cols[1])):
        part = pl.ds(col, H)
        out[:, :, H : H + W] = mid[:, :, :, part]
        out[:, :, pl.ds(rows[0], H)] = row_near[:, :, :, part]
        out[:, :, pl.ds(rows[1], H)] = row_far[:, :, :, part]


def column_slices(where, mid, row_near, row_far):
    rim = pl.BlockSpec((1, 2, H, W), lambda j: (j, 0, 0, 0))
    tall = pl.BlockSpec((1, 2, 2 * W, H), lambda j: (j, 0, 0, 0))
    return pl.pallas_call(
        column_slices_kernel,
        grid=(2,),
        in_specs=[SMEM, pl.BlockSpec((1, 2, W, W), lambda j: (j, 0, 0, 0)), rim, rim],
        out_specs=[tall, tall],
        out_shape=[struct(2, 2, 2 * W, H)] * 2,
        compiler_params=params(),
    )(where, mid, row_near, row_far)


def corner(pos, s):
    r = pos[s, 0]
    c = pos[s, 1]
    rows = pl.ds(pl.multiple_of(r // 8 * 8, 8), W + 8)
    cols = [pl.ds(pl.multiple_of(c // H * H + k * H, H), H) for k in range(3)]
    return rows, cols, r % 8, c % H


def start_all(pairs, sems):
    copies = [pltpu.make_async_copy(a, b, sems.at[k]) for k, (a, b) in enumerate(pairs)]
    for copy in copies:
        copy.start()
    return copies


def wait_all(copies):
    for copy in copies:
        copy.wait()


def rims_kernel(where, row_near, row_far, col_near, col_far, out_near, out_far, rows, sides, sems):
    starts, _ = rim_starts(where)
    _, halves_at = half_starts(where)
    pairs = [(row_near, rows.at[0]), (row_far, rows.at[1])]
    for k in range(2):
        cells = pl.ds(starts[k], H)
        pairs.append((col_near.at[:, :, cells, :], sides.at[2 * k]))
        pairs.append((col_far.at[:, :, cells, :], sides.at[2 * k + 1]))
    wait_all(start_all(pairs, sems))
    for k, out in ((0, out_near), (1, out_far)):
        for i in range(2):
            part = pl.ds(halves_at[i], H)
            out[:, :, :, part] = rows[k, :, :, :, part] + sides[2 * k + i]


def rims(where, row_near, row_far, col_near, col_far):
    return pl.pallas_call(
        rims_kernel,
        in_specs=[SMEM] + [HBM] * 4,
        out_specs=[VMEM] * 2,
        out_shape=[struct(2, 2, H, W)] * 2,
        scratch_shapes=[
            pltpu.VMEM((2, 2, 2, H, W), f32),
            pltpu.VMEM((4, 2, 2, H, H), f32),
            pltpu.SemaphoreType.DMA((6,)),
        ],
        compiler_params=params(),
    )(where, row_near, row_far, col_near, col_far)


def combine_near_kernel(where, mid, col_near, col_far, row_near, out, total, cols, rows, sems, out_sems):
    rows_at, cols_at = half_starts(where)
    inner = pl.ds(H, W)
    copies = []
    for j in range(2):
        pairs = [
            (mid.at[j], total.at[j]),
            (col_near.at[j, :, inner, :], cols.at[j, 0]),
            (col_far.at[j, :, inner, :], cols.at[j, 1]),
            (row_near.at[j], rows.at[j]),
        ]
        copies.append(start_all(pairs, sems.at[j]))
    done = []
    for j in range(2):
        wait_all(copies[j])
        for i in range(2):
            total[j, :, :, pl.ds(cols_at[i], H)] += cols[j, i]
        total[j, :, pl.ds(rows_at[0], H), :] += rows[j]
        done += start_all([(total.at[j], out.at[j])], out_sems.at[pl.ds(j, 1)])
    wait_all(done)


def combine_near(where, mid, col_near, col_far, row_near):
    return pl.pallas_call(
        combine_near_kernel,
        in_specs=[SMEM] + [HBM] * 4,
        out_specs=HBM,
        out_shape=struct(2, 2, W, W),
        scratch_shapes=[
            pltpu.VMEM((2, 2, W, W), f32),
            pltpu.VMEM((2, 2, 2, W, H), f32),
            pltpu.VMEM((2, 2, H, W), f32),
            pltpu.SemaphoreType.DMA((2, 4)),
            pltpu.SemaphoreType.DMA((2,)),
        ],
        compiler_params=params(),
    )(where, mid, col_near, col_far, row_near)


def even_odd_order():
    perm = np.zeros((W, W), ml_dtypes.bfloat16)
    perm[np.arange(W), np.concatenate([np.arange(0, W, 2), np.arange(1, W, 2)])] = 1
    return jnp.asarray(np.stack([perm, perm.T]))


def pieces_of(x):
    out = []
    for _ in range(3):
        out.append(x.astype(bf16))
        x = x - out[-1].astype(f32)
    return out


def reordered(order, x):
    a, b, c = pieces_of(x)
    x = (dot(order[0], a) + dot(order[0], b)) + dot(order[0], c)
    a, b, c = pieces_of(x)
    return (dot(a, order[1]) + dot(b, order[1])) + dot(c, order[1])


PROBE = (4, 4, 4, 16, W)


def block_rows(x, y, c):
    return pl.ds(pl.multiple_of((x % 2) * 128 + y * 32 + c * 16, 16), 16)


def ext_pieces(where, ext, mid, row_near, row_far, col_near, col_far):
    rows, cols = rim_starts(where)
    inner = pl.ds(H, W)
    full = pl.ds(0, 2 * W)
    return [
        (mid, ext.at[:, :, inner, inner]),
        (row_near, ext.at[:, :, pl.ds(rows[0], H), inner]),
        (row_far, ext.at[:, :, pl.ds(rows[1], H), inner]),
        (col_near, ext.at[:, :, full, pl.ds(cols[0], H)]),
        (col_far, ext.at[:, :, full, pl.ds(cols[1], H)]),
    ]


def extract(pos, ext, win):
    lane = lax.broadcasted_iota(jnp.int32, (W + 8, H), 1)
    sub = lax.broadcasted_iota(jnp.int32, (W // 8, 8, H), 1)
    for s in range(SLOTS):
        rows, cols, dr, dc = corner(pos, s)
        for j in range(2):
            for p in range(2):
                turned = [pltpu.roll(ext[j, p, rows, col], (H - dc) % H, 1) for col in cols]
                for k in range(2):
                    x = jnp.where(lane < H - dc, turned[k], turned[k + 1])
                    x = pltpu.roll(x.reshape(W // 8 + 1, 8, H), (8 - dr) % 8, 1)
                    x = jnp.where(sub < 8 - dr, x[:-1], x[1:])
                    win[s, j, p, :, k * H : k * H + H] = x.reshape(W, H)


def place(pos, grad, ext):
    lane = lax.broadcasted_iota(jnp.int32, (W + 8, H), 1)
    sub = lax.broadcasted_iota(jnp.int32, (W // 8 + 1, 8, H), 1)
    group = jnp.zeros((1, 8, H), f32)
    ext[...] = jnp.zeros_like(ext)
    for s in range(SLOTS):
        rows, cols, dr, dc = corner(pos, s)
        for j in range(2):
            for p in range(2):
                turned = []
                for k in range(2):
                    x = grad[s, j, p, :, k * H : k * H + H].reshape(W // 8, 8, H)
                    x = pltpu.roll(x, dr, 1)
                    x = jnp.where(
                        sub >= dr,
                        jnp.concatenate([x, group], 0),
                        jnp.concatenate([group, x], 0),
                    )
                    turned.append(pltpu.roll(x.reshape(W + 8, H), dc, 1))
                ext[j, p, rows, cols[0]] += jnp.where(lane >= dc, turned[0], 0.0)
                ext[j, p, rows, cols[1]] += jnp.where(lane >= dc, turned[1], turned[0])
                ext[j, p, rows, cols[2]] += jnp.where(lane >= dc, 0.0, turned[1])


def forward_step(tabs, probe, win, u, far, intensity, k):
    m, s = k // 2, k % 2
    pr, pi = probe[m, 0], probe[m, 1]
    a, b = win[s, 0, 0], win[s, 0, 1]
    ur, ui = propagate(tabs, pr * a - pi * b, pr * b + pi * a, False)
    u[k, 0] = ur
    u[k, 1] = ui
    a, b = win[s, 1, 0], win[s, 1, 1]
    fr, fi = dft(tabs, ur * a - ui * b, ur * b + ui * a)
    far[k, 0] = fr
    far[k, 1] = fi
    power = fr * fr + fi * fi
    intensity[s] = jnp.where(m == 0, power, intensity[s] + power)


def backward_step(tabs, probe, win, u, far, scale, grad_probe, grad_win, k):
    m, s = k // 2, k % 2
    factor = scale[s]
    gr, gi = dft_adjoint(tabs, factor * far[k, 0], factor * far[k, 1])
    ur, ui = u[k, 0], u[k, 1]
    vr = gr * ur + gi * ui
    vi = gi * ur - gr * ui
    grad_win[s, 1, 0] = jnp.where(m == 0, vr, grad_win[s, 1, 0] + vr)
    grad_win[s, 1, 1] = jnp.where(m == 0, vi, grad_win[s, 1, 1] + vi)
    a, b = win[s, 1, 0], win[s, 1, 1]
    gr, gi = propagate(tabs, gr * a + gi * b, gi * a - gr * b, True)
    pr, pi = probe[m, 0], probe[m, 1]
    wr = gr * pr + gi * pi
    wi = gi * pr - gr * pi
    grad_win[s, 0, 0] = jnp.where(m == 0, wr, grad_win[s, 0, 0] + wr)
    grad_win[s, 0, 1] = jnp.where(m == 0, wi, grad_win[s, 0, 1] + wi)
    a, b = win[s, 0, 0], win[s, 0, 1]
    qr = gr * a + gi * b
    qi = gi * a - gr * b
    grad_probe[m, 0] = jnp.where(s == 0, qr, grad_probe[m, 0] + qr)
    grad_probe[m, 1] = jnp.where(s == 0, qi, grad_probe[m, 1] + qi)


def main_kernel(
    loss_scale, where, pos, counts, order, high, low, mine, other, meas, meas_core, meas_far, meas_far_core,
    mid, row_near, row_far, col_near, col_far,
    out_mine, out_other, out_mid, out_row_near, out_row_far, out_col_near, out_col_far,
    ext, win, probe, u, far, scale, grad_probe, grad_win, blocks, hi, lo, rows, pattern, perm, sems, more_sems,
):
    copies = start_all(ext_pieces(where, ext, mid, row_near, row_far, col_near, col_far), sems)
    c, h, xl = where[0], where[1], where[2]
    pairs = [(high, hi), (low, lo), (mine, blocks.at[0]), (other, blocks.at[1]), (order, perm)]
    pairs += [(meas.at[:, h, c], rows.at[0, 0]), (meas_core, rows.at[0, 1])]
    pairs += [(meas_far.at[:, c], rows.at[1, 0]), (meas_far_core, rows.at[1, 1])]
    more = start_all(pairs, more_sems)
    wait_all(copies)
    extract(pos, ext, win)
    wait_all(more)
    for m in range(MODES):
        for k in range(4):
            x = (2 * xl + h + k) % 4
            for y in range(4):
                probe[m, x // 2, block_rows(x, y, c), :] = blocks[0, m, k, y]
                probe[m, x // 2, block_rows(x, y, 1 - c), :] = blocks[1, m, k, y]
    tabs = (hi, lo)

    def forward(k, _):
        forward_step(tabs, probe, win, u, far, scale, k)
        return 0

    lax.fori_loop(0, MODES * SLOTS, forward, 0)
    for s in range(SLOTS):
        weight = jnp.where(s < counts[0, 0], 2.0 * loss_scale, 0.0)
        for i, half in ((0, h), (1, 1 - h)):
            for k, core in ((0, c), (1, 1 - c)):
                for y in range(4):
                    start = pl.multiple_of(half * H + y * 32 + core * 16, 16)
                    pattern[pl.ds(start, 16), :] = rows[i, k, y, s]
        amplitude = reordered(perm, pattern[...])
        scale[s] = weight * (1.0 - amplitude * lax.rsqrt(scale[s] + amp_floor))

    def backward(k, _):
        backward_step(tabs, probe, win, u, far, scale, grad_probe, grad_win, k)
        return 0

    lax.fori_loop(0, MODES * SLOTS, backward, 0)
    place(pos, grad_win, ext)
    pairs = ext_pieces(where, ext, out_mid, out_row_near, out_row_far, out_col_near, out_col_far)
    copies = start_all([(b, a) for a, b in pairs], sems)
    for m in range(MODES):
        for x in range(4):
            for y in range(4):
                out_mine[m, x, y] = grad_probe[m, x // 2, block_rows(x, y, c), :]
                out_other[m, x, y] = grad_probe[m, x // 2, block_rows(x, y, 1 - c), :]
    wait_all(copies)


def gradients(tabs, loss_scale, where, pos, counts, *arrays):
    steps = MODES * SLOTS
    return pl.pallas_call(
        functools.partial(main_kernel, loss_scale),
        in_specs=[SMEM] * 3 + [HBM] * 14,
        out_specs=[VMEM] * 2 + [HBM] * 5,
        out_shape=[
            struct(*PROBE),
            struct(*PROBE),
            struct(2, 2, W, W),
            struct(2, 2, H, W),
            struct(2, 2, H, W),
            struct(2, 2, 2 * W, H),
            struct(2, 2, 2 * W, H),
        ],
        scratch_shapes=[
            pltpu.VMEM((2, 2, 2 * W, 2 * W), f32),
            pltpu.VMEM((SLOTS, 2, 2, W, W), f32),
            pltpu.VMEM((MODES, 2, W, W), f32),
            pltpu.VMEM((steps, 2, W, W), f32),
            pltpu.VMEM((steps, 2, W, W), f32),
            pltpu.VMEM((SLOTS, W, W), f32),
            pltpu.VMEM((MODES, 2, W, W), f32),
            pltpu.VMEM((SLOTS, 2, 2, W, W), f32),
            pltpu.VMEM((2,) + PROBE, f32),
            pltpu.VMEM((8, W, W), bf16),
            pltpu.VMEM((8, W, W), bf16),
            pltpu.VMEM((2, 2, 4, SLOTS, 16, W), f32),
            pltpu.VMEM((W, W), f32),
            pltpu.VMEM((2, W, W), bf16),
            pltpu.SemaphoreType.DMA((5,)),
            pltpu.SemaphoreType.DMA((9,)),
        ],
        compiler_params=pltpu.CompilerParams(vmem_limit_bytes=MAIN_BYTES),
        cost_estimate=cost(32),
    )(where, pos, counts, even_odd_order(), *tabs, *arrays)


TY = ("z", "xl")
TX = ("xh", "y", "c")
PLANE = ("xl", "xh", "y")
SWAP = [(0, 1), (1, 0)]


def far_pairs(count):
    return [(i, i + 1) for i in range(1, count - 1, 2)] + [(i + 1, i) for i in range(1, count - 1, 2)]


def after(x, *earlier):
    return lax.optimization_barrier((x,) + earlier)[0]


def exchange(x, axes):
    return lax.all_to_all(x, axes, split_axis=0, concat_axis=0, tiled=True)


def pick(x, index, axis):
    return lax.dynamic_index_in_dim(x, index, axis, keepdims=False)


def swap_rows(near, far):
    return lax.ppermute(near, "xl", SWAP), lax.ppermute(far, TY, far_pairs(8))


def swap_columns(near, far):
    return lax.ppermute(near, "c", SWAP), lax.ppermute(far, TX, far_pairs(16))


def body(object_slices, probe_rows, measured, positions, counts):
    tabs = tuple(jnp.asarray(t) for t in make_tables())
    pos = positions[0, 0]
    where = jnp.stack([lax.axis_index(name) for name in ("c", "xh", "xl")])

    mid = object_slices
    near, far = row_slices(where, mid)
    row_near, row_far = swap_rows(near, far)
    tiles = measured.reshape(2, 4, 2, SLOTS, 16, W).transpose(1, 0, 2, 3, 4, 5).reshape(4, 128, W)
    spread = jnp.broadcast_to(probe_rows[None], (4, 16, W))
    both = exchange(after(jnp.concatenate([spread, tiles], 1), near, far), "y")
    probe_rows = both[:, :16].reshape(64, W)
    meas = both[:, 16:].reshape(4, 2, 2, SLOTS, 16, W)
    c, h = where[0], where[1]
    meas_far = lax.ppermute(pick(meas, 1 - h, 1), "xh", SWAP)
    meas_core = lax.ppermute(pick(pick(meas, h, 1), 1 - c, 1), "c", SWAP)
    meas_far_core = lax.ppermute(pick(meas_far, 1 - c, 1), "c", SWAP)
    probe_rows = [probe_rows] + [
        lax.ppermute(probe_rows, ("xl", "xh"), [((i + k) % 4, i) for i in range(4)]) for k in range(1, 4)
    ]
    probe_rows = after(jnp.stack(probe_rows), row_near, row_far)
    mine = exchange(jnp.broadcast_to(probe_rows.reshape(1, 256, W), (4, 256, W)), "z")
    mine = mine.reshape(*PROBE)
    near, far = column_slices(where, mid, row_near, row_far)
    col_near, col_far = swap_columns(near, far)
    other = lax.ppermute(after(mine, meas_far), "c", SWAP)
    mine, other, mid, row_near, row_far, col_near, col_far = gradients(
        tabs, 1.0 / 16.0, where, pos, counts, mine, other, meas, meas_core, meas_far, meas_far_core,
        mid, row_near, row_far, col_near, col_far,
    )
    mine = mine + lax.ppermute(other, "c", SWAP)
    col_near, col_far = swap_columns(col_near, col_far)
    mine = exchange(mine.reshape(4, 256, W), "z")
    near, far = rims(where, row_near, row_far, col_near, col_far)
    row_near, row_far = swap_rows(near, far)
    mine = jnp.sum(after(mine, near, far), 0).reshape(16, 16, W)
    probe_grad = jnp.sum(exchange(mine, PLANE), 0)
    mid = after(mid, mine)
    held = combine_near(where, mid, col_near, col_far, row_near)
    corner_at = (0, 0, where[2] * H, 0)
    far = lax.dynamic_slice(held, corner_at, (2, 2, H, W)) + row_far
    return lax.dynamic_update_slice(held, far, corner_at), probe_grad


def solution(mesh):
    fine = Mesh(mesh.devices.reshape(4, 2, 2, 4, 2), ("z", "xl", "xh", "y", "c"))
    in_specs = (
        P(None, None, TY, TX),
        P(TY + TX, None),
        P(TY, None, None, TX, None),
        P(TY, TX, None, None),
        P(TY, TX),
    )
    out_specs = (P(None, None, TY, TX), P(TY + TX, None))
    return jax.shard_map(
        body, mesh=fine, in_specs=in_specs, out_specs=out_specs, check_vma=False
    )
```

time: 166 us -> 157 us (0.946)
  the two profiles are of different devices: /device:TPU:27 before, /device:TPU:32 now
where the time goes in v3:
time: 157 us; the launch traced here: 154 us
  waiting for transfers between devices  51.5 us (33%)
  Pallas kernels  42.7 us (27%)
  starting transfers between devices  42.5 us (27%)
  other arithmetic  8.08 us (5%)
  local copies, waits for them, and re-layouts  8 us (5%)
    pallas_call x1, Pallas kernels, gradients(): pl.pallas_call(functools.partial(main_kernel, loss_scale), in_specs=[SMEM...  35.9 us
    all_to_all x4, waiting for transfers between devices, exchange(): return lax.all_to_all(x, axes, split_axis=0, concat_axis=0, tiled=True)  29.2 us
    all_to_all x4, starting transfers between devices, exchange(): return lax.all_to_all(x, axes, split_axis=0, concat_axis=0, tiled=True)  24.9 us
    ppermute x3, waiting for transfers between devices, body(): lax.ppermute(probe_rows, ('xl', 'xh'), [((i + k) % 4, i) for i in range(4)])  14.4 us
    ppermute x4, starting transfers between devices, swap_rows(): return (lax.ppermute(near, 'xl', SWAP), lax.ppermute(far, TY, far_pairs(8)))  6.91 us
    ppermute x1, waiting for transfers between devices, body(): meas_far = lax.ppermute(pick(meas, 1 - h, 1), 'xh', SWAP)  5.43 us
    ppermute x1, starting transfers between devices, body(): mine = mine + lax.ppermute(other, 'c', SWAP)  4.23 us
    ppermute x3, starting transfers between devices, body(): lax.ppermute(probe_rows, ('xl', 'xh'), [((i + k) % 4, i) for i in range(4)])  4.12 us
  transfers between devices with their start and end apart: 20, of which 11 were waited for; matrix products, arithmetic and copies ran while one was open for 6% of the time, Pallas kernels for 4%

profile of v3, /device:TPU:32, one launch (start us, length us, event | category | flops | bytes accessed | tf_op | source)
XLA Modules:
  0.0 154.3 jit_solution(13917647677122163831)
XLA Ops:
  0.7 1.2 copy.11
  1.9 0.9 pad_maximum_fusion
  3.5 4.5 %all-to-all-start = ((f32[4,144,256]{2,1,0:T(8,128)}), f32[4,144,256]{2,1,0:T(8,128)}, u32[]{:S(2)}, u32[]{:S(2)}) async-start(f32[4,144,256]{2,1,0:T(8,128)} %pad_maximum_fusion), calls=%async_computation | async-start | bytes 1179648 | tf_op jit(solution)/shard_map/all_to_all | solution.py:485
  7.9 1.5 collective-permute-start.3
  9.4 2.0 %collective-permute-start.4 = (f32[2,2,128,256]{3,2,1,0:T(8,128)S(1)}, f32[2,2,128,256]{3,2,1,0:T(8,128)S(1)}, u32[]{:S(2)}, u32[]{:S(2)}) collective-permute-start(f32[2,2,128,256]{3,2,1,0:T(8,128)S(1)} %get-tuple-element.21), channel_id=1, source_target_pairs={{16,32},{48,64},{80,96},{32,16},{64,48},{96,80},{17,33},{49,65},{8... | collective-permute-start | bytes 1572872 | tf_op jit(solution)/shard_map/ppermute | solution.py:493
  11.4 6.8 %all-to-all-done = f32[4,144,256]{2,1,0:T(8,128)} async-done(((f32[4,144,256]{2,1,0:T(8,128)}), f32[4,144,256]{2,1,0:T(8,128)}, u32[]{:S(2)}, u32[]{:S(2)}) %all-to-all-start) | async-done | bytes 589856 | tf_op jit(solution)/shard_map/all_to_all | solution.py:485
  18.2 0.8 slice.8
  19.1 3.0 %collective-permute-start.2 = (f32[64,256]{1,0:T(8,128)S(1)}, f32[64,256]{1,0:T(8,128)S(1)}, u32[]{:S(2)}, u32[]{:S(2)}) collective-permute-start(f32[64,256]{1,0:T(8,128)S(1)} %bitcast.31), channel_id=1, source_target_pairs={{24,0},{0,8},{8,16},{16,24},{25,1},{1,9},{9,17},{17,25},{26,2},{2,... | collective-permute-start | bytes 196616 | tf_op jit(solution)/shard_map/ppermute | solution.py:518
  23.2 10.5 %collective-permute-done.2 = f32[64,256]{1,0:T(8,128)S(1)} collective-permute-done((f32[64,256]{1,0:T(8,128)S(1)}, f32[64,256]{1,0:T(8,128)S(1)}, u32[]{:S(2)}, u32[]{:S(2)}) %collective-permute-start.2) | collective-permute-done | bytes 65568 | tf_op jit(solution)/shard_map/ppermute | solution.py:518
  33.7 1.7 %collective-permute-done.1 = f32[64,256]{1,0:T(8,128)S(1)} collective-permute-done((f32[64,256]{1,0:T(8,128)S(1)}, f32[64,256]{1,0:T(8,128)S(1)}, u32[]{:S(2)}, u32[]{:S(2)}) %collective-permute-start.1) | collective-permute-done | bytes 65568 | tf_op jit(solution)/shard_map/ppermute | solution.py:518
  35.4 2.2 %collective-permute-done = f32[64,256]{1,0:T(8,128)S(1)} collective-permute-done((f32[64,256]{1,0:T(8,128)S(1)}, f32[64,256]{1,0:T(8,128)S(1)}, u32[]{:S(2)}, u32[]{:S(2)}) %collective-permute-start) | collective-permute-done | bytes 65568 | tf_op jit(solution)/shard_map/ppermute | solution.py:518
  37.7 1.2 broadcast_in_dim.15
  38.8 5.4 %all-to-all-start.1 = ((f32[4,256,256]{2,1,0:T(8,128)}), f32[4,256,256]{2,1,0:T(8,128)}, u32[]{:S(2)}, u32[]{:S(2)}) async-start(f32[4,256,256]{2,1,0:T(8,128)} %broadcast_in_dim.15), calls=%async_computation.1 | async-start | bytes 2097152 | tf_op jit(solution)/shard_map/all_to_all | solution.py:485
  44.2 1.1 slice.9
  46.2 1.6 %shard_map.96 = (f32[2,2,512,128]{3,2,1,0:T(8,128)}, f32[2,2,512,128]{3,2,1,0:T(8,128)S(1)}) custom-call(s32[3]{0:T(128)S(1)} %pad_add_fusion.where, f32[2,2,256,256]{3,2,1,0:T(8,128)S(1)} %copy-done, f32[2,2,128,256]{3,2,1,0:T(8,128)S(1)} %collective-permute-done.3.row_near, f32[2,2,128,256]{3,2,1,0:T(8,128)S(1)} %collective-permute-done.4.row_far), custom_call_target="tpu_custom_call" | custom-call | tf_op jit(solution)/shard_map/pallas_call | solution.py:161
  48.6 5.4 %collective-permute-done.5.meas_far = f32[4,2,2,16,256]{4,3,2,1,0:T(8,128)S(1)} collective-permute-done((f32[4,2,2,16,256]{4,3,2,1,0:T(8,128)S(1)}, f32[4,2,2,16,256]{4,3,2,1,0:T(8,128)S(1)}, u32[]{:S(2)}, u32[]{:S(2)}) %collective-permute-start.5) | collective-permute-done | bytes 262176 | tf_op jit(solution)/shard_map/ppermute | solution.py:514
  54.0 2.9 %all-to-all-done.1 = f32[4,256,256]{2,1,0:T(8,128)} async-done(((f32[4,256,256]{2,1,0:T(8,128)}), f32[4,256,256]{2,1,0:T(8,128)}, u32[]{:S(2)}, u32[]{:S(2)}) %all-to-all-start.1) | async-done | bytes 1048608 | tf_op jit(solution)/shard_map/all_to_all | solution.py:485
  56.8 0.9 dynamic-slice_bitcast_fusion.2
  61.3 35.9 %shard_map.97 = (f32[4,4,4,16,256]{4,3,2,1,0:T(8,128)}, f32[4,4,4,16,256]{4,3,2,1,0:T(8,128)}, f32[2,2,256,256]{3,2,1,0:T(8,128)}, f32[2,2,128,256]{3,2,1,0:T(8,...) custom-call(s32[3]{0:T(128)} %copy-done.6, s32[2,2]{1,0:T(2,128)} %bitcast.38, ...), custom_call_target="tpu_custom_call" | custom-call | flops 38400000000 | bytes 1048576 | tf_op jit(solution)/shard_map/pallas_call | solution.py:434
  97.2 4.2 %collective-permute-start.11 = (f32[4,4,4,16,256]{4,3,2,1,0:T(8,128)}, f32[4,4,4,16,256]{4,3,2,1,0:T(8,128)S(1)}, u32[]{:S(2)}, u32[]{:S(2)}) collective-permute-start(f32[4,4,4,16,256]{4,3,2,1,0:T(8,128)} %get-tuple-element.29), channel_id=1, source_target_pairs={{0,1},{1,0},{2,3},{3,2},{4,5},{5,4},{6,7},{7,6},{8,9},{9,8},{10,11... | collective-permute-start | bytes 3145736 | tf_op jit(solution)/shard_map/ppermute | solution.py:530
  102.2 1.7 %collective-permute-done.11 = f32[4,4,4,16,256]{4,3,2,1,0:T(8,128)S(1)} collective-permute-done((f32[4,4,4,16,256]{4,3,2,1,0:T(8,128)}, f32[4,4,4,16,256]{4,3,2,1,0:T(8,128)S(1)}, u32[]{:S(2)}, u32[]{:S(2)}) %collective-permute-start.11) | collective-permute-done | bytes 1048608 | tf_op jit(solution)/shard_map/ppermute | solution.py:530
  103.9 2.4 %add.33 = f32[4,4,4,16,256]{4,3,2,1,0:T(8,128)} add(f32[4,4,4,16,256]{4,3,2,1,0:T(8,128)} %get-tuple-element.28, f32[4,4,4,16,256]{4,3,2,1,0:T(8,128)S(1)} %collective-permute-done.11) | non-fusion elementwise | flops 262144 | bytes 3145728 | tf_op jit(solution)/shard_map/add | solution.py:530
  106.3 4.9 %all-to-all-start.2 = ((f32[4,256,256]{2,1,0:T(8,128)}), f32[4,256,256]{2,1,0:T(8,128)}, u32[]{:S(2)}, u32[]{:S(2)}) async-start(f32[4,256,256]{2,1,0:T(8,128)} %bitcast.24), calls=%async_computation.2 | async-start | bytes 2097152 | tf_op jit(solution)/shard_map/all_to_all | solution.py:485
  111.9 1.8 %shard_map.98 = (f32[2,2,128,256]{3,2,1,0:T(8,128)}, f32[2,2,128,256]{3,2,1,0:T(8,128)}) custom-call(s32[3]{0:T(128)S(1)} %copy-done.7, f32[2,2,128,256]{3,2,1,0:T(8,128)S(1)} %copy-done.4, f32[2,2,128,256]{3,2,1,0:T(8,128)S(1)} %copy-done.5, f32[2,2,512,128]{3,2,1,0:T(8,128)S(1)} %collective-permute-done.12.col_near, ...), custom_call_target="tpu_custom_call" | custom-call | tf_op jit(solution)/shard_map/pallas_call | solution.py:207
  113.8 0.8 collective-permute-start.14
  114.6 2.7 %collective-permute-start.15 = (f32[2,2,128,256]{3,2,1,0:T(8,128)}, f32[2,2,128,256]{3,2,1,0:T(8,128)}, u32[]{:S(2)}, u32[]{:S(2)}) collective-permute-start(f32[2,2,128,256]{3,2,1,0:T(8,128)} %get-tuple-element.35), channel_id=1, source_target_pairs={{16,32},{48,64},{80,96},{32,16},{64,48},{96,80},{17,33},{49,65},{8... | collective-permute-start | bytes 1572872 | tf_op jit(solution)/shard_map/ppermute | solution.py:493
  117.2 9.1 %all-to-all-done.2 = f32[4,256,256]{2,1,0:T(8,128)} async-done(((f32[4,256,256]{2,1,0:T(8,128)}), f32[4,256,256]{2,1,0:T(8,128)}, u32[]{:S(2)}, u32[]{:S(2)}) %all-to-all-start.2) | async-done | bytes 1048608 | tf_op jit(solution)/shard_map/all_to_all | solution.py:485
  126.3 2.0 %reduce_sum.18 = f32[256,256]{1,0:T(8,128)} reduce(f32[4,256,256]{2,1,0:T(8,128)} %all-to-all-done.2, f32[]{:T(128)} %constant.69.clone.1), dimensions={0}, to_apply=%region_0.1 | reduce | flops 196608 | bytes 1310724 | tf_op jit(solution)/shard_map/reduce_sum | solution.py:535
  128.4 10.1 %all-to-all-start.3 = ((f32[16,16,256]{2,1,0:T(8,128)}), f32[16,16,256]{2,1,0:T(8,128)S(1)}, u32[]{:S(2)}, u32[]{:S(2)}) async-start(f32[16,16,256]{2,1,0:T(8,128)} %bitcast.19), calls=%async_computation.3 | async-start | bytes 524288 | tf_op jit(solution)/shard_map/all_to_all | solution.py:485
  138.5 2.7 %shard_map.99 = f32[2,2,256,256]{3,2,1,0:T(8,128)} custom-call(s32[3]{0:T(128)S(1)} %copy-done.7, f32[2,2,256,256]{3,2,1,0:T(8,128)S(1)} %copy-done.1, f32[2,2,512,128]{3,2,1,0:T(8,128)S(1)} %collective-permute-done.12.col_near, f32[2,2,512,128]{3,2,1,0:T(8,128)S(1)} %collective-permute-done.13.col_far, f32[2,2,128,256]{3,2,1,0:T(8,128)} %collective-permute-done.14.row_near), custom_call_target="tpu_custom_call" | custom-call | tf_op jit(solution)/shard_map/pallas_call | solution.py:244
  141.2 2.1 %add_dynamic-update-slice_fusion = f32[2,2,256,256]{3,2,1,0:T(8,128)} fusion(f32[2,2,256,256]{3,2,1,0:T(8,128)} %shard_map.99, s32[]{:T(128)S(6)} %select_n.25, f32[2,2,128,256]{3,2,1,0:T(8,128)} %collective-permute-done.15), kind=kLoop, calls=%fused_computation.1 | loop fusion | flops 131072 | bytes 1572868 | tf_op jit(solution)/shard_map/dynamic_update_slice | solution.py:541
  143.3 10.4 %all-to-all-done.3 = f32[16,16,256]{2,1,0:T(8,128)S(1)} async-done(((f32[16,16,256]{2,1,0:T(8,128)}), f32[16,16,256]{2,1,0:T(8,128)S(1)}, u32[]{:S(2)}, u32[]{:S(2)}) %all-to-all-start.3) | async-done | bytes 262176 | tf_op jit(solution)/shard_map/all_to_all | solution.py:485
  (58 shorter events, 8.4 us)
Async XLA Ops:
  0.6 1.2 copy-start.10
  0.6 2.1 %copy-start = (f32[2,2,256,256]{3,2,1,0:T(8,128)S(1)}, f32[2,2,256,256]{3,2,1,0:T(8,128)}, u32[]{:S(2)}) copy-start(f32[2,2,256,256]{3,2,1,0:T(8,128)} %mid.5) | copy-start | bytes 3145732
  2.8 43.4 %copy-start.6 = (s32[3]{0:T(128)}, s32[3]{0:T(128)S(1)}, u32[]{:S(2)}) copy-start(s32[3]{0:T(128)S(1)} %pad_add_fusion.where) | copy-start | bytes 40
  3.5 14.8 %all-to-all-start = ((f32[4,144,256]{2,1,0:T(8,128)}), f32[4,144,256]{2,1,0:T(8,128)}, u32[]{:S(2)}, u32[]{:S(2)}) async-start(f32[4,144,256]{2,1,0:T(8,128)} %pad_maximum_fusion), calls=%async_computation | async-start | bytes 1179648 | tf_op jit(solution)/shard_map/all_to_all | solution.py:485
  7.9 29.7 %collective-permute-start.3 = (f32[2,2,128,256]{3,2,1,0:T(8,128)S(1)}, f32[2,2,128,256]{3,2,1,0:T(8,128)S(1)}, u32[]{:S(2)}, u32[]{:S(2)}) collective-permute-start(f32[2,2,128,256]{3,2,1,0:T(8,128)S(1)} %get-tuple-element.20), channel_id=1, source_target_pairs={{0,16},{16,0},{1,17},{17,1},{2,18},{18,2},{3,19},{19,3},{4,20},{20... | collective-permute-start | bytes 1572872 | tf_op jit(solution)/shard_map/ppermute | solution.py:493
  9.4 28.2 %collective-permute-start.4 = (f32[2,2,128,256]{3,2,1,0:T(8,128)S(1)}, f32[2,2,128,256]{3,2,1,0:T(8,128)S(1)}, u32[]{:S(2)}, u32[]{:S(2)}) collective-permute-start(f32[2,2,128,256]{3,2,1,0:T(8,128)S(1)} %get-tuple-element.21), channel_id=1, source_target_pairs={{16,32},{48,64},{80,96},{32,16},{64,48},{96,80},{17,33},{49,65},{8... | collective-permute-start | bytes 1572872 | tf_op jit(solution)/shard_map/ppermute | solution.py:493
  19.1 14.7 %collective-permute-start.2 = (f32[64,256]{1,0:T(8,128)S(1)}, f32[64,256]{1,0:T(8,128)S(1)}, u32[]{:S(2)}, u32[]{:S(2)}) collective-permute-start(f32[64,256]{1,0:T(8,128)S(1)} %bitcast.31), channel_id=1, source_target_pairs={{24,0},{0,8},{8,16},{16,24},{25,1},{1,9},{9,17},{17,25},{26,2},{2,... | collective-permute-start | bytes 196616 | tf_op jit(solution)/shard_map/ppermute | solution.py:518
  22.1 13.3 %collective-permute-start.1 = (f32[64,256]{1,0:T(8,128)S(1)}, f32[64,256]{1,0:T(8,128)S(1)}, u32[]{:S(2)}, u32[]{:S(2)}) collective-permute-start(f32[64,256]{1,0:T(8,128)S(1)} %bitcast.32), channel_id=1, source_target_pairs={{16,0},{24,8},{0,16},{8,24},{17,1},{25,9},{1,17},{9,25},{18,2},{26... | collective-permute-start | bytes 196616 | tf_op jit(solution)/shard_map/ppermute | solution.py:518
  22.7 14.9 %collective-permute-start = (f32[64,256]{1,0:T(8,128)S(1)}, f32[64,256]{1,0:T(8,128)S(1)}, u32[]{:S(2)}, u32[]{:S(2)}) collective-permute-start(f32[64,256]{1,0:T(8,128)S(1)} %bitcast.33), channel_id=1, source_target_pairs={{8,0},{16,8},{24,16},{0,24},{9,1},{17,9},{25,17},{1,25},{10,2},{18... | collective-permute-start | bytes 196616 | tf_op jit(solution)/shard_map/ppermute | solution.py:518
  37.6 8.6 %copy-start.2 = (f32[2,2,128,256]{3,2,1,0:T(8,128)}, f32[2,2,128,256]{3,2,1,0:T(8,128)S(1)}, u32[]{:S(2)}) copy-start(f32[2,2,128,256]{3,2,1,0:T(8,128)S(1)} %collective-permute-done.3.row_near) | copy-start | bytes 1572868
  37.7 8.6 %copy-start.3 = (f32[2,2,128,256]{3,2,1,0:T(8,128)}, f32[2,2,128,256]{3,2,1,0:T(8,128)S(1)}, u32[]{:S(2)}) copy-start(f32[2,2,128,256]{3,2,1,0:T(8,128)S(1)} %collective-permute-done.4.row_far) | copy-start | bytes 1572868
  38.8 18.0 %all-to-all-start.1 = ((f32[4,256,256]{2,1,0:T(8,128)}), f32[4,256,256]{2,1,0:T(8,128)}, u32[]{:S(2)}, u32[]{:S(2)}) async-start(f32[4,256,256]{2,1,0:T(8,128)} %broadcast_in_dim.15), calls=%async_computation.1 | async-start | bytes 2097152 | tf_op jit(solution)/shard_map/all_to_all | solution.py:485
  45.3 0.8 copy-start.8
  46.1 7.9 %collective-permute-start.5 = (f32[4,2,2,16,256]{4,3,2,1,0:T(8,128)S(1)}, f32[4,2,2,16,256]{4,3,2,1,0:T(8,128)S(1)}, u32[]{:S(2)}, u32[]{:S(2)}) collective-permute-start(f32[4,2,2,16,256]{4,3,2,1,0:T(8,128)S(1)} %dynamic-slice_bitcast_fusion), channel_id=1, source_target_pairs={{0,8},{8,0},{1,9},{9,1},{2,10},{10,2},{3,11},{11,3},{4,12},{12,4},... | collective-permute-start | bytes 786440 | tf_op jit(solution)/shard_map/ppermute | solution.py:514
  47.8 12.0 %collective-permute-start.9 = (f32[2,2,512,128]{3,2,1,0:T(8,128)}, f32[2,2,512,128]{3,2,1,0:T(8,128)S(1)}, u32[]{:S(2)}, u32[]{:S(2)}) collective-permute-start(f32[2,2,512,128]{3,2,1,0:T(8,128)} %get-tuple-element.25), channel_id=1, source_target_pairs={{0,1},{1,0},{2,3},{3,2},{4,5},{5,4},{6,7},{7,6},{8,9},{9,8},{10,11... | collective-permute-start | bytes 3145736 | tf_op jit(solution)/shard_map/ppermute | solution.py:497
  47.8 12.1 %collective-permute-start.10 = (f32[2,2,512,128]{3,2,1,0:T(8,128)S(1)}, f32[2,2,512,128]{3,2,1,0:T(8,128)S(1)}, u32[]{:S(2)}, u32[]{:S(2)}) collective-permute-start(f32[2,2,512,128]{3,2,1,0:T(8,128)S(1)} %get-tuple-element.26), channel_id=1, source_target_pairs={{1,2},{3,4},{5,6},{7,8},{9,10},{11,12},{13,14},{2,1},{4,3},{6,5},{... | collective-permute-start | bytes 3145736 | tf_op jit(solution)/shard_map/ppermute | solution.py:497
  54.0 4.4 %copy-start.9 = (f32[4,2,2,16,256]{4,3,2,1,0:T(8,128)}, f32[4,2,2,16,256]{4,3,2,1,0:T(8,128)S(1)}, u32[]{:S(2)}) copy-start(f32[4,2,2,16,256]{4,3,2,1,0:T(8,128)S(1)} %collective-permute-done.5.meas_far) | copy-start | bytes 786436
  56.8 3.1 %collective-permute-start.6 = (f32[4,4,4,16,256]{4,3,2,1,0:T(8,128)}, f32[4,4,4,16,256]{4,3,2,1,0:T(8,128)}, u32[]{:S(2)}, u32[]{:S(2)}) collective-permute-start(f32[4,4,4,16,256]{4,3,2,1,0:T(8,128)} %bitcast.13.mine), channel_id=1, source_target_pairs={{0,1},{1,0},{2,3},{3,2},{4,5},{5,4},{6,7},{7,6},{8,9},{9,8},{10,11... | collective-permute-start | bytes 3145736 | tf_op jit(solution)/shard_map/ppermute | solution.py:525
  57.8 1.9 %collective-permute-start.7 = (f32[4,2,16,256]{3,2,1,0:T(8,128)S(1)}, f32[4,2,16,256]{3,2,1,0:T(8,128)S(1)}, u32[]{:S(2)}, u32[]{:S(2)}) collective-permute-start(f32[4,2,16,256]{3,2,1,0:T(8,128)S(1)} %dynamic-slice_bitcast_fusion.2), channel_id=1, source_target_pairs={{0,1},{1,0},{2,3},{3,2},{4,5},{5,4},{6,7},{7,6},{8,9},{9,8},{10,11... | collective-permute-start | bytes 393224 | tf_op jit(solution)/shard_map/ppermute | solution.py:515
  58.4 1.5 collective-permute-start.8
  59.9 1.0 copy-start.11
  59.9 1.4 copy-start.12
  97.2 6.7 %collective-permute-start.11 = (f32[4,4,4,16,256]{4,3,2,1,0:T(8,128)}, f32[4,4,4,16,256]{4,3,2,1,0:T(8,128)S(1)}, u32[]{:S(2)}, u32[]{:S(2)}) collective-permute-start(f32[4,4,4,16,256]{4,3,2,1,0:T(8,128)} %get-tuple-element.29), channel_id=1, source_target_pairs={{0,1},{1,0},{2,3},{3,2},{4,5},{5,4},{6,7},{7,6},{8,9},{9,8},{10,11... | collective-permute-start | bytes 3145736 | tf_op jit(solution)/shard_map/ppermute | solution.py:530
  101.4 9.9 %collective-permute-start.12 = (f32[2,2,512,128]{3,2,1,0:T(8,128)}, f32[2,2,512,128]{3,2,1,0:T(8,128)S(1)}, u32[]{:S(2)}, u32[]{:S(2)}) collective-permute-start(f32[2,2,512,128]{3,2,1,0:T(8,128)} %get-tuple-element.32), channel_id=1, source_target_pairs={{0,1},{1,0},{2,3},{3,2},{4,5},{5,4},{6,7},{7,6},{8,9},{9,8},{10,11... | collective-permute-start | bytes 3145736 | tf_op jit(solution)/shard_map/ppermute | solution.py:497
  101.5 9.8 %collective-permute-start.13 = (f32[2,2,512,128]{3,2,1,0:T(8,128)}, f32[2,2,512,128]{3,2,1,0:T(8,128)S(1)}, u32[]{:S(2)}, u32[]{:S(2)}) collective-permute-start(f32[2,2,512,128]{3,2,1,0:T(8,128)} %get-tuple-element.33), channel_id=1, source_target_pairs={{1,2},{3,4},{5,6},{7,8},{9,10},{11,12},{13,14},{2,1},{4,3},{6,5},{... | collective-permute-start | bytes 3145736 | tf_op jit(solution)/shard_map/ppermute | solution.py:497
  106.3 5.0 %copy-start.4 = (f32[2,2,128,256]{3,2,1,0:T(8,128)S(1)}, f32[2,2,128,256]{3,2,1,0:T(8,128)}, u32[]{:S(2)}) copy-start(f32[2,2,128,256]{3,2,1,0:T(8,128)} %get-tuple-element.30.row_near) | copy-start | bytes 1572868
  106.3 5.0 %copy-start.5 = (f32[2,2,128,256]{3,2,1,0:T(8,128)S(1)}, f32[2,2,128,256]{3,2,1,0:T(8,128)}, u32[]{:S(2)}) copy-start(f32[2,2,128,256]{3,2,1,0:T(8,128)} %get-tuple-element.31.row_far) | copy-start | bytes 1572868
  106.3 20.0 %all-to-all-start.2 = ((f32[4,256,256]{2,1,0:T(8,128)}), f32[4,256,256]{2,1,0:T(8,128)}, u32[]{:S(2)}, u32[]{:S(2)}) async-start(f32[4,256,256]{2,1,0:T(8,128)} %bitcast.24), calls=%async_computation.2 | async-start | bytes 2097152 | tf_op jit(solution)/shard_map/all_to_all | solution.py:485
  113.8 24.7 %copy-start.1 = (f32[2,2,256,256]{3,2,1,0:T(8,128)S(1)}, f32[2,2,256,256]{3,2,1,0:T(8,128)}, u32[]{:S(2)}) copy-start(f32[2,2,256,256]{3,2,1,0:T(8,128)} %get-tuple-element.37.mid) | copy-start | bytes 3145732
  113.8 24.7 %collective-permute-start.14 = (f32[2,2,128,256]{3,2,1,0:T(8,128)}, f32[2,2,128,256]{3,2,1,0:T(8,128)}, u32[]{:S(2)}, u32[]{:S(2)}) collective-permute-start(f32[2,2,128,256]{3,2,1,0:T(8,128)} %get-tuple-element.34), channel_id=1, source_target_pairs={{0,16},{16,0},{1,17},{17,1},{2,18},{18,2},{3,19},{19,3},{4,20},{20... | collective-permute-start | bytes 1572872 | tf_op jit(solution)/shard_map/ppermute | solution.py:493
  114.6 26.6 %collective-permute-start.15 = (f32[2,2,128,256]{3,2,1,0:T(8,128)}, f32[2,2,128,256]{3,2,1,0:T(8,128)}, u32[]{:S(2)}, u32[]{:S(2)}) collective-permute-start(f32[2,2,128,256]{3,2,1,0:T(8,128)} %get-tuple-element.35), channel_id=1, source_target_pairs={{16,32},{48,64},{80,96},{32,16},{64,48},{96,80},{17,33},{49,65},{8... | collective-permute-start | bytes 1572872 | tf_op jit(solution)/shard_map/ppermute | solution.py:493
  128.4 25.4 %all-to-all-start.3 = ((f32[16,16,256]{2,1,0:T(8,128)}), f32[16,16,256]{2,1,0:T(8,128)S(1)}, u32[]{:S(2)}, u32[]{:S(2)}) async-start(f32[16,16,256]{2,1,0:T(8,128)} %bitcast.19), calls=%async_computation.3 | async-start | bytes 524288 | tf_op jit(solution)/shard_map/all_to_all | solution.py:485
  (3 other events, 2.0 us)

commit v4 on v3

--- a/solution.py
+++ b/solution.py
@@ -54,24 +54,26 @@
 def left_product(tabs, i, x):
     top, rest = split(x)
     hi, lo = tabs
-    return dot(hi[i], top) + dot(lo[i], top) + dot(hi[i], rest)
+    y = dot(jnp.concatenate([hi[i], lo[i]], 0), top)
+    return y[:W] + (y[W:] + dot(hi[i], rest))
 
 
 def right_product(tabs, i, x):
     top, rest = split(x)
     hi, lo = tabs
-    return dot(top, hi[i]) + dot(top, lo[i]) + dot(rest, hi[i])
+    y = dot(jnp.concatenate([top, rest], 0), hi[i])
+    return y[:W] + (y[W:] + dot(top, lo[i]))
 
 
 def halves(x, axis):
     return (x[:H], x[H:]) if axis == 0 else (x[:, :H], x[:, H:])
 
 
-def one_side(tabs, axis, ia, ib, xr, xi, fold_in, fold_out):
-    (ar, br), (ai, bi) = halves(xr, axis), halves(xi, axis)
+def one_field(tabs, axis, ia, ib, field, fold_in, fold_out):
+    product = left_product if axis == 0 else right_product
+    (ar, br), (ai, bi) = halves(field[0], axis), halves(field[1], axis)
     if fold_in:
         ar, br, ai, bi = ar + br, ar - br, ai + bi, ai - bi
-    product = left_product if axis == 0 else right_product
     ya = product(tabs, ia, jnp.concatenate([ar, ai], axis))
     yb = product(tabs, ib, jnp.concatenate([br, bi], axis))
     if fold_out:
@@ -80,20 +82,24 @@
     return jnp.concatenate([ar, br], axis), jnp.concatenate([ai, bi], axis)
 
 
-def propagate(tabs, xr, xi, adjoint):
+def one_side(tabs, axis, ia, ib, fields, fold_in, fold_out):
+    return [one_field(tabs, axis, ia, ib, field, fold_in, fold_out) for field in fields]
+
+
+def propagate(tabs, fields, adjoint):
     t = 1 if adjoint else 0
-    xr, xi = one_side(tabs, 0, 0 + t, 2 + t, xr, xi, True, True)
-    return one_side(tabs, 1, 1 - t, 3 - t, xr, xi, True, True)
-
-
-def dft(tabs, xr, xi):
-    xr, xi = one_side(tabs, 0, 4, 6, xr, xi, True, False)
-    return one_side(tabs, 1, 5, 7, xr, xi, True, False)
-
-
-def dft_adjoint(tabs, xr, xi):
-    xr, xi = one_side(tabs, 0, 5, 7, xr, xi, False, True)
-    return one_side(tabs, 1, 4, 6, xr, xi, False, True)
+    fields = one_side(tabs, 0, 0 + t, 2 + t, fields, True, True)
+    return one_side(tabs, 1, 1 - t, 3 - t, fields, True, True)
+
+
+def dft(tabs, fields):
+    fields = one_side(tabs, 0, 4, 6, fields, True, False)
+    return one_side(tabs, 1, 5, 7, fields, True, False)
+
+
+def dft_adjoint(tabs, fields):
+    fields = one_side(tabs, 0, 5, 7, fields, False, True)
+    return one_side(tabs, 1, 4, 6, fields, False, True)
 
 
 def params():
@@ -313,128 +319,162 @@
                     win[s, j, p, :, k * H : k * H + H] = x.reshape(W, H)
 
 
-def place(pos, grad, ext):
+def place(pos, grad, ext, j):
     lane = lax.broadcasted_iota(jnp.int32, (W + 8, H), 1)
     sub = lax.broadcasted_iota(jnp.int32, (W // 8 + 1, 8, H), 1)
     group = jnp.zeros((1, 8, H), f32)
-    ext[...] = jnp.zeros_like(ext)
+    ext[j] = jnp.zeros(ext.shape[1:], f32)
     for s in range(SLOTS):
         rows, cols, dr, dc = corner(pos, s)
-        for j in range(2):
-            for p in range(2):
-                turned = []
-                for k in range(2):
-                    x = grad[s, j, p, :, k * H : k * H + H].reshape(W // 8, 8, H)
-                    x = pltpu.roll(x, dr, 1)
-                    x = jnp.where(
-                        sub >= dr,
-                        jnp.concatenate([x, group], 0),
-                        jnp.concatenate([group, x], 0),
-                    )
-                    turned.append(pltpu.roll(x.reshape(W + 8, H), dc, 1))
-                ext[j, p, rows, cols[0]] += jnp.where(lane >= dc, turned[0], 0.0)
-                ext[j, p, rows, cols[1]] += jnp.where(lane >= dc, turned[1], turned[0])
-                ext[j, p, rows, cols[2]] += jnp.where(lane >= dc, 0.0, turned[1])
-
-
-def forward_step(tabs, probe, win, u, far, intensity, k):
-    m, s = k // 2, k % 2
-    pr, pi = probe[m, 0], probe[m, 1]
-    a, b = win[s, 0, 0], win[s, 0, 1]
-    ur, ui = propagate(tabs, pr * a - pi * b, pr * b + pi * a, False)
-    u[k, 0] = ur
-    u[k, 1] = ui
-    a, b = win[s, 1, 0], win[s, 1, 1]
-    fr, fi = dft(tabs, ur * a - ui * b, ur * b + ui * a)
-    far[k, 0] = fr
-    far[k, 1] = fi
-    power = fr * fr + fi * fi
-    intensity[s] = jnp.where(m == 0, power, intensity[s] + power)
-
-
-def backward_step(tabs, probe, win, u, far, scale, grad_probe, grad_win, k):
-    m, s = k // 2, k % 2
-    factor = scale[s]
-    gr, gi = dft_adjoint(tabs, factor * far[k, 0], factor * far[k, 1])
-    ur, ui = u[k, 0], u[k, 1]
-    vr = gr * ur + gi * ui
-    vi = gi * ur - gr * ui
-    grad_win[s, 1, 0] = jnp.where(m == 0, vr, grad_win[s, 1, 0] + vr)
-    grad_win[s, 1, 1] = jnp.where(m == 0, vi, grad_win[s, 1, 1] + vi)
-    a, b = win[s, 1, 0], win[s, 1, 1]
-    gr, gi = propagate(tabs, gr * a + gi * b, gi * a - gr * b, True)
-    pr, pi = probe[m, 0], probe[m, 1]
-    wr = gr * pr + gi * pi
-    wi = gi * pr - gr * pi
-    grad_win[s, 0, 0] = jnp.where(m == 0, wr, grad_win[s, 0, 0] + wr)
-    grad_win[s, 0, 1] = jnp.where(m == 0, wi, grad_win[s, 0, 1] + wi)
-    a, b = win[s, 0, 0], win[s, 0, 1]
-    qr = gr * a + gi * b
-    qi = gi * a - gr * b
-    grad_probe[m, 0] = jnp.where(s == 0, qr, grad_probe[m, 0] + qr)
-    grad_probe[m, 1] = jnp.where(s == 0, qi, grad_probe[m, 1] + qi)
+        for p in range(2):
+            turned = []
+            for k in range(2):
+                x = grad[s, j, p, :, k * H : k * H + H].reshape(W // 8, 8, H)
+                x = pltpu.roll(x, dr, 1)
+                x = jnp.where(
+                    sub >= dr,
+                    jnp.concatenate([x, group], 0),
+                    jnp.concatenate([group, x], 0),
+                )
+                turned.append(pltpu.roll(x.reshape(W + 8, H), dc, 1))
+            ext[j, p, rows, cols[0]] += jnp.where(lane >= dc, turned[0], 0.0)
+            ext[j, p, rows, cols[1]] += jnp.where(lane >= dc, turned[1], turned[0])
+            ext[j, p, rows, cols[2]] += jnp.where(lane >= dc, 0.0, turned[1])
+
+
+def times(x, y):
+    return x[0] * y[0] - x[1] * y[1], x[0] * y[1] + x[1] * y[0]
+
+
+def times_conj(x, y):
+    return x[0] * y[0] + x[1] * y[1], x[1] * y[0] - x[0] * y[1]
+
+
+def read(ref, *index):
+    return ref[(*index, 0)], ref[(*index, 1)]
+
+
+def write(ref, value, *index):
+    for part in range(2):
+        ref[(*index, part)] = value[part]
+
+
+def add_to(ref, value, first, *index):
+    for part in range(2):
+        at = (*index, part)
+        ref[at] = jnp.where(first, value[part], ref[at] + value[part])
+
+
+def forward_step(tabs, probe, win, u, far, intensity, m):
+    slots = range(SLOTS)
+    here = read(probe, m)
+    fields = propagate(tabs, [times(here, read(win, s, 0)) for s in slots], False)
+    for s in slots:
+        write(u, fields[s], m, s)
+    fields = dft(tabs, [times(fields[s], read(win, s, 1)) for s in slots])
+    for s in slots:
+        write(far, fields[s], m, s)
+        power = fields[s][0] * fields[s][0] + fields[s][1] * fields[s][1]
+        intensity[s] = jnp.where(m == 0, power, intensity[s] + power)
+
+
+def backward_step(tabs, probe, win, u, far, scale, grad_probe, grad_win, m, between):
+    slots = range(SLOTS)
+    fields = [tuple(scale[s] * part for part in read(far, m, s)) for s in slots]
+    fields = dft_adjoint(tabs, fields)
+    for s in slots:
+        add_to(grad_win, times_conj(fields[s], read(u, m, s)), m == 0, s, 1)
+    between()
+    fields = propagate(tabs, [times_conj(fields[s], read(win, s, 1)) for s in slots], True)
+    here = read(probe, m)
+    for s in slots:
+        add_to(grad_win, times_conj(fields[s], here), m == 0, s, 0)
+    terms = [times_conj(fields[s], read(win, s, 0)) for s in slots]
+    write(grad_probe, tuple(a + b for a, b in zip(*terms)))
 
 
 def main_kernel(
     loss_scale, where, pos, counts, order, high, low, mine, other, meas, meas_core, meas_far, meas_far_core,
     mid, row_near, row_far, col_near, col_far,
     out_mine, out_other, out_mid, out_row_near, out_row_far, out_col_near, out_col_far,
-    ext, win, probe, u, far, scale, grad_probe, grad_win, blocks, hi, lo, rows, pattern, perm, sems, more_sems,
+    ext, win, probe, u, far, scale, grad_probe, grad_win, blocks, out_blocks, hi, lo, rows, pattern, perm,
+    meas_sems, ext_sems, table_sems, probe_sems, out_sems,
 ):
-    copies = start_all(ext_pieces(where, ext, mid, row_near, row_far, col_near, col_far), sems)
     c, h, xl = where[0], where[1], where[2]
-    pairs = [(high, hi), (low, lo), (mine, blocks.at[0]), (other, blocks.at[1]), (order, perm)]
-    pairs += [(meas.at[:, h, c], rows.at[0, 0]), (meas_core, rows.at[0, 1])]
-    pairs += [(meas_far.at[:, c], rows.at[1, 0]), (meas_far_core, rows.at[1, 1])]
-    more = start_all(pairs, more_sems)
-    wait_all(copies)
+    pairs = [(meas.at[:, h, c], rows.at[0, 0]), (meas_core, rows.at[0, 1])]
+    pairs += [(meas_far.at[:, c], rows.at[1, 0]), (meas_far_core, rows.at[1, 1]), (order, perm)]
+    meas_copies = start_all(pairs, meas_sems)
+    ext_copies = start_all(ext_pieces(where, ext, mid, row_near, row_far, col_near, col_far), ext_sems)
+    table_copies = start_all([(high, hi), (low, lo)], table_sems)
+
+    def probe_copies(m):
+        pairs = ((mine, 0), (other, 1))
+        return [pltpu.make_async_copy(a.at[m], blocks.at[k, m], probe_sems.at[m, k]) for a, k in pairs]
+
+    for m in range(MODES):
+        for copy in probe_copies(m):
+            copy.start()
+    wait_all(meas_copies)
+    for s in range(SLOTS):
+        for i, half in ((0, h), (1, 1 - h)):
+            for k, core in ((0, c), (1, 1 - c)):
+                for y in range(4):
+                    start = pl.multiple_of(half * H + y * 32 + core * 16, 16)
+                    pattern[s, pl.ds(start, 16), :] = rows[i, k, y, s]
+        pattern[s] = reordered(perm, pattern[s])
+    wait_all(ext_copies)
     extract(pos, ext, win)
-    wait_all(more)
-    for m in range(MODES):
+    wait_all(table_copies)
+    tabs = (hi, lo)
+
+    def forward(m, _):
+        wait_all(probe_copies(m))
         for k in range(4):
             x = (2 * xl + h + k) % 4
             for y in range(4):
                 probe[m, x // 2, block_rows(x, y, c), :] = blocks[0, m, k, y]
                 probe[m, x // 2, block_rows(x, y, 1 - c), :] = blocks[1, m, k, y]
-    tabs = (hi, lo)
-
-    def forward(k, _):
-        forward_step(tabs, probe, win, u, far, scale, k)
+        forward_step(tabs, probe, win, u, far, scale, m)
         return 0
 
-    lax.fori_loop(0, MODES * SLOTS, forward, 0)
+    lax.fori_loop(0, MODES, forward, 0)
     for s in range(SLOTS):
         weight = jnp.where(s < counts[0, 0], 2.0 * loss_scale, 0.0)
-        for i, half in ((0, h), (1, 1 - h)):
-            for k, core in ((0, c), (1, 1 - c)):
-                for y in range(4):
-                    start = pl.multiple_of(half * H + y * 32 + core * 16, 16)
-                    pattern[pl.ds(start, 16), :] = rows[i, k, y, s]
-        amplitude = reordered(perm, pattern[...])
-        scale[s] = weight * (1.0 - amplitude * lax.rsqrt(scale[s] + amp_floor))
-
-    def backward(k, _):
-        backward_step(tabs, probe, win, u, far, scale, grad_probe, grad_win, k)
-        return 0
-
-    lax.fori_loop(0, MODES * SLOTS, backward, 0)
-    place(pos, grad_win, ext)
-    pairs = ext_pieces(where, ext, out_mid, out_row_near, out_row_far, out_col_near, out_col_far)
-    copies = start_all([(b, a) for a, b in pairs], sems)
-    for m in range(MODES):
+        scale[s] = weight * (1.0 - pattern[s] * lax.rsqrt(scale[s] + amp_floor))
+
+    def out_copies(m):
+        pairs = ((out_mine, 0), (out_other, 1))
+        return [pltpu.make_async_copy(out_blocks.at[k, m], a.at[m], probe_sems.at[m, k]) for a, k in pairs]
+
+    def backward(m, between):
+        backward_step(tabs, probe, win, u, far, scale, grad_probe, grad_win, m, between)
         for x in range(4):
             for y in range(4):
-                out_mine[m, x, y] = grad_probe[m, x // 2, block_rows(x, y, c), :]
-                out_other[m, x, y] = grad_probe[m, x // 2, block_rows(x, y, 1 - c), :]
+                out_blocks[0, m, x, y] = grad_probe[x // 2, block_rows(x, y, c), :]
+                out_blocks[1, m, x, y] = grad_probe[x // 2, block_rows(x, y, 1 - c), :]
+        for copy in out_copies(m):
+            copy.start()
+        return 0
+
+    def place_slice(j):
+        place(pos, grad_win, ext, j)
+        pairs = ext_pieces(where, ext, out_mid, out_row_near, out_row_far, out_col_near, out_col_far)
+        return start_all([(b.at[j], a.at[j]) for a, b in pairs], out_sems.at[j])
+
+    copies = []
+    lax.fori_loop(0, MODES - 1, lambda m, _: backward(m, lambda: None), 0)
+    backward(MODES - 1, lambda: copies.extend(place_slice(1)))
+    copies += place_slice(0)
+    for m in range(MODES):
+        copies += out_copies(m)
     wait_all(copies)
 
 
 def gradients(tabs, loss_scale, where, pos, counts, *arrays):
-    steps = MODES * SLOTS
     return pl.pallas_call(
         functools.partial(main_kernel, loss_scale),
         in_specs=[SMEM] * 3 + [HBM] * 14,
-        out_specs=[VMEM] * 2 + [HBM] * 5,
+        out_specs=[HBM] * 7,
         out_shape=[
             struct(*PROBE),
             struct(*PROBE),
@@ -448,19 +488,23 @@
             pltpu.VMEM((2, 2, 2 * W, 2 * W), f32),
             pltpu.VMEM((SLOTS, 2, 2, W, W), f32),
             pltpu.VMEM((MODES, 2, W, W), f32),
-            pltpu.VMEM((steps, 2, W, W), f32),
-            pltpu.VMEM((steps, 2, W, W), f32),
+            pltpu.VMEM((MODES, SLOTS, 2, W, W), f32),
+            pltpu.VMEM((MODES, SLOTS, 2, W, W), f32),
             pltpu.VMEM((SLOTS, W, W), f32),
-            pltpu.VMEM((MODES, 2, W, W), f32),
+            pltpu.VMEM((2, W, W), f32),
             pltpu.VMEM((SLOTS, 2, 2, W, W), f32),
+            pltpu.VMEM((2,) + PROBE, f32),
             pltpu.VMEM((2,) + PROBE, f32),
             pltpu.VMEM((8, W, W), bf16),
             pltpu.VMEM((8, W, W), bf16),
             pltpu.VMEM((2, 2, 4, SLOTS, 16, W), f32),
-            pltpu.VMEM((W, W), f32),
+            pltpu.VMEM((SLOTS, W, W), f32),
             pltpu.VMEM((2, W, W), bf16),
             pltpu.SemaphoreType.DMA((5,)),
-            pltpu.SemaphoreType.DMA((9,)),
+            pltpu.SemaphoreType.DMA((5,)),
+            pltpu.SemaphoreType.DMA((2,)),
+            pltpu.SemaphoreType.DMA((MODES, 2)),
+            pltpu.SemaphoreType.DMA((2, 5)),
         ],
         compiler_params=pltpu.CompilerParams(vmem_limit_bytes=MAIN_BYTES),
         cost_estimate=cost(32),

time: 157 us -> 147 us (0.936)
  the two profiles are of different devices: /device:TPU:32 before, /device:TPU:1 now
where the time goes in v4:
time: 147 us; the launch traced here: 146 us
  waiting for transfers between devices  51.4 us (35%)
  starting transfers between devices  45.1 us (31%)
  Pallas kernels  32 us (22%)
  other arithmetic  8.08 us (5%)
  local copies, waits for them, and re-layouts  7.65 us (5%)
  between operations  1.59 us (1%)
    all_to_all x4, waiting for transfers between devices, exchange(): return lax.all_to_all(x, axes, split_axis=0, concat_axis=0, tiled=True)  28.8 us
    pallas_call x1, Pallas kernels, gradients(): pl.pallas_call(functools.partial(main_kernel, loss_scale), in_specs=[SMEM...  25.2 us
    all_to_all x4, starting transfers between devices, exchange(): return lax.all_to_all(x, axes, split_axis=0, concat_axis=0, tiled=True)  24 us
    ppermute x3, waiting for transfers between devices, body(): lax.ppermute(probe_rows, ('xl', 'xh'), [((i + k) % 4, i) for i in range(4)])  12.7 us
    ppermute x4, waiting for transfers between devices, swap_columns(): return (lax.ppermute(near, 'c', SWAP), lax.ppermute(far, TX, far_pairs(16)))  9.5 us
    ppermute x4, starting transfers between devices, swap_columns(): return (lax.ppermute(near, 'c', SWAP), lax.ppermute(far, TX, far_pairs(16)))  9.44 us
    ppermute x4, starting transfers between devices, swap_rows(): return (lax.ppermute(near, 'xl', SWAP), lax.ppermute(far, TY, far_pairs(8)))  3.92 us
    ppermute x1, starting transfers between devices, body(): other = lax.ppermute(after(mine, meas_far), 'c', SWAP)  3.6 us
  transfers between devices with their start and end apart: 20, of which 9 were waited for; matrix products, arithmetic and copies ran while one was open for 6% of the time, Pallas kernels for 4%

profile of v4, /device:TPU:1, one launch (start us, length us, event | category | flops | bytes accessed | tf_op | source)
XLA Modules:
  0.0 145.9 jit_solution(2924886144697711187)
XLA Ops:
  0.7 1.2 copy.11
  1.9 0.9 pad_maximum_fusion
  3.5 5.0 %all-to-all-start = ((f32[4,144,256]{2,1,0:T(8,128)}), f32[4,144,256]{2,1,0:T(8,128)}, u32[]{:S(2)}, u32[]{:S(2)}) async-start(f32[4,144,256]{2,1,0:T(8,128)} %pad_maximum_fusion), calls=%async_computation | async-start | bytes 1179648 | tf_op jit(solution)/shard_map/all_to_all | solution.py:529
  8.5 1.3 collective-permute-start.3
  10.4 7.4 %all-to-all-done = f32[4,144,256]{2,1,0:T(8,128)} async-done(((f32[4,144,256]{2,1,0:T(8,128)}), f32[4,144,256]{2,1,0:T(8,128)}, u32[]{:S(2)}, u32[]{:S(2)}) %all-to-all-start) | async-done | bytes 589856 | tf_op jit(solution)/shard_map/all_to_all | solution.py:529
  18.7 2.7 %collective-permute-start.2 = (f32[64,256]{1,0:T(8,128)S(1)}, f32[64,256]{1,0:T(8,128)S(1)}, u32[]{:S(2)}, u32[]{:S(2)}) collective-permute-start(f32[64,256]{1,0:T(8,128)S(1)} %bitcast.31), channel_id=1, source_target_pairs={{24,0},{0,8},{8,16},{16,24},{25,1},{1,9},{9,17},{17,25},{26,2},{2,... | collective-permute-start | bytes 196616 | tf_op jit(solution)/shard_map/ppermute | solution.py:562
  22.0 1.0 collective-permute-done.2
  23.0 11.7 %collective-permute-done.1 = f32[64,256]{1,0:T(8,128)S(1)} collective-permute-done((f32[64,256]{1,0:T(8,128)S(1)}, f32[64,256]{1,0:T(8,128)S(1)}, u32[]{:S(2)}, u32[]{:S(2)}) %collective-permute-start.1) | collective-permute-done | bytes 65568 | tf_op jit(solution)/shard_map/ppermute | solution.py:562
  34.8 1.2 broadcast_in_dim.15
  35.9 7.3 %all-to-all-start.1 = ((f32[4,256,256]{2,1,0:T(8,128)}), f32[4,256,256]{2,1,0:T(8,128)}, u32[]{:S(2)}, u32[]{:S(2)}) async-start(f32[4,256,256]{2,1,0:T(8,128)} %broadcast_in_dim.15), calls=%async_computation.1 | async-start | bytes 2097152 | tf_op jit(solution)/shard_map/all_to_all | solution.py:529
  43.3 1.1 slice.9
  45.1 1.6 %shard_map.96 = (f32[2,2,512,128]{3,2,1,0:T(8,128)}, f32[2,2,512,128]{3,2,1,0:T(8,128)S(1)}) custom-call(s32[3]{0:T(128)S(1)} %pad_add_fusion.where, f32[2,2,256,256]{3,2,1,0:T(8,128)S(1)} %copy-done, f32[2,2,128,256]{3,2,1,0:T(8,128)S(1)} %collective-permute-done.3.row_near, f32[2,2,128,256]{3,2,1,0:T(8,128)S(1)} %collective-permute-done.4.row_far), custom_call_target="tpu_custom_call" | custom-call | tf_op jit(solution)/shard_map/pallas_call | solution.py:167
  46.8 2.5 %collective-permute-start.9 = (f32[2,2,512,128]{3,2,1,0:T(8,128)}, f32[2,2,512,128]{3,2,1,0:T(8,128)S(1)}, u32[]{:S(2)}, u32[]{:S(2)}) collective-permute-start(f32[2,2,512,128]{3,2,1,0:T(8,128)} %get-tuple-element.25), channel_id=1, source_target_pairs={{0,1},{1,0},{2,3},{3,2},{4,5},{5,4},{6,7},{7,6},{8,9},{9,8},{10,11... | collective-permute-start | bytes 3145736 | tf_op jit(solution)/shard_map/ppermute | solution.py:541
  49.2 3.2 %collective-permute-start.10 = (f32[2,2,512,128]{3,2,1,0:T(8,128)S(1)}, f32[2,2,512,128]{3,2,1,0:T(8,128)S(1)}, u32[]{:S(2)}, u32[]{:S(2)}) collective-permute-start(f32[2,2,512,128]{3,2,1,0:T(8,128)S(1)} %get-tuple-element.26), channel_id=1, source_target_pairs={{1,2},{3,4},{5,6},{7,8},{9,10},{11,12},{13,14},{2,1},{4,3},{6,5},{... | collective-permute-start | bytes 3145736 | tf_op jit(solution)/shard_map/ppermute | solution.py:541
  52.4 3.4 %all-to-all-done.1 = f32[4,256,256]{2,1,0:T(8,128)} async-done(((f32[4,256,256]{2,1,0:T(8,128)}), f32[4,256,256]{2,1,0:T(8,128)}, u32[]{:S(2)}, u32[]{:S(2)}) %all-to-all-start.1) | async-done | bytes 1048608 | tf_op jit(solution)/shard_map/all_to_all | solution.py:529
  55.8 3.6 %collective-permute-start.6 = (f32[4,4,4,16,256]{4,3,2,1,0:T(8,128)}, f32[4,4,4,16,256]{4,3,2,1,0:T(8,128)}, u32[]{:S(2)}, u32[]{:S(2)}) collective-permute-start(f32[4,4,4,16,256]{4,3,2,1,0:T(8,128)} %bitcast.13.mine), channel_id=1, source_target_pairs={{0,1},{1,0},{2,3},{3,2},{4,5},{5,4},{6,7},{7,6},{8,9},{9,8},{10,11... | collective-permute-start | bytes 3145736 | tf_op jit(solution)/shard_map/ppermute | solution.py:569
  59.4 0.9 dynamic-slice_bitcast_fusion.2
  62.2 3.1 %collective-permute-done.10.col_far = f32[2,2,512,128]{3,2,1,0:T(8,128)S(1)} collective-permute-done((f32[2,2,512,128]{3,2,1,0:T(8,128)S(1)}, f32[2,2,512,128]{3,2,1,0:T(8,128)S(1)}, u32[]{:S(2)}, u32[]{:S(2)}) %collective-permute-start.10) | collective-permute-done | bytes 1048608 | tf_op jit(solution)/shard_map/ppermute | solution.py:541
  65.4 1.0 copy-done.12
  66.3 25.2 %shard_map.97 = (f32[4,4,4,16,256]{4,3,2,1,0:T(8,128)}, f32[4,4,4,16,256]{4,3,2,1,0:T(8,128)}, f32[2,2,256,256]{3,2,1,0:T(8,128)}, f32[2,2,128,256]{3,2,1,0:T(8,...) custom-call(s32[3]{0:T(128)} %copy-done.6, s32[2,2]{1,0:T(2,128)} %bitcast.38, ...), custom_call_target="tpu_custom_call" | custom-call | flops 38400000000 | bytes 1048576 | tf_op jit(solution)/shard_map/pallas_call | solution.py:474
  92.1 3.3 %collective-permute-start.13 = (f32[2,2,512,128]{3,2,1,0:T(8,128)}, f32[2,2,512,128]{3,2,1,0:T(8,128)S(1)}, u32[]{:S(2)}, u32[]{:S(2)}) collective-permute-start(f32[2,2,512,128]{3,2,1,0:T(8,128)} %get-tuple-element.33), channel_id=1, source_target_pairs={{1,2},{3,4},{5,6},{7,8},{9,10},{11,12},{13,14},{2,1},{4,3},{6,5},{... | collective-permute-start | bytes 3145736 | tf_op jit(solution)/shard_map/ppermute | solution.py:541
  95.4 2.4 %add.33 = f32[4,4,4,16,256]{4,3,2,1,0:T(8,128)} add(f32[4,4,4,16,256]{4,3,2,1,0:T(8,128)} %get-tuple-element.28, f32[4,4,4,16,256]{4,3,2,1,0:T(8,128)S(1)} %collective-permute-done.11) | non-fusion elementwise | flops 262144 | bytes 3145728 | tf_op jit(solution)/shard_map/add | solution.py:574
  97.8 4.6 %all-to-all-start.2 = ((f32[4,256,256]{2,1,0:T(8,128)}), f32[4,256,256]{2,1,0:T(8,128)}, u32[]{:S(2)}, u32[]{:S(2)}) async-start(f32[4,256,256]{2,1,0:T(8,128)} %bitcast.24), calls=%async_computation.2 | async-start | bytes 2097152 | tf_op jit(solution)/shard_map/all_to_all | solution.py:529
  102.5 6.4 %collective-permute-done.13.col_far = f32[2,2,512,128]{3,2,1,0:T(8,128)S(1)} collective-permute-done((f32[2,2,512,128]{3,2,1,0:T(8,128)}, f32[2,2,512,128]{3,2,1,0:T(8,128)S(1)}, u32[]{:S(2)}, u32[]{:S(2)}) %collective-permute-start.13) | collective-permute-done | bytes 1048608 | tf_op jit(solution)/shard_map/ppermute | solution.py:541
  109.5 1.8 %shard_map.98 = (f32[2,2,128,256]{3,2,1,0:T(8,128)}, f32[2,2,128,256]{3,2,1,0:T(8,128)}) custom-call(s32[3]{0:T(128)S(1)} %copy-done.7, f32[2,2,128,256]{3,2,1,0:T(8,128)S(1)} %copy-done.4, f32[2,2,128,256]{3,2,1,0:T(8,128)S(1)} %copy-done.5, f32[2,2,512,128]{3,2,1,0:T(8,128)S(1)} %collective-permute-done.12.col_near, ...), custom_call_target="tpu_custom_call" | custom-call | tf_op jit(solution)/shard_map/pallas_call | solution.py:213
  111.9 1.5 collective-permute-start.15
  113.4 7.1 %all-to-all-done.2 = f32[4,256,256]{2,1,0:T(8,128)} async-done(((f32[4,256,256]{2,1,0:T(8,128)}), f32[4,256,256]{2,1,0:T(8,128)}, u32[]{:S(2)}, u32[]{:S(2)}) %all-to-all-start.2) | async-done | bytes 1048608 | tf_op jit(solution)/shard_map/all_to_all | solution.py:529
  120.4 2.0 %reduce_sum.18 = f32[256,256]{1,0:T(8,128)} reduce(f32[4,256,256]{2,1,0:T(8,128)} %all-to-all-done.2, f32[]{:T(128)} %constant.69.clone.1), dimensions={0}, to_apply=%region_0.1 | reduce | flops 196608 | bytes 1310724 | tf_op jit(solution)/shard_map/reduce_sum | solution.py:579
  122.4 7.0 %all-to-all-start.3 = ((f32[16,16,256]{2,1,0:T(8,128)}), f32[16,16,256]{2,1,0:T(8,128)S(1)}, u32[]{:S(2)}, u32[]{:S(2)}) async-start(f32[16,16,256]{2,1,0:T(8,128)} %bitcast.19), calls=%async_computation.3 | async-start | bytes 524288 | tf_op jit(solution)/shard_map/all_to_all | solution.py:529
  129.4 2.7 %shard_map.99 = f32[2,2,256,256]{3,2,1,0:T(8,128)} custom-call(s32[3]{0:T(128)S(1)} %copy-done.7, f32[2,2,256,256]{3,2,1,0:T(8,128)S(1)} %copy-done.1, f32[2,2,512,128]{3,2,1,0:T(8,128)S(1)} %collective-permute-done.12.col_near, f32[2,2,512,128]{3,2,1,0:T(8,128)S(1)} %collective-permute-done.13.col_far, f32[2,2,128,256]{3,2,1,0:T(8,128)} %collective-permute-done.14.row_near), custom_call_target="tpu_custom_call" | custom-call | tf_op jit(solution)/shard_map/pallas_call | solution.py:250
  132.2 2.1 %add_dynamic-update-slice_fusion = f32[2,2,256,256]{3,2,1,0:T(8,128)} fusion(f32[2,2,256,256]{3,2,1,0:T(8,128)} %shard_map.99, s32[]{:T(128)S(6)} %select_n.25, f32[2,2,128,256]{3,2,1,0:T(8,128)} %collective-permute-done.15), kind=kLoop, calls=%fused_computation.1 | loop fusion | flops 131072 | bytes 1572868 | tf_op jit(solution)/shard_map/dynamic_update_slice | solution.py:585
  134.2 11.0 %all-to-all-done.3 = f32[16,16,256]{2,1,0:T(8,128)S(1)} async-done(((f32[16,16,256]{2,1,0:T(8,128)}), f32[16,16,256]{2,1,0:T(8,128)S(1)}, u32[]{:S(2)}, u32[]{:S(2)}) %all-to-all-start.3) | async-done | bytes 262176 | tf_op jit(solution)/shard_map/all_to_all | solution.py:529
  (58 shorter events, 7.3 us)
Async XLA Ops:
  0.6 1.2 copy-start.10
  0.6 2.1 %copy-start = (f32[2,2,256,256]{3,2,1,0:T(8,128)S(1)}, f32[2,2,256,256]{3,2,1,0:T(8,128)}, u32[]{:S(2)}) copy-start(f32[2,2,256,256]{3,2,1,0:T(8,128)} %mid.5) | copy-start | bytes 3145732
  2.8 42.3 %copy-start.6 = (s32[3]{0:T(128)}, s32[3]{0:T(128)S(1)}, u32[]{:S(2)}) copy-start(s32[3]{0:T(128)S(1)} %pad_add_fusion.where) | copy-start | bytes 40
  3.5 14.4 %all-to-all-start = ((f32[4,144,256]{2,1,0:T(8,128)}), f32[4,144,256]{2,1,0:T(8,128)}, u32[]{:S(2)}, u32[]{:S(2)}) async-start(f32[4,144,256]{2,1,0:T(8,128)} %pad_maximum_fusion), calls=%async_computation | async-start | bytes 1179648 | tf_op jit(solution)/shard_map/all_to_all | solution.py:529
  8.5 26.3 %collective-permute-start.3 = (f32[2,2,128,256]{3,2,1,0:T(8,128)S(1)}, f32[2,2,128,256]{3,2,1,0:T(8,128)S(1)}, u32[]{:S(2)}, u32[]{:S(2)}) collective-permute-start(f32[2,2,128,256]{3,2,1,0:T(8,128)S(1)} %get-tuple-element.20), channel_id=1, source_target_pairs={{0,16},{16,0},{1,17},{17,1},{2,18},{18,2},{3,19},{19,3},{4,20},{20... | collective-permute-start | bytes 1572872 | tf_op jit(solution)/shard_map/ppermute | solution.py:537
  9.7 25.0 %collective-permute-start.4 = (f32[2,2,128,256]{3,2,1,0:T(8,128)S(1)}, f32[2,2,128,256]{3,2,1,0:T(8,128)S(1)}, u32[]{:S(2)}, u32[]{:S(2)}) collective-permute-start(f32[2,2,128,256]{3,2,1,0:T(8,128)S(1)} %get-tuple-element.21), channel_id=1, source_target_pairs={{16,32},{48,64},{80,96},{32,16},{64,48},{96,80},{17,33},{49,65},{8... | collective-permute-start | bytes 1572872 | tf_op jit(solution)/shard_map/ppermute | solution.py:537
  18.7 4.3 %collective-permute-start.2 = (f32[64,256]{1,0:T(8,128)S(1)}, f32[64,256]{1,0:T(8,128)S(1)}, u32[]{:S(2)}, u32[]{:S(2)}) collective-permute-start(f32[64,256]{1,0:T(8,128)S(1)} %bitcast.31), channel_id=1, source_target_pairs={{24,0},{0,8},{8,16},{16,24},{25,1},{1,9},{9,17},{17,25},{26,2},{2,... | collective-permute-start | bytes 196616 | tf_op jit(solution)/shard_map/ppermute | solution.py:562
  21.4 13.3 %collective-permute-start.1 = (f32[64,256]{1,0:T(8,128)S(1)}, f32[64,256]{1,0:T(8,128)S(1)}, u32[]{:S(2)}, u32[]{:S(2)}) collective-permute-start(f32[64,256]{1,0:T(8,128)S(1)} %bitcast.32), channel_id=1, source_target_pairs={{16,0},{24,8},{0,16},{8,24},{17,1},{25,9},{1,17},{9,25},{18,2},{26... | collective-permute-start | bytes 196616 | tf_op jit(solution)/shard_map/ppermute | solution.py:562
  21.8 12.9 %collective-permute-start = (f32[64,256]{1,0:T(8,128)S(1)}, f32[64,256]{1,0:T(8,128)S(1)}, u32[]{:S(2)}, u32[]{:S(2)}) collective-permute-start(f32[64,256]{1,0:T(8,128)S(1)} %bitcast.33), channel_id=1, source_target_pairs={{8,0},{16,8},{24,16},{0,24},{9,1},{17,9},{25,17},{1,25},{10,2},{18... | collective-permute-start | bytes 196616 | tf_op jit(solution)/shard_map/ppermute | solution.py:562
  34.7 10.4 %copy-start.2 = (f32[2,2,128,256]{3,2,1,0:T(8,128)}, f32[2,2,128,256]{3,2,1,0:T(8,128)S(1)}, u32[]{:S(2)}) copy-start(f32[2,2,128,256]{3,2,1,0:T(8,128)S(1)} %collective-permute-done.3.row_near) | copy-start | bytes 1572868
  34.8 10.4 %copy-start.3 = (f32[2,2,128,256]{3,2,1,0:T(8,128)}, f32[2,2,128,256]{3,2,1,0:T(8,128)S(1)}, u32[]{:S(2)}) copy-start(f32[2,2,128,256]{3,2,1,0:T(8,128)S(1)} %collective-permute-done.4.row_far) | copy-start | bytes 1572868
  35.9 19.9 %all-to-all-start.1 = ((f32[4,256,256]{2,1,0:T(8,128)}), f32[4,256,256]{2,1,0:T(8,128)}, u32[]{:S(2)}, u32[]{:S(2)}) async-start(f32[4,256,256]{2,1,0:T(8,128)} %broadcast_in_dim.15), calls=%async_computation.1 | async-start | bytes 2097152 | tf_op jit(solution)/shard_map/all_to_all | solution.py:529
  45.1 7.3 %collective-permute-start.5 = (f32[4,2,2,16,256]{4,3,2,1,0:T(8,128)S(1)}, f32[4,2,2,16,256]{4,3,2,1,0:T(8,128)S(1)}, u32[]{:S(2)}, u32[]{:S(2)}) collective-permute-start(f32[4,2,2,16,256]{4,3,2,1,0:T(8,128)S(1)} %dynamic-slice_bitcast_fusion), channel_id=1, source_target_pairs={{0,8},{8,0},{1,9},{9,1},{2,10},{10,2},{3,11},{11,3},{4,12},{12,4},... | collective-permute-start | bytes 786440 | tf_op jit(solution)/shard_map/ppermute | solution.py:558
  46.8 15.4 %collective-permute-start.9 = (f32[2,2,512,128]{3,2,1,0:T(8,128)}, f32[2,2,512,128]{3,2,1,0:T(8,128)S(1)}, u32[]{:S(2)}, u32[]{:S(2)}) collective-permute-start(f32[2,2,512,128]{3,2,1,0:T(8,128)} %get-tuple-element.25), channel_id=1, source_target_pairs={{0,1},{1,0},{2,3},{3,2},{4,5},{5,4},{6,7},{7,6},{8,9},{9,8},{10,11... | collective-permute-start | bytes 3145736 | tf_op jit(solution)/shard_map/ppermute | solution.py:541
  49.2 16.1 %collective-permute-start.10 = (f32[2,2,512,128]{3,2,1,0:T(8,128)S(1)}, f32[2,2,512,128]{3,2,1,0:T(8,128)S(1)}, u32[]{:S(2)}, u32[]{:S(2)}) collective-permute-start(f32[2,2,512,128]{3,2,1,0:T(8,128)S(1)} %get-tuple-element.26), channel_id=1, source_target_pairs={{1,2},{3,4},{5,6},{7,8},{9,10},{11,12},{13,14},{2,1},{4,3},{6,5},{... | collective-permute-start | bytes 3145736 | tf_op jit(solution)/shard_map/ppermute | solution.py:541
  52.4 8.0 %copy-start.9 = (f32[4,2,2,16,256]{4,3,2,1,0:T(8,128)}, f32[4,2,2,16,256]{4,3,2,1,0:T(8,128)S(1)}, u32[]{:S(2)}) copy-start(f32[4,2,2,16,256]{4,3,2,1,0:T(8,128)S(1)} %collective-permute-done.5.meas_far) | copy-start | bytes 786436
  55.8 9.5 %collective-permute-start.6 = (f32[4,4,4,16,256]{4,3,2,1,0:T(8,128)}, f32[4,4,4,16,256]{4,3,2,1,0:T(8,128)}, u32[]{:S(2)}, u32[]{:S(2)}) collective-permute-start(f32[4,4,4,16,256]{4,3,2,1,0:T(8,128)} %bitcast.13.mine), channel_id=1, source_target_pairs={{0,1},{1,0},{2,3},{3,2},{4,5},{5,4},{6,7},{7,6},{8,9},{9,8},{10,11... | collective-permute-start | bytes 3145736 | tf_op jit(solution)/shard_map/ppermute | solution.py:569
  60.3 1.6 %collective-permute-start.7 = (f32[4,2,16,256]{3,2,1,0:T(8,128)S(1)}, f32[4,2,16,256]{3,2,1,0:T(8,128)S(1)}, u32[]{:S(2)}, u32[]{:S(2)}) collective-permute-start(f32[4,2,16,256]{3,2,1,0:T(8,128)S(1)} %dynamic-slice_bitcast_fusion.2), channel_id=1, source_target_pairs={{0,1},{1,0},{2,3},{3,2},{4,5},{5,4},{6,7},{7,6},{8,9},{9,8},{10,11... | collective-permute-start | bytes 393224 | tf_op jit(solution)/shard_map/ppermute | solution.py:559
  60.5 1.7 %collective-permute-start.8 = (f32[4,2,16,256]{3,2,1,0:T(8,128)S(1)}, f32[4,2,16,256]{3,2,1,0:T(8,128)S(1)}, u32[]{:S(2)}, u32[]{:S(2)}) collective-permute-start(f32[4,2,16,256]{3,2,1,0:T(8,128)S(1)} %dynamic-slice_bitcast_fusion.1), channel_id=1, source_target_pairs={{0,1},{1,0},{2,3},{3,2},{4,5},{5,4},{6,7},{7,6},{8,9},{9,8},{10,11... | collective-permute-start | bytes 393224 | tf_op jit(solution)/shard_map/ppermute | solution.py:560
  61.9 3.5 %copy-start.13 = (f32[4,2,16,256]{3,2,1,0:T(8,128)}, f32[4,2,16,256]{3,2,1,0:T(8,128)S(1)}, u32[]{:S(2)}) copy-start(f32[4,2,16,256]{3,2,1,0:T(8,128)S(1)} %collective-permute-done.7.meas_core) | copy-start | bytes 393220
  62.2 3.2 %copy-start.14 = (f32[4,2,16,256]{3,2,1,0:T(8,128)}, f32[4,2,16,256]{3,2,1,0:T(8,128)S(1)}, u32[]{:S(2)}) copy-start(f32[4,2,16,256]{3,2,1,0:T(8,128)S(1)} %collective-permute-done.8.meas_far_core) | copy-start | bytes 393220
  62.2 3.2 %copy-start.11 = (f32[2,2,512,128]{3,2,1,0:T(8,128)}, f32[2,2,512,128]{3,2,1,0:T(8,128)S(1)}, u32[]{:S(2)}) copy-start(f32[2,2,512,128]{3,2,1,0:T(8,128)S(1)} %collective-permute-done.9.col_near) | copy-start | bytes 3145732
  91.5 3.9 %collective-permute-start.11 = (f32[4,4,4,16,256]{4,3,2,1,0:T(8,128)}, f32[4,4,4,16,256]{4,3,2,1,0:T(8,128)S(1)}, u32[]{:S(2)}, u32[]{:S(2)}) collective-permute-start(f32[4,4,4,16,256]{4,3,2,1,0:T(8,128)} %get-tuple-element.29), channel_id=1, source_target_pairs={{0,1},{1,0},{2,3},{3,2},{4,5},{5,4},{6,7},{7,6},{8,9},{9,8},{10,11... | collective-permute-start | bytes 3145736 | tf_op jit(solution)/shard_map/ppermute | solution.py:574
  91.6 10.9 %collective-permute-start.12 = (f32[2,2,512,128]{3,2,1,0:T(8,128)}, f32[2,2,512,128]{3,2,1,0:T(8,128)S(1)}, u32[]{:S(2)}, u32[]{:S(2)}) collective-permute-start(f32[2,2,512,128]{3,2,1,0:T(8,128)} %get-tuple-element.32), channel_id=1, source_target_pairs={{0,1},{1,0},{2,3},{3,2},{4,5},{5,4},{6,7},{7,6},{8,9},{9,8},{10,11... | collective-permute-start | bytes 3145736 | tf_op jit(solution)/shard_map/ppermute | solution.py:541
  92.1 16.7 %collective-permute-start.13 = (f32[2,2,512,128]{3,2,1,0:T(8,128)}, f32[2,2,512,128]{3,2,1,0:T(8,128)S(1)}, u32[]{:S(2)}, u32[]{:S(2)}) collective-permute-start(f32[2,2,512,128]{3,2,1,0:T(8,128)} %get-tuple-element.33), channel_id=1, source_target_pairs={{1,2},{3,4},{5,6},{7,8},{9,10},{11,12},{13,14},{2,1},{4,3},{6,5},{... | collective-permute-start | bytes 3145736 | tf_op jit(solution)/shard_map/ppermute | solution.py:541
  97.8 11.0 %copy-start.4 = (f32[2,2,128,256]{3,2,1,0:T(8,128)S(1)}, f32[2,2,128,256]{3,2,1,0:T(8,128)}, u32[]{:S(2)}) copy-start(f32[2,2,128,256]{3,2,1,0:T(8,128)} %get-tuple-element.30.row_near) | copy-start | bytes 1572868
  97.8 11.0 %copy-start.5 = (f32[2,2,128,256]{3,2,1,0:T(8,128)S(1)}, f32[2,2,128,256]{3,2,1,0:T(8,128)}, u32[]{:S(2)}) copy-start(f32[2,2,128,256]{3,2,1,0:T(8,128)} %get-tuple-element.31.row_far) | copy-start | bytes 1572868
  97.8 22.6 %all-to-all-start.2 = ((f32[4,256,256]{2,1,0:T(8,128)}), f32[4,256,256]{2,1,0:T(8,128)}, u32[]{:S(2)}, u32[]{:S(2)}) async-start(f32[4,256,256]{2,1,0:T(8,128)} %bitcast.24), calls=%async_computation.2 | async-start | bytes 2097152 | tf_op jit(solution)/shard_map/all_to_all | solution.py:529
  111.4 18.1 %copy-start.1 = (f32[2,2,256,256]{3,2,1,0:T(8,128)S(1)}, f32[2,2,256,256]{3,2,1,0:T(8,128)}, u32[]{:S(2)}) copy-start(f32[2,2,256,256]{3,2,1,0:T(8,128)} %get-tuple-element.37.mid) | copy-start | bytes 3145732
  111.4 18.0 %collective-permute-start.14 = (f32[2,2,128,256]{3,2,1,0:T(8,128)}, f32[2,2,128,256]{3,2,1,0:T(8,128)}, u32[]{:S(2)}, u32[]{:S(2)}) collective-permute-start(f32[2,2,128,256]{3,2,1,0:T(8,128)} %get-tuple-element.34), channel_id=1, source_target_pairs={{0,16},{16,0},{1,17},{17,1},{2,18},{18,2},{3,19},{19,3},{4,20},{20... | collective-permute-start | bytes 1572872 | tf_op jit(solution)/shard_map/ppermute | solution.py:537
  111.9 20.3 %collective-permute-start.15 = (f32[2,2,128,256]{3,2,1,0:T(8,128)}, f32[2,2,128,256]{3,2,1,0:T(8,128)}, u32[]{:S(2)}, u32[]{:S(2)}) collective-permute-start(f32[2,2,128,256]{3,2,1,0:T(8,128)} %get-tuple-element.35), channel_id=1, source_target_pairs={{16,32},{48,64},{80,96},{32,16},{64,48},{96,80},{17,33},{49,65},{8... | collective-permute-start | bytes 1572872 | tf_op jit(solution)/shard_map/ppermute | solution.py:537
  122.4 22.8 %all-to-all-start.3 = ((f32[16,16,256]{2,1,0:T(8,128)}), f32[16,16,256]{2,1,0:T(8,128)S(1)}, u32[]{:S(2)}, u32[]{:S(2)}) async-start(f32[16,16,256]{2,1,0:T(8,128)} %bitcast.19), calls=%async_computation.3 | async-start | bytes 524288 | tf_op jit(solution)/shard_map/all_to_all | solution.py:529
  (3 other events, 2.5 us)

commit v5 on v4

--- a/solution.py
+++ b/solution.py
@@ -171,6 +171,7 @@
         out_specs=[tall, tall],
         out_shape=[struct(2, 2, 2 * W, H)] * 2,
         compiler_params=params(),
+        cost_estimate=cost(40),
     )(where, mid, row_near, row_far)
 
 
@@ -359,10 +360,10 @@
         ref[(*index, part)] = value[part]
 
 
-def add_to(ref, value, first, *index):
+def add_to(ref, value, *index):
     for part in range(2):
         at = (*index, part)
-        ref[at] = jnp.where(first, value[part], ref[at] + value[part])
+        ref[at] += value[part]
 
 
 def forward_step(tabs, probe, win, u, far, intensity, m):
@@ -375,7 +376,7 @@
     for s in slots:
         write(far, fields[s], m, s)
         power = fields[s][0] * fields[s][0] + fields[s][1] * fields[s][1]
-        intensity[s] = jnp.where(m == 0, power, intensity[s] + power)
+        intensity[s] += power
 
 
 def backward_step(tabs, probe, win, u, far, scale, grad_probe, grad_win, m, between):
@@ -383,12 +384,12 @@
     fields = [tuple(scale[s] * part for part in read(far, m, s)) for s in slots]
     fields = dft_adjoint(tabs, fields)
     for s in slots:
-        add_to(grad_win, times_conj(fields[s], read(u, m, s)), m == 0, s, 1)
+        add_to(grad_win, times_conj(fields[s], read(u, m, s)), s, 1)
     between()
     fields = propagate(tabs, [times_conj(fields[s], read(win, s, 1)) for s in slots], True)
     here = read(probe, m)
     for s in slots:
-        add_to(grad_win, times_conj(fields[s], here), m == 0, s, 0)
+        add_to(grad_win, times_conj(fields[s], here), s, 0)
     terms = [times_conj(fields[s], read(win, s, 0)) for s in slots]
     write(grad_probe, tuple(a + b for a, b in zip(*terms)))
 
@@ -414,6 +415,8 @@
     for m in range(MODES):
         for copy in probe_copies(m):
             copy.start()
+    scale[...] = jnp.zeros_like(scale)
+    grad_win[...] = jnp.zeros_like(grad_win)
     wait_all(meas_copies)
     for s in range(SLOTS):
         for i, half in ((0, h), (1, 1 - h)):
@@ -437,7 +440,7 @@
         forward_step(tabs, probe, win, u, far, scale, m)
         return 0
 
-    lax.fori_loop(0, MODES, forward, 0)
+    lax.fori_loop(0, MODES, forward, 0, unroll=2)
     for s in range(SLOTS):
         weight = jnp.where(s < counts[0, 0], 2.0 * loss_scale, 0.0)
         scale[s] = weight * (1.0 - pattern[s] * lax.rsqrt(scale[s] + amp_floor))
@@ -462,7 +465,7 @@
         return start_all([(b.at[j], a.at[j]) for a, b in pairs], out_sems.at[j])
 
     copies = []
-    lax.fori_loop(0, MODES - 1, lambda m, _: backward(m, lambda: None), 0)
+    lax.fori_loop(0, MODES - 1, lambda m, _: backward(m, lambda: None), 0, unroll=3)
     backward(MODES - 1, lambda: copies.extend(place_slice(1)))
     copies += place_slice(0)
     for m in range(MODES):
@@ -576,8 +579,14 @@
     mine = exchange(mine.reshape(4, 256, W), "z")
     near, far = rims(where, row_near, row_far, col_near, col_far)
     row_near, row_far = swap_rows(near, far)
-    mine = jnp.sum(after(mine, near, far), 0).reshape(16, 16, W)
-    probe_grad = jnp.sum(exchange(mine, PLANE), 0)
+    mine = jnp.sum(after(mine, near, far), 0).reshape(4, 4, 16, W).swapaxes(0, 1)
+    total = jnp.sum(exchange(mine, "y"), 0)
+    x = 2 * where[2] + h
+    parts = [
+        lax.ppermute(pick(total, (x + k) % 4, 0), ("xl", "xh"), [(i, (i + k) % 4) for i in range(4)])
+        for k in range(1, 4)
+    ]
+    probe_grad = pick(total, x, 0) + parts[0] + parts[1] + parts[2]
     mid = after(mid, mine)
     held = combine_near(where, mid, col_near, col_far, row_near)
     corner_at = (0, 0, where[2] * H, 0)

time: 147 us -> 143 us (0.973)
  the two profiles are of different devices: /device:TPU:1 before, /device:TPU:32 now
where the time goes in v5:
time: 143 us; the launch traced here: 142 us
  starting transfers between devices  50.9 us (36%)
  waiting for transfers between devices  40.6 us (28%)
  Pallas kernels  30.4 us (21%)
  local copies, waits for them, and re-layouts  10.9 us (8%)
  other arithmetic  7.38 us (5%)
  between operations  1.55 us (1%)
    all_to_all x4, waiting for transfers between devices, exchange(): return lax.all_to_all(x, axes, split_axis=0, concat_axis=0, tiled=True)  24.7 us
    pallas_call x1, Pallas kernels, gradients(): pl.pallas_call(functools.partial(main_kernel, loss_scale), in_specs=[SMEM...  24.5 us
    all_to_all x4, starting transfers between devices, exchange(): return lax.all_to_all(x, axes, split_axis=0, concat_axis=0, tiled=True)  20.1 us
    ppermute x3, waiting for transfers between devices, body(): lax.ppermute(probe_rows, ('xl', 'xh'), [((i + k) % 4, i) for i in range(4)])  10.4 us
    ppermute x4, starting transfers between devices, swap_rows(): return (lax.ppermute(near, 'xl', SWAP), lax.ppermute(far, TY, far_pairs(8)))  7.04 us
    ppermute x3, starting transfers between devices, body(): lax.ppermute(pick(total, (x + k) % 4, 0), ('xl', 'xh'), [(i, (i + k) % 4)...  5.89 us
    ppermute x4, starting transfers between devices, swap_columns(): return (lax.ppermute(near, 'c', SWAP), lax.ppermute(far, TX, far_pairs(16)))  4.95 us
    ppermute x3, starting transfers between devices, body(): lax.ppermute(probe_rows, ('xl', 'xh'), [((i + k) % 4, i) for i in range(4)])  4.73 us
  transfers between devices with their start and end apart: 23, of which 10 were waited for; matrix products, arithmetic and copies ran while one was open for 8% of the time, Pallas kernels for 4%

profile of v5, /device:TPU:32, one launch (start us, length us, event | category | flops | bytes accessed | tf_op | source)
XLA Modules:
  0.0 141.7 jit_solution(5999189768498649165)
XLA Ops:
  0.6 1.2 copy.12
  3.6 4.5 %all-to-all-start = ((f32[4,144,256]{2,1,0:T(8,128)}), f32[4,144,256]{2,1,0:T(8,128)}, u32[]{:S(2)}, u32[]{:S(2)}) async-start(f32[4,144,256]{2,1,0:T(8,128)} %pad_maximum_fusion), calls=%async_computation | async-start | bytes 1179648 | tf_op jit(solution)/shard_map/all_to_all | solution.py:532
  8.1 1.5 %collective-permute-start.3 = (f32[2,2,128,256]{3,2,1,0:T(8,128)S(1)}, f32[2,2,128,256]{3,2,1,0:T(8,128)S(1)}, u32[]{:S(2)}, u32[]{:S(2)}) collective-permute-start(f32[2,2,128,256]{3,2,1,0:T(8,128)S(1)} %get-tuple-element.20), channel_id=1, source_target_pairs={{0,16},{16,0},{1,17},{17,1},{2,18},{18,2},{3,19},{19,3},{4,20},{20... | collective-permute-start | bytes 1572872 | tf_op jit(solution)/shard_map/ppermute | solution.py:540
  9.6 2.0 %collective-permute-start.4 = (f32[2,2,128,256]{3,2,1,0:T(8,128)S(1)}, f32[2,2,128,256]{3,2,1,0:T(8,128)S(1)}, u32[]{:S(2)}, u32[]{:S(2)}) collective-permute-start(f32[2,2,128,256]{3,2,1,0:T(8,128)S(1)} %get-tuple-element.21), channel_id=1, source_target_pairs={{16,32},{48,64},{80,96},{32,16},{64,48},{96,80},{17,33},{49,65},{8... | collective-permute-start | bytes 1572872 | tf_op jit(solution)/shard_map/ppermute | solution.py:540
  11.5 6.8 %all-to-all-done = f32[4,144,256]{2,1,0:T(8,128)} async-done(((f32[4,144,256]{2,1,0:T(8,128)}), f32[4,144,256]{2,1,0:T(8,128)}, u32[]{:S(2)}, u32[]{:S(2)}) %all-to-all-start) | async-done | bytes 589856 | tf_op jit(solution)/shard_map/all_to_all | solution.py:532
  19.2 1.5 %collective-permute-start.1 = (f32[64,256]{1,0:T(8,128)S(1)}, f32[64,256]{1,0:T(8,128)S(1)}, u32[]{:S(2)}, u32[]{:S(2)}) collective-permute-start(f32[64,256]{1,0:T(8,128)S(1)} %bitcast.46), channel_id=1, source_target_pairs={{16,0},{24,8},{0,16},{8,24},{17,1},{25,9},{1,17},{9,25},{18,2},{26... | collective-permute-start | bytes 196616 | tf_op jit(solution)/shard_map/ppermute | solution.py:565
  20.7 2.7 %collective-permute-start.2 = (f32[64,256]{1,0:T(8,128)S(1)}, f32[64,256]{1,0:T(8,128)S(1)}, u32[]{:S(2)}, u32[]{:S(2)}) collective-permute-start(f32[64,256]{1,0:T(8,128)S(1)} %bitcast.47), channel_id=1, source_target_pairs={{24,0},{0,8},{8,16},{16,24},{25,1},{1,9},{9,17},{17,25},{26,2},{2,... | collective-permute-start | bytes 196616 | tf_op jit(solution)/shard_map/ppermute | solution.py:565
  23.9 1.1 slice.9
  25.1 9.8 %collective-permute-done.1 = f32[64,256]{1,0:T(8,128)S(1)} collective-permute-done((f32[64,256]{1,0:T(8,128)S(1)}, f32[64,256]{1,0:T(8,128)S(1)}, u32[]{:S(2)}, u32[]{:S(2)}) %collective-permute-start.1) | collective-permute-done | bytes 65568 | tf_op jit(solution)/shard_map/ppermute | solution.py:565
  34.8 3.0 %collective-permute-start.5 = (f32[4,2,2,16,256]{4,3,2,1,0:T(8,128)S(1)}, f32[4,2,2,16,256]{4,3,2,1,0:T(8,128)}, u32[]{:S(2)}, u32[]{:S(2)}) collective-permute-start(f32[4,2,2,16,256]{4,3,2,1,0:T(8,128)S(1)} %dynamic-slice_bitcast_fusion), channel_id=1, source_target_pairs={{0,8},{8,0},{1,9},{9,1},{2,10},{10,2},{3,11},{11,3},{4,12},{12,4},... | collective-permute-start | bytes 786440 | tf_op jit(solution)/shard_map/ppermute | solution.py:561
  38.6 1.2 broadcast_in_dim.15
  39.9 6.1 %all-to-all-start.1 = ((f32[4,256,256]{2,1,0:T(8,128)}), f32[4,256,256]{2,1,0:T(8,128)}, u32[]{:S(2)}, u32[]{:S(2)}) async-start(f32[4,256,256]{2,1,0:T(8,128)} %broadcast_in_dim.15), calls=%async_computation.1 | async-start | bytes 2097152 | tf_op jit(solution)/shard_map/all_to_all | solution.py:532
  46.0 1.0 copy-done.7
  47.0 1.0 copy-done.9
  49.5 3.4 %collective-permute-start.9 = (f32[2,2,512,128]{3,2,1,0:T(8,128)S(1)}, f32[2,2,512,128]{3,2,1,0:T(8,128)}, u32[]{:S(2)}, u32[]{:S(2)}) collective-permute-start(f32[2,2,512,128]{3,2,1,0:T(8,128)S(1)} %get-tuple-element.25), channel_id=1, source_target_pairs={{0,1},{1,0},{2,3},{3,2},{4,5},{5,4},{6,7},{7,6},{8,9},{9,8},{10,11... | collective-permute-start | bytes 3145736 | tf_op jit(solution)/shard_map/ppermute | solution.py:544
  53.0 4.2 %all-to-all-done.1 = f32[4,256,256]{2,1,0:T(8,128)} async-done(((f32[4,256,256]{2,1,0:T(8,128)}), f32[4,256,256]{2,1,0:T(8,128)}, u32[]{:S(2)}, u32[]{:S(2)}) %all-to-all-start.1) | async-done | bytes 1048608 | tf_op jit(solution)/shard_map/all_to_all | solution.py:532
  62.0 24.5 %shard_map.97 = (f32[4,4,4,16,256]{4,3,2,1,0:T(8,128)}, f32[4,4,4,16,256]{4,3,2,1,0:T(8,128)}, f32[2,2,256,256]{3,2,1,0:T(8,128)}, f32[2,2,128,256]{3,2,1,0:T(8,...) custom-call(s32[3]{0:T(128)} %copy-done.4, s32[2,2]{1,0:T(2,128)} %bitcast.53, ...), custom_call_target="tpu_custom_call" | custom-call | flops 38400000000 | bytes 1048576 | tf_op jit(solution)/shard_map/pallas_call | solution.py:477
  86.5 4.4 %collective-permute-start.11 = (f32[4,4,4,16,256]{4,3,2,1,0:T(8,128)}, f32[4,4,4,16,256]{4,3,2,1,0:T(8,128)S(1)}, u32[]{:S(2)}, u32[]{:S(2)}) collective-permute-start(f32[4,4,4,16,256]{4,3,2,1,0:T(8,128)} %get-tuple-element.29), channel_id=1, source_target_pairs={{0,1},{1,0},{2,3},{3,2},{4,5},{5,4},{6,7},{7,6},{8,9},{9,8},{10,11... | collective-permute-start | bytes 3145736 | tf_op jit(solution)/shard_map/ppermute | solution.py:577
  91.7 1.7 %collective-permute-done.11 = f32[4,4,4,16,256]{4,3,2,1,0:T(8,128)S(1)} collective-permute-done((f32[4,4,4,16,256]{4,3,2,1,0:T(8,128)}, f32[4,4,4,16,256]{4,3,2,1,0:T(8,128)S(1)}, u32[]{:S(2)}, u32[]{:S(2)}) %collective-permute-start.11) | collective-permute-done | bytes 1048608 | tf_op jit(solution)/shard_map/ppermute | solution.py:577
  93.4 2.4 %add.77 = f32[4,4,4,16,256]{4,3,2,1,0:T(8,128)} add(f32[4,4,4,16,256]{4,3,2,1,0:T(8,128)} %get-tuple-element.28, f32[4,4,4,16,256]{4,3,2,1,0:T(8,128)S(1)} %collective-permute-done.11) | non-fusion elementwise | flops 262144 | bytes 3145728 | tf_op jit(solution)/shard_map/add | solution.py:577
  95.8 4.9 %all-to-all-start.2 = ((f32[4,256,256]{2,1,0:T(8,128)}), f32[4,256,256]{2,1,0:T(8,128)}, u32[]{:S(2)}, u32[]{:S(2)}) async-start(f32[4,256,256]{2,1,0:T(8,128)} %bitcast.38), calls=%async_computation.2 | async-start | bytes 2097152 | tf_op jit(solution)/shard_map/all_to_all | solution.py:532
  101.4 1.8 %shard_map.98 = (f32[2,2,128,256]{3,2,1,0:T(8,128)}, f32[2,2,128,256]{3,2,1,0:T(8,128)}) custom-call(s32[3]{0:T(128)S(1)} %copy-done.5, f32[2,2,128,256]{3,2,1,0:T(8,128)S(1)} %copy-done.2, f32[2,2,128,256]{3,2,1,0:T(8,128)S(1)} %copy-done.3, f32[2,2,512,128]{3,2,1,0:T(8,128)S(1)} %collective-permute-done.12.col_near, ...), custom_call_target="tpu_custom_call" | custom-call | tf_op jit(solution)/shard_map/pallas_call | solution.py:214
  103.4 3.5 %collective-permute-start.15 = (f32[2,2,128,256]{3,2,1,0:T(8,128)}, f32[2,2,128,256]{3,2,1,0:T(8,128)}, u32[]{:S(2)}, u32[]{:S(2)}) collective-permute-start(f32[2,2,128,256]{3,2,1,0:T(8,128)} %get-tuple-element.35), channel_id=1, source_target_pairs={{16,32},{48,64},{80,96},{32,16},{64,48},{96,80},{17,33},{49,65},{8... | collective-permute-start | bytes 1572872 | tf_op jit(solution)/shard_map/ppermute | solution.py:540
  106.8 8.7 %all-to-all-done.2 = f32[4,256,256]{2,1,0:T(8,128)} async-done(((f32[4,256,256]{2,1,0:T(8,128)}), f32[4,256,256]{2,1,0:T(8,128)}, u32[]{:S(2)}, u32[]{:S(2)}) %all-to-all-start.2) | async-done | bytes 1048608 | tf_op jit(solution)/shard_map/all_to_all | solution.py:532
  115.6 1.3 reduce_sum.18
  117.6 4.7 %all-to-all-start.3 = ((f32[4,4,16,256]{3,2,1,0:T(8,128)}), f32[4,4,16,256]{3,2,1,0:T(8,128)S(1)}, u32[]{:S(2)}, u32[]{:S(2)}) async-start(f32[4,4,16,256]{3,2,1,0:T(8,128)} %copy.13), calls=%async_computation.3 | async-start | bytes 524288 | tf_op jit(solution)/shard_map/all_to_all | solution.py:532
  122.3 2.7 %shard_map.99 = f32[2,2,256,256]{3,2,1,0:T(8,128)} custom-call(s32[3]{0:T(128)S(1)} %copy-done.5, f32[2,2,256,256]{3,2,1,0:T(8,128)S(1)} %copy-done, f32[2,2,512,128]{3,2,1,0:T(8,128)S(1)} %collective-permute-done.12.col_near, f32[2,2,512,128]{3,2,1,0:T(8,128)S(1)} %collective-permute-done.13.col_far, f32[2,2,128,256]{3,2,1,0:T(8,128)} %collective-permute-done.14.row_near), custom_call_target="tpu_custom_call" | custom-call | tf_op jit(solution)/shard_map/pallas_call | solution.py:251
  125.0 4.9 %all-to-all-done.3 = f32[4,4,16,256]{3,2,1,0:T(8,128)S(1)} async-done(((f32[4,4,16,256]{3,2,1,0:T(8,128)}), f32[4,4,16,256]{3,2,1,0:T(8,128)S(1)}, u32[]{:S(2)}, u32[]{:S(2)}) %all-to-all-start.3) | async-done | bytes 262176 | tf_op jit(solution)/shard_map/all_to_all | solution.py:532
  130.0 4.7 %collective-permute-start.16 = (f32[16,256]{1,0:T(8,128)S(1)}, f32[16,256]{1,0:T(8,128)S(1)}, u32[]{:S(2)}, u32[]{:S(2)}) collective-permute-start(f32[16,256]{1,0:T(8,128)S(1)} %get-tuple-element.38), channel_id=1, source_target_pairs={{0,8},{8,16},{16,24},{24,0},{1,9},{9,17},{17,25},{25,1},{2,10},{10... | collective-permute-start | bytes 49160 | tf_op jit(solution)/shard_map/ppermute | solution.py:586
  134.7 1.2 collective-permute-start.17
  135.9 2.1 %add_dynamic-update-slice_fusion = f32[2,2,256,256]{3,2,1,0:T(8,128)} fusion(f32[2,2,256,256]{3,2,1,0:T(8,128)} %shard_map.99, s32[]{:T(128)S(6)} %select_n.53, f32[2,2,128,256]{3,2,1,0:T(8,128)} %collective-permute-done.15), kind=kLoop, calls=%fused_computation.1 | loop fusion | flops 131072 | bytes 1572868 | tf_op jit(solution)/shard_map/dynamic_update_slice | solution.py:594
  138.4 2.7 %collective-permute-done.18 = f32[16,256]{1,0:T(8,128)S(1)} collective-permute-done((f32[16,256]{1,0:T(8,128)S(1)}, f32[16,256]{1,0:T(8,128)S(1)}, u32[]{:S(2)}, u32[]{:S(2)}) %collective-permute-start.18) | collective-permute-done | bytes 16416 | tf_op jit(solution)/shard_map/ppermute | solution.py:586
  (67 shorter events, 13.0 us)
Async XLA Ops:
  0.6 1.4 copy-start.1
  2.0 44.0 %copy-start.4 = (s32[3]{0:T(128)}, s32[3]{0:T(128)S(1)}, u32[]{:S(2)}) copy-start(s32[3]{0:T(128)S(1)} %pad_add_fusion.where) | copy-start | bytes 40
  3.6 14.7 %all-to-all-start = ((f32[4,144,256]{2,1,0:T(8,128)}), f32[4,144,256]{2,1,0:T(8,128)}, u32[]{:S(2)}, u32[]{:S(2)}) async-start(f32[4,144,256]{2,1,0:T(8,128)} %pad_maximum_fusion), calls=%async_computation | async-start | bytes 1179648 | tf_op jit(solution)/shard_map/all_to_all | solution.py:532
  8.1 30.4 %collective-permute-start.3 = (f32[2,2,128,256]{3,2,1,0:T(8,128)S(1)}, f32[2,2,128,256]{3,2,1,0:T(8,128)S(1)}, u32[]{:S(2)}, u32[]{:S(2)}) collective-permute-start(f32[2,2,128,256]{3,2,1,0:T(8,128)S(1)} %get-tuple-element.20), channel_id=1, source_target_pairs={{0,16},{16,0},{1,17},{17,1},{2,18},{18,2},{3,19},{19,3},{4,20},{20... | collective-permute-start | bytes 1572872 | tf_op jit(solution)/shard_map/ppermute | solution.py:540
  9.6 29.0 %collective-permute-start.4 = (f32[2,2,128,256]{3,2,1,0:T(8,128)S(1)}, f32[2,2,128,256]{3,2,1,0:T(8,128)S(1)}, u32[]{:S(2)}, u32[]{:S(2)}) collective-permute-start(f32[2,2,128,256]{3,2,1,0:T(8,128)S(1)} %get-tuple-element.21), channel_id=1, source_target_pairs={{16,32},{48,64},{80,96},{32,16},{64,48},{96,80},{17,33},{49,65},{8... | collective-permute-start | bytes 1572872 | tf_op jit(solution)/shard_map/ppermute | solution.py:540
  19.2 15.6 %collective-permute-start.1 = (f32[64,256]{1,0:T(8,128)S(1)}, f32[64,256]{1,0:T(8,128)S(1)}, u32[]{:S(2)}, u32[]{:S(2)}) collective-permute-start(f32[64,256]{1,0:T(8,128)S(1)} %bitcast.46), channel_id=1, source_target_pairs={{16,0},{24,8},{0,16},{8,24},{17,1},{25,9},{1,17},{9,25},{18,2},{26... | collective-permute-start | bytes 196616 | tf_op jit(solution)/shard_map/ppermute | solution.py:565
  20.7 17.2 %collective-permute-start.2 = (f32[64,256]{1,0:T(8,128)S(1)}, f32[64,256]{1,0:T(8,128)S(1)}, u32[]{:S(2)}, u32[]{:S(2)}) collective-permute-start(f32[64,256]{1,0:T(8,128)S(1)} %bitcast.47), channel_id=1, source_target_pairs={{24,0},{0,8},{8,16},{16,24},{25,1},{1,9},{9,17},{17,25},{26,2},{2,... | collective-permute-start | bytes 196616 | tf_op jit(solution)/shard_map/ppermute | solution.py:565
  23.4 15.1 %collective-permute-start = (f32[64,256]{1,0:T(8,128)S(1)}, f32[64,256]{1,0:T(8,128)S(1)}, u32[]{:S(2)}, u32[]{:S(2)}) collective-permute-start(f32[64,256]{1,0:T(8,128)S(1)} %bitcast.48), channel_id=1, source_target_pairs={{8,0},{16,8},{24,16},{0,24},{9,1},{17,9},{25,17},{1,25},{10,2},{18... | collective-permute-start | bytes 196616 | tf_op jit(solution)/shard_map/ppermute | solution.py:565
  25.0 13.5 %copy-start.10 = (f32[4,128,256]{2,1,0:T(8,128)}, f32[4,128,256]{2,1,0:T(8,128)S(1)}, u32[]{:S(2)}) copy-start(f32[4,128,256]{2,1,0:T(8,128)S(1)} %slice.9) | copy-start | bytes 1572868
  34.8 18.1 %collective-permute-start.5 = (f32[4,2,2,16,256]{4,3,2,1,0:T(8,128)S(1)}, f32[4,2,2,16,256]{4,3,2,1,0:T(8,128)}, u32[]{:S(2)}, u32[]{:S(2)}) collective-permute-start(f32[4,2,2,16,256]{4,3,2,1,0:T(8,128)S(1)} %dynamic-slice_bitcast_fusion), channel_id=1, source_target_pairs={{0,8},{8,0},{1,9},{9,1},{2,10},{10,2},{3,11},{11,3},{4,12},{12,4},... | collective-permute-start | bytes 786440 | tf_op jit(solution)/shard_map/ppermute | solution.py:561
  38.5 1.2 copy-start.6
  38.5 1.4 copy-start.8
  39.9 17.3 %all-to-all-start.1 = ((f32[4,256,256]{2,1,0:T(8,128)}), f32[4,256,256]{2,1,0:T(8,128)}, u32[]{:S(2)}, u32[]{:S(2)}) async-start(f32[4,256,256]{2,1,0:T(8,128)} %broadcast_in_dim.15), calls=%async_computation.1 | async-start | bytes 2097152 | tf_op jit(solution)/shard_map/all_to_all | solution.py:532
  46.0 1.0 copy-start.7
  48.8 12.2 %collective-permute-start.10 = (f32[2,2,512,128]{3,2,1,0:T(8,128)S(1)}, f32[2,2,512,128]{3,2,1,0:T(8,128)S(1)}, u32[]{:S(2)}, u32[]{:S(2)}) collective-permute-start(f32[2,2,512,128]{3,2,1,0:T(8,128)S(1)} %get-tuple-element.26), channel_id=1, source_target_pairs={{1,2},{3,4},{5,6},{7,8},{9,10},{11,12},{13,14},{2,1},{4,3},{6,5},{... | collective-permute-start | bytes 3145736 | tf_op jit(solution)/shard_map/ppermute | solution.py:544
  49.5 11.5 %collective-permute-start.9 = (f32[2,2,512,128]{3,2,1,0:T(8,128)S(1)}, f32[2,2,512,128]{3,2,1,0:T(8,128)}, u32[]{:S(2)}, u32[]{:S(2)}) collective-permute-start(f32[2,2,512,128]{3,2,1,0:T(8,128)S(1)} %get-tuple-element.25), channel_id=1, source_target_pairs={{0,1},{1,0},{2,3},{3,2},{4,5},{5,4},{6,7},{7,6},{8,9},{9,8},{10,11... | collective-permute-start | bytes 3145736 | tf_op jit(solution)/shard_map/ppermute | solution.py:544
  57.2 3.9 %collective-permute-start.6 = (f32[4,4,4,16,256]{4,3,2,1,0:T(8,128)}, f32[4,4,4,16,256]{4,3,2,1,0:T(8,128)}, u32[]{:S(2)}, u32[]{:S(2)}) collective-permute-start(f32[4,4,4,16,256]{4,3,2,1,0:T(8,128)} %bitcast.13.mine), channel_id=1, source_target_pairs={{0,1},{1,0},{2,3},{3,2},{4,5},{5,4},{6,7},{7,6},{8,9},{9,8},{10,11... | collective-permute-start | bytes 3145736 | tf_op jit(solution)/shard_map/ppermute | solution.py:572
  58.1 2.3 %collective-permute-start.7 = (f32[4,2,16,256]{3,2,1,0:T(8,128)S(1)}, f32[4,2,16,256]{3,2,1,0:T(8,128)S(1)}, u32[]{:S(2)}, u32[]{:S(2)}) collective-permute-start(f32[4,2,16,256]{3,2,1,0:T(8,128)S(1)} %dynamic-slice_bitcast_fusion.2), channel_id=1, source_target_pairs={{0,1},{1,0},{2,3},{3,2},{4,5},{5,4},{6,7},{7,6},{8,9},{9,8},{10,11... | collective-permute-start | bytes 393224 | tf_op jit(solution)/shard_map/ppermute | solution.py:562
  59.6 1.4 %collective-permute-start.8 = (f32[4,2,16,256]{3,2,1,0:T(8,128)S(1)}, f32[4,2,16,256]{3,2,1,0:T(8,128)S(1)}, u32[]{:S(2)}, u32[]{:S(2)}) collective-permute-start(f32[4,2,16,256]{3,2,1,0:T(8,128)S(1)} %dynamic-slice_bitcast_fusion.1), channel_id=1, source_target_pairs={{0,1},{1,0},{2,3},{3,2},{4,5},{5,4},{6,7},{7,6},{8,9},{9,8},{10,11... | collective-permute-start | bytes 393224 | tf_op jit(solution)/shard_map/ppermute | solution.py:563
  86.5 6.9 %collective-permute-start.11 = (f32[4,4,4,16,256]{4,3,2,1,0:T(8,128)}, f32[4,4,4,16,256]{4,3,2,1,0:T(8,128)S(1)}, u32[]{:S(2)}, u32[]{:S(2)}) collective-permute-start(f32[4,4,4,16,256]{4,3,2,1,0:T(8,128)} %get-tuple-element.29), channel_id=1, source_target_pairs={{0,1},{1,0},{2,3},{3,2},{4,5},{5,4},{6,7},{7,6},{8,9},{9,8},{10,11... | collective-permute-start | bytes 3145736 | tf_op jit(solution)/shard_map/ppermute | solution.py:577
  90.9 9.8 %collective-permute-start.12 = (f32[2,2,512,128]{3,2,1,0:T(8,128)}, f32[2,2,512,128]{3,2,1,0:T(8,128)S(1)}, u32[]{:S(2)}, u32[]{:S(2)}) collective-permute-start(f32[2,2,512,128]{3,2,1,0:T(8,128)} %get-tuple-element.32), channel_id=1, source_target_pairs={{0,1},{1,0},{2,3},{3,2},{4,5},{5,4},{6,7},{7,6},{8,9},{9,8},{10,11... | collective-permute-start | bytes 3145736 | tf_op jit(solution)/shard_map/ppermute | solution.py:544
  91.0 9.8 %collective-permute-start.13 = (f32[2,2,512,128]{3,2,1,0:T(8,128)}, f32[2,2,512,128]{3,2,1,0:T(8,128)S(1)}, u32[]{:S(2)}, u32[]{:S(2)}) collective-permute-start(f32[2,2,512,128]{3,2,1,0:T(8,128)} %get-tuple-element.33), channel_id=1, source_target_pairs={{1,2},{3,4},{5,6},{7,8},{9,10},{11,12},{13,14},{2,1},{4,3},{6,5},{... | collective-permute-start | bytes 3145736 | tf_op jit(solution)/shard_map/ppermute | solution.py:544
  95.8 5.0 %copy-start.2 = (f32[2,2,128,256]{3,2,1,0:T(8,128)S(1)}, f32[2,2,128,256]{3,2,1,0:T(8,128)}, u32[]{:S(2)}) copy-start(f32[2,2,128,256]{3,2,1,0:T(8,128)} %get-tuple-element.30.row_near) | copy-start | bytes 1572868
  95.8 5.0 %copy-start.3 = (f32[2,2,128,256]{3,2,1,0:T(8,128)S(1)}, f32[2,2,128,256]{3,2,1,0:T(8,128)}, u32[]{:S(2)}) copy-start(f32[2,2,128,256]{3,2,1,0:T(8,128)} %get-tuple-element.31.row_far) | copy-start | bytes 1572868
  95.8 19.8 %all-to-all-start.2 = ((f32[4,256,256]{2,1,0:T(8,128)}), f32[4,256,256]{2,1,0:T(8,128)}, u32[]{:S(2)}, u32[]{:S(2)}) async-start(f32[4,256,256]{2,1,0:T(8,128)} %bitcast.38), calls=%async_computation.2 | async-start | bytes 2097152 | tf_op jit(solution)/shard_map/all_to_all | solution.py:532
  103.3 19.0 %collective-permute-start.14 = (f32[2,2,128,256]{3,2,1,0:T(8,128)}, f32[2,2,128,256]{3,2,1,0:T(8,128)}, u32[]{:S(2)}, u32[]{:S(2)}) collective-permute-start(f32[2,2,128,256]{3,2,1,0:T(8,128)} %get-tuple-element.34), channel_id=1, source_target_pairs={{0,16},{16,0},{1,17},{17,1},{2,18},{18,2},{3,19},{19,3},{4,20},{20... | collective-permute-start | bytes 1572872 | tf_op jit(solution)/shard_map/ppermute | solution.py:540
  103.4 18.9 %copy-start = (f32[2,2,256,256]{3,2,1,0:T(8,128)S(1)}, f32[2,2,256,256]{3,2,1,0:T(8,128)}, u32[]{:S(2)}) copy-start(f32[2,2,256,256]{3,2,1,0:T(8,128)} %get-tuple-element.37.mid) | copy-start | bytes 3145732
  103.4 32.5 %collective-permute-start.15 = (f32[2,2,128,256]{3,2,1,0:T(8,128)}, f32[2,2,128,256]{3,2,1,0:T(8,128)}, u32[]{:S(2)}, u32[]{:S(2)}) collective-permute-start(f32[2,2,128,256]{3,2,1,0:T(8,128)} %get-tuple-element.35), channel_id=1, source_target_pairs={{16,32},{48,64},{80,96},{32,16},{64,48},{96,80},{17,33},{49,65},{8... | collective-permute-start | bytes 1572872 | tf_op jit(solution)/shard_map/ppermute | solution.py:540
  117.6 12.3 %all-to-all-start.3 = ((f32[4,4,16,256]{3,2,1,0:T(8,128)}), f32[4,4,16,256]{3,2,1,0:T(8,128)S(1)}, u32[]{:S(2)}, u32[]{:S(2)}) async-start(f32[4,4,16,256]{3,2,1,0:T(8,128)} %copy.13), calls=%async_computation.3 | async-start | bytes 524288 | tf_op jit(solution)/shard_map/all_to_all | solution.py:532
  130.0 8.0 %collective-permute-start.16 = (f32[16,256]{1,0:T(8,128)S(1)}, f32[16,256]{1,0:T(8,128)S(1)}, u32[]{:S(2)}, u32[]{:S(2)}) collective-permute-start(f32[16,256]{1,0:T(8,128)S(1)} %get-tuple-element.38), channel_id=1, source_target_pairs={{0,8},{8,16},{16,24},{24,0},{1,9},{9,17},{17,25},{25,1},{2,10},{10... | collective-permute-start | bytes 49160 | tf_op jit(solution)/shard_map/ppermute | solution.py:586
  134.7 3.7 %collective-permute-start.17 = (f32[16,256]{1,0:T(8,128)S(1)}, f32[16,256]{1,0:T(8,128)S(1)}, u32[]{:S(2)}, u32[]{:S(2)}) collective-permute-start(f32[16,256]{1,0:T(8,128)S(1)} %get-tuple-element.40), channel_id=1, source_target_pairs={{0,16},{8,24},{16,0},{24,8},{1,17},{9,25},{17,1},{25,9},{2,18},{10... | collective-permute-start | bytes 49160 | tf_op jit(solution)/shard_map/ppermute | solution.py:586
  135.9 5.2 %collective-permute-start.18 = (f32[16,256]{1,0:T(8,128)S(1)}, f32[16,256]{1,0:T(8,128)S(1)}, u32[]{:S(2)}, u32[]{:S(2)}) collective-permute-start(f32[16,256]{1,0:T(8,128)S(1)} %get-tuple-element.39), channel_id=1, source_target_pairs={{0,24},{8,0},{16,8},{24,16},{1,25},{9,1},{17,9},{25,17},{2,26},{10... | collective-permute-start | bytes 49160 | tf_op jit(solution)/shard_map/ppermute | solution.py:586
  (6 other events, 4.8 us)

commit v6 on v5

--- a/solution.py
+++ b/solution.py
@@ -222,6 +222,7 @@
             pltpu.SemaphoreType.DMA((6,)),
         ],
         compiler_params=params(),
+        cost_estimate=cost(40),
     )(where, row_near, row_far, col_near, col_far)
 
 
@@ -453,8 +454,8 @@
         backward_step(tabs, probe, win, u, far, scale, grad_probe, grad_win, m, between)
         for x in range(4):
             for y in range(4):
-                out_blocks[0, m, x, y] = grad_probe[x // 2, block_rows(x, y, c), :]
-                out_blocks[1, m, x, y] = grad_probe[x // 2, block_rows(x, y, 1 - c), :]
+                out_blocks[0, m, y, x] = grad_probe[x // 2, block_rows(x, y, c), :]
+                out_blocks[1, m, y, x] = grad_probe[x // 2, block_rows(x, y, 1 - c), :]
         for copy in out_copies(m):
             copy.start()
         return 0
@@ -554,7 +555,7 @@
     row_near, row_far = swap_rows(near, far)
     tiles = measured.reshape(2, 4, 2, SLOTS, 16, W).transpose(1, 0, 2, 3, 4, 5).reshape(4, 128, W)
     spread = jnp.broadcast_to(probe_rows[None], (4, 16, W))
-    both = exchange(after(jnp.concatenate([spread, tiles], 1), near, far), "y")
+    both = exchange(jnp.concatenate([spread, tiles], 1), "y")
     probe_rows = both[:, :16].reshape(64, W)
     meas = both[:, 16:].reshape(4, 2, 2, SLOTS, 16, W)
     c, h = where[0], where[1]
@@ -579,7 +580,7 @@
     mine = exchange(mine.reshape(4, 256, W), "z")
     near, far = rims(where, row_near, row_far, col_near, col_far)
     row_near, row_far = swap_rows(near, far)
-    mine = jnp.sum(after(mine, near, far), 0).reshape(4, 4, 16, W).swapaxes(0, 1)
+    mine = jnp.sum(after(mine, near, far), 0).reshape(4, 4, 16, W)
     total = jnp.sum(exchange(mine, "y"), 0)
     x = 2 * where[2] + h
     parts = [

time: 143 us -> 142 us (level)
    unnamed x30 -> x28, local copies, waits for them, and re-layouts: 4.1 us -> 3.56 us
where the time goes in v6:
time: 142 us; the launch traced here: 141 us
  starting transfers between devices  50.5 us (36%)
  waiting for transfers between devices  40.6 us (29%)
  Pallas kernels  31.1 us (22%)
  local copies, waits for them, and re-layouts  9.62 us (7%)
  other arithmetic  8.01 us (6%)
  between operations  1.55 us (1%)
    pallas_call x1, Pallas kernels, gradients(): pl.pallas_call(functools.partial(main_kernel, loss_scale), in_specs=[SMEM...  25.2 us
    all_to_all x4, waiting for transfers between devices, exchange(): return lax.all_to_all(x, axes, split_axis=0, concat_axis=0, tiled=True)  23.8 us
    all_to_all x4, starting transfers between devices, exchange(): return lax.all_to_all(x, axes, split_axis=0, concat_axis=0, tiled=True)  20.2 us
    ppermute x3, waiting for transfers between devices, body(): lax.ppermute(probe_rows, ('xl', 'xh'), [((i + k) % 4, i) for i in range(4)])  11.2 us
    ppermute x4, starting transfers between devices, swap_rows(): return (lax.ppermute(near, 'xl', SWAP), lax.ppermute(far, TY, far_pairs(8)))  6.99 us
    ppermute x3, starting transfers between devices, body(): lax.ppermute(pick(total, (x + k) % 4, 0), ('xl', 'xh'), [(i, (i + k) % 4)...  5.96 us
    ppermute x4, starting transfers between devices, swap_columns(): return (lax.ppermute(near, 'c', SWAP), lax.ppermute(far, TX, far_pairs(16)))  4.96 us
    ppermute x3, starting transfers between devices, body(): lax.ppermute(probe_rows, ('xl', 'xh'), [((i + k) % 4, i) for i in range(4)])  4.73 us
  transfers between devices with their start and end apart: 23, of which 10 were waited for; matrix products, arithmetic and copies ran while one was open for 8% of the time, Pallas kernels for 4%

profile of v6, /device:TPU:32, one launch (start us, length us, event | category | flops | bytes accessed | tf_op | source)
XLA Modules:
  0.0 141.4 jit_solution(1688927220089686006)
XLA Ops:
  0.6 1.1 copy.11
  2.6 4.5 %all-to-all-start = ((f32[4,144,256]{2,1,0:T(8,128)}), f32[4,144,256]{2,1,0:T(8,128)}, u32[]{:S(2)}, u32[]{:S(2)}) async-start(f32[4,144,256]{2,1,0:T(8,128)} %pad_maximum_fusion), calls=%async_computation | async-start | bytes 1179648 | tf_op jit(solution)/shard_map/all_to_all | solution.py:533
  7.8 1.6 %collective-permute-start.3 = (f32[2,2,128,256]{3,2,1,0:T(8,128)S(1)}, f32[2,2,128,256]{3,2,1,0:T(8,128)S(1)}, u32[]{:S(2)}, u32[]{:S(2)}) collective-permute-start(f32[2,2,128,256]{3,2,1,0:T(8,128)S(1)} %get-tuple-element.19), channel_id=1, source_target_pairs={{0,16},{16,0},{1,17},{17,1},{2,18},{18,2},{3,19},{19,3},{4,20},{20... | collective-permute-start | bytes 1572872 | tf_op jit(solution)/shard_map/ppermute | solution.py:541
  9.4 2.0 %collective-permute-start.4 = (f32[2,2,128,256]{3,2,1,0:T(8,128)S(1)}, f32[2,2,128,256]{3,2,1,0:T(8,128)S(1)}, u32[]{:S(2)}, u32[]{:S(2)}) collective-permute-start(f32[2,2,128,256]{3,2,1,0:T(8,128)S(1)} %get-tuple-element.20), channel_id=1, source_target_pairs={{16,32},{48,64},{80,96},{32,16},{64,48},{96,80},{17,33},{49,65},{8... | collective-permute-start | bytes 1572872 | tf_op jit(solution)/shard_map/ppermute | solution.py:541
  11.4 6.0 %all-to-all-done = f32[4,144,256]{2,1,0:T(8,128)} async-done(((f32[4,144,256]{2,1,0:T(8,128)}), f32[4,144,256]{2,1,0:T(8,128)}, u32[]{:S(2)}, u32[]{:S(2)}) %all-to-all-start) | async-done | bytes 589856 | tf_op jit(solution)/shard_map/all_to_all | solution.py:533
  18.2 1.5 %collective-permute-start.1 = (f32[64,256]{1,0:T(8,128)S(1)}, f32[64,256]{1,0:T(8,128)S(1)}, u32[]{:S(2)}, u32[]{:S(2)}) collective-permute-start(f32[64,256]{1,0:T(8,128)S(1)} %bitcast.43), channel_id=1, source_target_pairs={{16,0},{24,8},{0,16},{8,24},{17,1},{25,9},{1,17},{9,25},{18,2},{26... | collective-permute-start | bytes 196616 | tf_op jit(solution)/shard_map/ppermute | solution.py:566
  19.7 2.7 %collective-permute-start.2 = (f32[64,256]{1,0:T(8,128)S(1)}, f32[64,256]{1,0:T(8,128)S(1)}, u32[]{:S(2)}, u32[]{:S(2)}) collective-permute-start(f32[64,256]{1,0:T(8,128)S(1)} %bitcast.44), channel_id=1, source_target_pairs={{24,0},{0,8},{8,16},{16,24},{25,1},{1,9},{9,17},{17,25},{26,2},{2,... | collective-permute-start | bytes 196616 | tf_op jit(solution)/shard_map/ppermute | solution.py:566
  22.9 1.1 slice.9
  24.1 10.6 %collective-permute-done.1 = f32[64,256]{1,0:T(8,128)S(1)} collective-permute-done((f32[64,256]{1,0:T(8,128)S(1)}, f32[64,256]{1,0:T(8,128)S(1)}, u32[]{:S(2)}, u32[]{:S(2)}) %collective-permute-start.1) | collective-permute-done | bytes 65568 | tf_op jit(solution)/shard_map/ppermute | solution.py:566
  34.6 3.0 %collective-permute-start.5 = (f32[4,2,2,16,256]{4,3,2,1,0:T(8,128)S(1)}, f32[4,2,2,16,256]{4,3,2,1,0:T(8,128)}, u32[]{:S(2)}, u32[]{:S(2)}) collective-permute-start(f32[4,2,2,16,256]{4,3,2,1,0:T(8,128)S(1)} %dynamic-slice_bitcast_fusion), channel_id=1, source_target_pairs={{0,8},{8,0},{1,9},{9,1},{2,10},{10,2},{3,11},{11,3},{4,12},{12,4},... | collective-permute-start | bytes 786440 | tf_op jit(solution)/shard_map/ppermute | solution.py:562
  38.4 1.2 broadcast_in_dim.15
  39.7 6.1 %all-to-all-start.1 = ((f32[4,256,256]{2,1,0:T(8,128)}), f32[4,256,256]{2,1,0:T(8,128)}, u32[]{:S(2)}, u32[]{:S(2)}) async-start(f32[4,256,256]{2,1,0:T(8,128)} %broadcast_in_dim.15), calls=%async_computation.1 | async-start | bytes 2097152 | tf_op jit(solution)/shard_map/all_to_all | solution.py:533
  45.8 1.0 copy-done.5
  48.7 1.7 %collective-permute-start.10 = (f32[2,2,512,128]{3,2,1,0:T(8,128)S(1)}, f32[2,2,512,128]{3,2,1,0:T(8,128)}, u32[]{:S(2)}, u32[]{:S(2)}) collective-permute-start(f32[2,2,512,128]{3,2,1,0:T(8,128)S(1)} %get-tuple-element.24), channel_id=1, source_target_pairs={{1,2},{3,4},{5,6},{7,8},{9,10},{11,12},{13,14},{2,1},{4,3},{6,5},{... | collective-permute-start | bytes 3145736 | tf_op jit(solution)/shard_map/ppermute | solution.py:545
  50.3 2.5 %collective-permute-start.9 = (f32[2,2,512,128]{3,2,1,0:T(8,128)S(1)}, f32[2,2,512,128]{3,2,1,0:T(8,128)}, u32[]{:S(2)}, u32[]{:S(2)}) collective-permute-start(f32[2,2,512,128]{3,2,1,0:T(8,128)S(1)} %get-tuple-element.23), channel_id=1, source_target_pairs={{0,1},{1,0},{2,3},{3,2},{4,5},{5,4},{6,7},{7,6},{8,9},{9,8},{10,11... | collective-permute-start | bytes 3145736 | tf_op jit(solution)/shard_map/ppermute | solution.py:545
  52.8 4.1 %all-to-all-done.1 = f32[4,256,256]{2,1,0:T(8,128)} async-done(((f32[4,256,256]{2,1,0:T(8,128)}), f32[4,256,256]{2,1,0:T(8,128)}, u32[]{:S(2)}, u32[]{:S(2)}) %all-to-all-start.1) | async-done | bytes 1048608 | tf_op jit(solution)/shard_map/all_to_all | solution.py:533
  61.4 25.2 %shard_map.97 = (f32[4,4,4,16,256]{4,3,2,1,0:T(8,128)}, f32[4,4,4,16,256]{4,3,2,1,0:T(8,128)}, f32[2,2,256,256]{3,2,1,0:T(8,128)}, f32[2,2,128,256]{3,2,1,0:T(8,...) custom-call(s32[3]{0:T(128)} %copy-done.2, s32[2,2]{1,0:T(2,128)} %bitcast.50, ...), custom_call_target="tpu_custom_call" | custom-call | flops 38400000000 | bytes 1048576 | tf_op jit(solution)/shard_map/pallas_call | solution.py:478
  86.6 4.0 %collective-permute-start.11 = (f32[4,4,4,16,256]{4,3,2,1,0:T(8,128)}, f32[4,4,4,16,256]{4,3,2,1,0:T(8,128)S(1)}, u32[]{:S(2)}, u32[]{:S(2)}) collective-permute-start(f32[4,4,4,16,256]{4,3,2,1,0:T(8,128)} %get-tuple-element.27), channel_id=1, source_target_pairs={{0,1},{1,0},{2,3},{3,2},{4,5},{5,4},{6,7},{7,6},{8,9},{9,8},{10,11... | collective-permute-start | bytes 3145736 | tf_op jit(solution)/shard_map/ppermute | solution.py:578
  91.4 1.7 %collective-permute-done.11 = f32[4,4,4,16,256]{4,3,2,1,0:T(8,128)S(1)} collective-permute-done((f32[4,4,4,16,256]{4,3,2,1,0:T(8,128)}, f32[4,4,4,16,256]{4,3,2,1,0:T(8,128)S(1)}, u32[]{:S(2)}, u32[]{:S(2)}) %collective-permute-start.11) | collective-permute-done | bytes 1048608 | tf_op jit(solution)/shard_map/ppermute | solution.py:578
  93.1 2.3 %add.77 = f32[4,4,4,16,256]{4,3,2,1,0:T(8,128)} add(f32[4,4,4,16,256]{4,3,2,1,0:T(8,128)} %get-tuple-element.26, f32[4,4,4,16,256]{4,3,2,1,0:T(8,128)S(1)} %collective-permute-done.11) | non-fusion elementwise | flops 262144 | bytes 3145728 | tf_op jit(solution)/shard_map/add | solution.py:578
  95.4 4.9 %all-to-all-start.2 = ((f32[4,256,256]{2,1,0:T(8,128)}), f32[4,256,256]{2,1,0:T(8,128)}, u32[]{:S(2)}, u32[]{:S(2)}) async-start(f32[4,256,256]{2,1,0:T(8,128)} %bitcast.36), calls=%async_computation.2 | async-start | bytes 2097152 | tf_op jit(solution)/shard_map/all_to_all | solution.py:533
  101.0 1.9 %shard_map.98 = (f32[2,2,128,256]{3,2,1,0:T(8,128)}, f32[2,2,128,256]{3,2,1,0:T(8,128)}) custom-call(s32[3]{0:T(128)S(1)} %copy-done.3, f32[2,2,128,256]{3,2,1,0:T(8,128)S(1)} %copy-done.8, f32[2,2,128,256]{3,2,1,0:T(8,128)S(1)} %copy-done.9, f32[2,2,512,128]{3,2,1,0:T(8,128)S(1)} %collective-permute-done.12.col_near, ...), custom_call_target="tpu_custom_call" | custom-call | flops 48000000000 | bytes 1048576 | tf_op jit(solution)/shard_map/pallas_call | solution.py:214
  103.0 3.3 %collective-permute-start.15 = (f32[2,2,128,256]{3,2,1,0:T(8,128)}, f32[2,2,128,256]{3,2,1,0:T(8,128)}, u32[]{:S(2)}, u32[]{:S(2)}) collective-permute-start(f32[2,2,128,256]{3,2,1,0:T(8,128)} %get-tuple-element.33), channel_id=1, source_target_pairs={{16,32},{48,64},{80,96},{32,16},{64,48},{96,80},{17,33},{49,65},{8... | collective-permute-start | bytes 1572872 | tf_op jit(solution)/shard_map/ppermute | solution.py:541
  106.4 8.8 %all-to-all-done.2 = f32[4,256,256]{2,1,0:T(8,128)} async-done(((f32[4,256,256]{2,1,0:T(8,128)}), f32[4,256,256]{2,1,0:T(8,128)}, u32[]{:S(2)}, u32[]{:S(2)}) %all-to-all-start.2) | async-done | bytes 1048608 | tf_op jit(solution)/shard_map/all_to_all | solution.py:533
  115.2 2.0 %reduce_sum.18 = f32[256,256]{1,0:T(8,128)} reduce(f32[4,256,256]{2,1,0:T(8,128)} %all-to-all-done.2, f32[]{:T(128)} %constant.99.clone.1), dimensions={0}, to_apply=%region_0.1 | reduce | flops 196608 | bytes 1310724 | tf_op jit(solution)/shard_map/reduce_sum | solution.py:583
  117.2 4.7 %all-to-all-start.3 = ((f32[4,4,16,256]{3,2,1,0:T(8,128)}), f32[4,4,16,256]{3,2,1,0:T(8,128)S(1)}, u32[]{:S(2)}, u32[]{:S(2)}) async-start(f32[4,4,16,256]{3,2,1,0:T(8,128)} %bitcast.19), calls=%async_computation.3 | async-start | bytes 524288 | tf_op jit(solution)/shard_map/all_to_all | solution.py:533
  121.9 2.7 %shard_map.99 = f32[2,2,256,256]{3,2,1,0:T(8,128)} custom-call(s32[3]{0:T(128)S(1)} %copy-done.3, f32[2,2,256,256]{3,2,1,0:T(8,128)S(1)} %copy-done, f32[2,2,512,128]{3,2,1,0:T(8,128)S(1)} %collective-permute-done.12.col_near, f32[2,2,512,128]{3,2,1,0:T(8,128)S(1)} %collective-permute-done.13.col_far, f32[2,2,128,256]{3,2,1,0:T(8,128)} %collective-permute-done.14.row_near), custom_call_target="tpu_custom_call" | custom-call | tf_op jit(solution)/shard_map/pallas_call | solution.py:252
  124.7 4.9 %all-to-all-done.3 = f32[4,4,16,256]{3,2,1,0:T(8,128)S(1)} async-done(((f32[4,4,16,256]{3,2,1,0:T(8,128)}), f32[4,4,16,256]{3,2,1,0:T(8,128)S(1)}, u32[]{:S(2)}, u32[]{:S(2)}) %all-to-all-start.3) | async-done | bytes 262176 | tf_op jit(solution)/shard_map/all_to_all | solution.py:533
  129.6 4.8 %collective-permute-start.16 = (f32[16,256]{1,0:T(8,128)S(1)}, f32[16,256]{1,0:T(8,128)S(1)}, u32[]{:S(2)}, u32[]{:S(2)}) collective-permute-start(f32[16,256]{1,0:T(8,128)S(1)} %get-tuple-element.36), channel_id=1, source_target_pairs={{0,8},{8,16},{16,24},{24,0},{1,9},{9,17},{17,25},{25,1},{2,10},{10... | collective-permute-start | bytes 49160 | tf_op jit(solution)/shard_map/ppermute | solution.py:587
  134.4 1.1 collective-permute-start.17
  135.6 2.1 %add_dynamic-update-slice_fusion = f32[2,2,256,256]{3,2,1,0:T(8,128)} fusion(f32[2,2,256,256]{3,2,1,0:T(8,128)} %shard_map.99, s32[]{:T(128)S(6)} %select_n.53, f32[2,2,128,256]{3,2,1,0:T(8,128)} %collective-permute-done.15), kind=kLoop, calls=%fused_computation.1 | loop fusion | flops 131072 | bytes 1572868 | tf_op jit(solution)/shard_map/dynamic_update_slice | solution.py:595
  138.2 2.6 %collective-permute-done.18 = f32[16,256]{1,0:T(8,128)S(1)} collective-permute-done((f32[16,256]{1,0:T(8,128)S(1)}, f32[16,256]{1,0:T(8,128)S(1)}, u32[]{:S(2)}, u32[]{:S(2)}) %collective-permute-start.18) | collective-permute-done | bytes 16416 | tf_op jit(solution)/shard_map/ppermute | solution.py:587
  (64 shorter events, 12.2 us)
Async XLA Ops:
  0.6 1.1 copy-start.11
  1.7 5.4 %copy-start.1 = (f32[2,2,256,256]{3,2,1,0:T(8,128)S(1)}, f32[2,2,256,256]{3,2,1,0:T(8,128)}, u32[]{:S(2)}) copy-start(f32[2,2,256,256]{3,2,1,0:T(8,128)} %mid.5) | copy-start | bytes 3145732
  2.6 14.7 %all-to-all-start = ((f32[4,144,256]{2,1,0:T(8,128)}), f32[4,144,256]{2,1,0:T(8,128)}, u32[]{:S(2)}, u32[]{:S(2)}) async-start(f32[4,144,256]{2,1,0:T(8,128)} %pad_maximum_fusion), calls=%async_computation | async-start | bytes 1179648 | tf_op jit(solution)/shard_map/all_to_all | solution.py:533
  7.2 38.7 %copy-start.2 = (s32[3]{0:T(128)}, s32[3]{0:T(128)S(1)}, u32[]{:S(2)}) copy-start(s32[3]{0:T(128)S(1)} %pad_add_fusion.where) | copy-start | bytes 40
  7.8 30.5 %collective-permute-start.3 = (f32[2,2,128,256]{3,2,1,0:T(8,128)S(1)}, f32[2,2,128,256]{3,2,1,0:T(8,128)S(1)}, u32[]{:S(2)}, u32[]{:S(2)}) collective-permute-start(f32[2,2,128,256]{3,2,1,0:T(8,128)S(1)} %get-tuple-element.19), channel_id=1, source_target_pairs={{0,16},{16,0},{1,17},{17,1},{2,18},{18,2},{3,19},{19,3},{4,20},{20... | collective-permute-start | bytes 1572872 | tf_op jit(solution)/shard_map/ppermute | solution.py:541
  9.4 29.0 %collective-permute-start.4 = (f32[2,2,128,256]{3,2,1,0:T(8,128)S(1)}, f32[2,2,128,256]{3,2,1,0:T(8,128)S(1)}, u32[]{:S(2)}, u32[]{:S(2)}) collective-permute-start(f32[2,2,128,256]{3,2,1,0:T(8,128)S(1)} %get-tuple-element.20), channel_id=1, source_target_pairs={{16,32},{48,64},{80,96},{32,16},{64,48},{96,80},{17,33},{49,65},{8... | collective-permute-start | bytes 1572872 | tf_op jit(solution)/shard_map/ppermute | solution.py:541
  18.2 16.4 %collective-permute-start.1 = (f32[64,256]{1,0:T(8,128)S(1)}, f32[64,256]{1,0:T(8,128)S(1)}, u32[]{:S(2)}, u32[]{:S(2)}) collective-permute-start(f32[64,256]{1,0:T(8,128)S(1)} %bitcast.43), channel_id=1, source_target_pairs={{16,0},{24,8},{0,16},{8,24},{17,1},{25,9},{1,17},{9,25},{18,2},{26... | collective-permute-start | bytes 196616 | tf_op jit(solution)/shard_map/ppermute | solution.py:566
  19.7 18.0 %collective-permute-start.2 = (f32[64,256]{1,0:T(8,128)S(1)}, f32[64,256]{1,0:T(8,128)S(1)}, u32[]{:S(2)}, u32[]{:S(2)}) collective-permute-start(f32[64,256]{1,0:T(8,128)S(1)} %bitcast.44), channel_id=1, source_target_pairs={{24,0},{0,8},{8,16},{16,24},{25,1},{1,9},{9,17},{17,25},{26,2},{2,... | collective-permute-start | bytes 196616 | tf_op jit(solution)/shard_map/ppermute | solution.py:566
  22.4 15.9 %collective-permute-start = (f32[64,256]{1,0:T(8,128)S(1)}, f32[64,256]{1,0:T(8,128)S(1)}, u32[]{:S(2)}, u32[]{:S(2)}) collective-permute-start(f32[64,256]{1,0:T(8,128)S(1)} %bitcast.45), channel_id=1, source_target_pairs={{8,0},{16,8},{24,16},{0,24},{9,1},{17,9},{25,17},{1,25},{10,2},{18... | collective-permute-start | bytes 196616 | tf_op jit(solution)/shard_map/ppermute | solution.py:566
  24.0 14.3 %copy-start.10 = (f32[4,128,256]{2,1,0:T(8,128)}, f32[4,128,256]{2,1,0:T(8,128)S(1)}, u32[]{:S(2)}) copy-start(f32[4,128,256]{2,1,0:T(8,128)S(1)} %slice.9) | copy-start | bytes 1572868
  34.6 18.2 %collective-permute-start.5 = (f32[4,2,2,16,256]{4,3,2,1,0:T(8,128)S(1)}, f32[4,2,2,16,256]{4,3,2,1,0:T(8,128)}, u32[]{:S(2)}, u32[]{:S(2)}) collective-permute-start(f32[4,2,2,16,256]{4,3,2,1,0:T(8,128)S(1)} %dynamic-slice_bitcast_fusion), channel_id=1, source_target_pairs={{0,8},{8,0},{1,9},{9,1},{2,10},{10,2},{3,11},{11,3},{4,12},{12,4},... | collective-permute-start | bytes 786440 | tf_op jit(solution)/shard_map/ppermute | solution.py:562
  38.4 1.2 copy-start.4
  38.4 1.4 copy-start.6
  39.7 17.2 %all-to-all-start.1 = ((f32[4,256,256]{2,1,0:T(8,128)}), f32[4,256,256]{2,1,0:T(8,128)}, u32[]{:S(2)}, u32[]{:S(2)}) async-start(f32[4,256,256]{2,1,0:T(8,128)} %broadcast_in_dim.15), calls=%async_computation.1 | async-start | bytes 2097152 | tf_op jit(solution)/shard_map/all_to_all | solution.py:533
  48.7 12.1 %collective-permute-start.10 = (f32[2,2,512,128]{3,2,1,0:T(8,128)S(1)}, f32[2,2,512,128]{3,2,1,0:T(8,128)}, u32[]{:S(2)}, u32[]{:S(2)}) collective-permute-start(f32[2,2,512,128]{3,2,1,0:T(8,128)S(1)} %get-tuple-element.24), channel_id=1, source_target_pairs={{1,2},{3,4},{5,6},{7,8},{9,10},{11,12},{13,14},{2,1},{4,3},{6,5},{... | collective-permute-start | bytes 3145736 | tf_op jit(solution)/shard_map/ppermute | solution.py:545
  50.3 10.4 %collective-permute-start.9 = (f32[2,2,512,128]{3,2,1,0:T(8,128)S(1)}, f32[2,2,512,128]{3,2,1,0:T(8,128)}, u32[]{:S(2)}, u32[]{:S(2)}) collective-permute-start(f32[2,2,512,128]{3,2,1,0:T(8,128)S(1)} %get-tuple-element.23), channel_id=1, source_target_pairs={{0,1},{1,0},{2,3},{3,2},{4,5},{5,4},{6,7},{7,6},{8,9},{9,8},{10,11... | collective-permute-start | bytes 3145736 | tf_op jit(solution)/shard_map/ppermute | solution.py:545
  56.9 3.9 %collective-permute-start.6 = (f32[4,4,4,16,256]{4,3,2,1,0:T(8,128)}, f32[4,4,4,16,256]{4,3,2,1,0:T(8,128)}, u32[]{:S(2)}, u32[]{:S(2)}) collective-permute-start(f32[4,4,4,16,256]{4,3,2,1,0:T(8,128)} %bitcast.13.mine), channel_id=1, source_target_pairs={{0,1},{1,0},{2,3},{3,2},{4,5},{5,4},{6,7},{7,6},{8,9},{9,8},{10,11... | collective-permute-start | bytes 3145736 | tf_op jit(solution)/shard_map/ppermute | solution.py:573
  57.8 2.3 %collective-permute-start.7 = (f32[4,2,16,256]{3,2,1,0:T(8,128)S(1)}, f32[4,2,16,256]{3,2,1,0:T(8,128)S(1)}, u32[]{:S(2)}, u32[]{:S(2)}) collective-permute-start(f32[4,2,16,256]{3,2,1,0:T(8,128)S(1)} %dynamic-slice_bitcast_fusion.2), channel_id=1, source_target_pairs={{0,1},{1,0},{2,3},{3,2},{4,5},{5,4},{6,7},{7,6},{8,9},{9,8},{10,11... | collective-permute-start | bytes 393224 | tf_op jit(solution)/shard_map/ppermute | solution.py:563
  59.3 1.4 %collective-permute-start.8 = (f32[4,2,16,256]{3,2,1,0:T(8,128)S(1)}, f32[4,2,16,256]{3,2,1,0:T(8,128)S(1)}, u32[]{:S(2)}, u32[]{:S(2)}) collective-permute-start(f32[4,2,16,256]{3,2,1,0:T(8,128)S(1)} %dynamic-slice_bitcast_fusion.1), channel_id=1, source_target_pairs={{0,1},{1,0},{2,3},{3,2},{4,5},{5,4},{6,7},{7,6},{8,9},{9,8},{10,11... | collective-permute-start | bytes 393224 | tf_op jit(solution)/shard_map/ppermute | solution.py:564
  86.6 6.5 %collective-permute-start.11 = (f32[4,4,4,16,256]{4,3,2,1,0:T(8,128)}, f32[4,4,4,16,256]{4,3,2,1,0:T(8,128)S(1)}, u32[]{:S(2)}, u32[]{:S(2)}) collective-permute-start(f32[4,4,4,16,256]{4,3,2,1,0:T(8,128)} %get-tuple-element.27), channel_id=1, source_target_pairs={{0,1},{1,0},{2,3},{3,2},{4,5},{5,4},{6,7},{7,6},{8,9},{9,8},{10,11... | collective-permute-start | bytes 3145736 | tf_op jit(solution)/shard_map/ppermute | solution.py:578
  90.6 9.8 %collective-permute-start.12 = (f32[2,2,512,128]{3,2,1,0:T(8,128)}, f32[2,2,512,128]{3,2,1,0:T(8,128)S(1)}, u32[]{:S(2)}, u32[]{:S(2)}) collective-permute-start(f32[2,2,512,128]{3,2,1,0:T(8,128)} %get-tuple-element.30), channel_id=1, source_target_pairs={{0,1},{1,0},{2,3},{3,2},{4,5},{5,4},{6,7},{7,6},{8,9},{9,8},{10,11... | collective-permute-start | bytes 3145736 | tf_op jit(solution)/shard_map/ppermute | solution.py:545
  90.7 9.7 %collective-permute-start.13 = (f32[2,2,512,128]{3,2,1,0:T(8,128)}, f32[2,2,512,128]{3,2,1,0:T(8,128)S(1)}, u32[]{:S(2)}, u32[]{:S(2)}) collective-permute-start(f32[2,2,512,128]{3,2,1,0:T(8,128)} %get-tuple-element.31), channel_id=1, source_target_pairs={{1,2},{3,4},{5,6},{7,8},{9,10},{11,12},{13,14},{2,1},{4,3},{6,5},{... | collective-permute-start | bytes 3145736 | tf_op jit(solution)/shard_map/ppermute | solution.py:545
  95.4 5.0 %copy-start.8 = (f32[2,2,128,256]{3,2,1,0:T(8,128)S(1)}, f32[2,2,128,256]{3,2,1,0:T(8,128)}, u32[]{:S(2)}) copy-start(f32[2,2,128,256]{3,2,1,0:T(8,128)} %get-tuple-element.28.row_near) | copy-start | bytes 1572868
  95.4 5.0 %copy-start.9 = (f32[2,2,128,256]{3,2,1,0:T(8,128)S(1)}, f32[2,2,128,256]{3,2,1,0:T(8,128)}, u32[]{:S(2)}) copy-start(f32[2,2,128,256]{3,2,1,0:T(8,128)} %get-tuple-element.29.row_far) | copy-start | bytes 1572868
  95.4 19.8 %all-to-all-start.2 = ((f32[4,256,256]{2,1,0:T(8,128)}), f32[4,256,256]{2,1,0:T(8,128)}, u32[]{:S(2)}, u32[]{:S(2)}) async-start(f32[4,256,256]{2,1,0:T(8,128)} %bitcast.36), calls=%async_computation.2 | async-start | bytes 2097152 | tf_op jit(solution)/shard_map/all_to_all | solution.py:533
  102.9 19.0 %copy-start = (f32[2,2,256,256]{3,2,1,0:T(8,128)S(1)}, f32[2,2,256,256]{3,2,1,0:T(8,128)}, u32[]{:S(2)}) copy-start(f32[2,2,256,256]{3,2,1,0:T(8,128)} %get-tuple-element.35.mid) | copy-start | bytes 3145732
  102.9 19.0 %collective-permute-start.14 = (f32[2,2,128,256]{3,2,1,0:T(8,128)}, f32[2,2,128,256]{3,2,1,0:T(8,128)}, u32[]{:S(2)}, u32[]{:S(2)}) collective-permute-start(f32[2,2,128,256]{3,2,1,0:T(8,128)} %get-tuple-element.32), channel_id=1, source_target_pairs={{0,16},{16,0},{1,17},{17,1},{2,18},{18,2},{3,19},{19,3},{4,20},{20... | collective-permute-start | bytes 1572872 | tf_op jit(solution)/shard_map/ppermute | solution.py:541
  103.0 32.5 %collective-permute-start.15 = (f32[2,2,128,256]{3,2,1,0:T(8,128)}, f32[2,2,128,256]{3,2,1,0:T(8,128)}, u32[]{:S(2)}, u32[]{:S(2)}) collective-permute-start(f32[2,2,128,256]{3,2,1,0:T(8,128)} %get-tuple-element.33), channel_id=1, source_target_pairs={{16,32},{48,64},{80,96},{32,16},{64,48},{96,80},{17,33},{49,65},{8... | collective-permute-start | bytes 1572872 | tf_op jit(solution)/shard_map/ppermute | solution.py:541
  117.2 12.3 %all-to-all-start.3 = ((f32[4,4,16,256]{3,2,1,0:T(8,128)}), f32[4,4,16,256]{3,2,1,0:T(8,128)S(1)}, u32[]{:S(2)}, u32[]{:S(2)}) async-start(f32[4,4,16,256]{3,2,1,0:T(8,128)} %bitcast.19), calls=%async_computation.3 | async-start | bytes 524288 | tf_op jit(solution)/shard_map/all_to_all | solution.py:533
  129.6 8.0 %collective-permute-start.16 = (f32[16,256]{1,0:T(8,128)S(1)}, f32[16,256]{1,0:T(8,128)S(1)}, u32[]{:S(2)}, u32[]{:S(2)}) collective-permute-start(f32[16,256]{1,0:T(8,128)S(1)} %get-tuple-element.36), channel_id=1, source_target_pairs={{0,8},{8,16},{16,24},{24,0},{1,9},{9,17},{17,25},{25,1},{2,10},{10... | collective-permute-start | bytes 49160 | tf_op jit(solution)/shard_map/ppermute | solution.py:587
  134.4 3.7 %collective-permute-start.17 = (f32[16,256]{1,0:T(8,128)S(1)}, f32[16,256]{1,0:T(8,128)S(1)}, u32[]{:S(2)}, u32[]{:S(2)}) collective-permute-start(f32[16,256]{1,0:T(8,128)S(1)} %get-tuple-element.38), channel_id=1, source_target_pairs={{0,16},{8,24},{16,0},{24,8},{1,17},{9,25},{17,1},{25,9},{2,18},{10... | collective-permute-start | bytes 49160 | tf_op jit(solution)/shard_map/ppermute | solution.py:587
  135.6 5.2 %collective-permute-start.18 = (f32[16,256]{1,0:T(8,128)S(1)}, f32[16,256]{1,0:T(8,128)S(1)}, u32[]{:S(2)}, u32[]{:S(2)}) collective-permute-start(f32[16,256]{1,0:T(8,128)S(1)} %get-tuple-element.37), channel_id=1, source_target_pairs={{0,24},{8,0},{16,8},{24,16},{1,25},{9,1},{17,9},{25,17},{2,26},{10... | collective-permute-start | bytes 49160 | tf_op jit(solution)/shard_map/ppermute | solution.py:587
  (5 other events, 4.1 us)
